TPU v7x, 32 devices: a whole 2x2x4 slice. The times are simulated.
32 devices in a mesh: groups: 1, tensor: 32 (over z, y, x, core).
Axes of the slice: x: 2, y: 2, z: 4, core: 2. Of those that a mesh axis runs over, the one named last changes fastest.
Arguments:
- tokens: bfloat16 [32, 8192], P(('groups', 'tensor')), may hold values from -6 to 6
- norm_gain: float32 [2, 8192], replicated, may hold values from 0.5 to 1.5
- gate_codes: int32 [2, 2048, 24576], P(None, None, 'tensor'), may hold values from 0 to 255
- up_codes: int32 [2, 2048, 24576], P(None, None, 'tensor'), may hold values from 0 to 255
- down_codes: int32 [2, 6144, 8192], P(None, 'tensor'), may hold values from 0 to 255
- gate_zero: int32 [2, 128, 24576], P(None, None, 'tensor'), may hold values from 0 to 3
- up_zero: int32 [2, 128, 24576], P(None, None, 'tensor'), may hold values from 0 to 3
- down_zero: int32 [2, 384, 8192], P(None, 'tensor'), may hold values from 0 to 3
- gate_step: float32 [2, 128, 24576], P(None, None, 'tensor'), may hold values from 0.00386699 to 0.01546796
- up_step: float32 [2, 128, 24576], P(None, None, 'tensor'), may hold values from 0.00386699 to 0.01546796
- down_step: float32 [2, 384, 8192], P(None, 'tensor'), may hold values from 0.00159472 to 0.00637888
- out_grad: bfloat16 [32, 8192], P(('groups', 'tensor')), may hold values from -6 to 6
- doc_lengths: int32 [4, 3], P('groups'), may hold values from 1 to 4, 8 in all within a row
Outputs:
- input_grad: bfloat16 [32, 8192], P(('groups', 'tensor'))
- gate_step_grad: float32 [2, 128, 24576], P('groups', None, 'tensor')
- up_step_grad: float32 [2, 128, 24576], P('groups', None, 'tensor')
- down_step_grad: float32 [2, 384, 8192], P('groups', 'tensor')
Inputs may be any that keep to these rules, and one draw needn't show every extreme that they name: `gate_codes`: each word holds four codes of 0 to 3. `up_codes`: each word holds four codes of 0 to 3. `down_codes`: each word holds four codes of 0 to 3. `doc_lengths`: each row sums to 8.
All inputs are finite; a program needn't handle non-finite values.
Results may differ from a plain program's by a relative error of at most 0.015.
Values may be sent and summed in bfloat16 or wider, within the bound.
No kernel may reach another device: no remote copies, remote signals or barrier semaphores. Data moves between devices by JAX's collectives and lax.ppermute only.
A program may use at most 512 MiB of HBM per device.

v0:
```python
import jax
import jax.numpy as jnp
from jax import lax
from jax.sharding import PartitionSpec as P

GROUP = 64
LAYERS = 2


norm_epsilon = 1e-05


def unpack(packed):
    shifts = 2 * jnp.arange(4, dtype=jnp.int32)
    pieces = jnp.bitwise_and(jnp.right_shift(packed[:, None, :], shifts[None, :, None]), 3)
    return pieces.reshape(packed.shape[0] * 4, packed.shape[1])


def offsets_of(packed, zeros):
    return (unpack(packed) - jnp.repeat(zeros, GROUP, axis=0)).astype(jnp.float32)


def dequant(packed, zeros, steps):
    return (offsets_of(packed, zeros) * jnp.repeat(steps, GROUP, axis=0)).astype(jnp.bfloat16)


def group_grad(packed, zeros, weight_grad):
    product = offsets_of(packed, zeros) * weight_grad
    return jnp.sum(product.reshape(product.shape[0] // GROUP, GROUP, product.shape[1]), axis=1)


def norm_rows(state, gain):
    values = state.astype(jnp.float32)
    scale = lax.rsqrt(jnp.mean(values * values, axis=-1, keepdims=True) + norm_epsilon)
    return (values * scale * gain).astype(jnp.bfloat16)


def norm_back(state, gain, upstream):
    values = state.astype(jnp.float32)
    scale = lax.rsqrt(jnp.mean(values * values, axis=-1, keepdims=True) + norm_epsilon)
    normal = values * scale
    inner = upstream * gain
    return scale * (inner - normal * jnp.mean(inner * normal, axis=-1, keepdims=True))


def token_lengths(doc_lengths, first_row, row_count, micro_rows):
    index_rows = first_row + jnp.arange(row_count, dtype=jnp.int32)
    batch_index = index_rows // micro_rows
    position = index_rows % micro_rows
    picked = (
        batch_index[:, None] == jnp.arange(doc_lengths.shape[0], dtype=jnp.int32)[None, :]
    ).astype(jnp.int32)
    chosen = jnp.sum(picked[:, :, None] * doc_lengths[None, :, :], axis=1)
    doc_ends = jnp.cumsum(chosen, axis=1)
    starts = doc_ends - chosen
    inside = (position[:, None] >= starts) & (position[:, None] < doc_ends)
    return jnp.sum(jnp.where(inside, chosen, 0), axis=1).astype(jnp.float32)


def hidden_back(cotangent, gate_pre, up_value, down_weight):
    hidden_grad = jnp.dot(cotangent, down_weight.T, preferred_element_type=jnp.float32)
    gate_sigmoid = jax.nn.sigmoid(gate_pre)
    gate_grad = (
        hidden_grad * up_value * gate_sigmoid * (1.0 + gate_pre * (1.0 - gate_sigmoid))
    ).astype(jnp.bfloat16)
    up_grad = (hidden_grad * gate_pre * gate_sigmoid).astype(jnp.bfloat16)
    return (gate_grad, up_grad)


def row_product(left_rows, right_matrix):
    return jnp.dot(left_rows, right_matrix, preferred_element_type=jnp.float32)


def input_product(gate_grad, up_grad, gate_weight, up_weight):

    def product_rows(first_index, row_count):
        return jnp.dot(gate_grad, gate_weight.T, preferred_element_type=jnp.float32) + jnp.dot(
            up_grad, up_weight.T, preferred_element_type=jnp.float32
        )

    return product_rows


def on_device(
    tokens,
    norm_gain,
    gate_codes,
    up_codes,
    down_codes,
    gate_zero,
    up_zero,
    down_zero,
    gate_step,
    up_step,
    down_step,
    out_grad,
    doc_lengths,
):
    shard_rows = tokens.shape[0]
    device_count = lax.axis_size("tensor")
    first_row = lax.axis_index("tensor") * shard_rows
    micro_rows = shard_rows * device_count // doc_lengths.shape[0]
    local_state = tokens
    whole_state = None
    stored = []
    for layer_index in range(LAYERS):
        gate_weight = dequant(
            gate_codes[layer_index], gate_zero[layer_index], gate_step[layer_index]
        )
        up_weight = dequant(up_codes[layer_index], up_zero[layer_index], up_step[layer_index])
        down_weight = dequant(
            down_codes[layer_index], down_zero[layer_index], down_step[layer_index]
        )
        normed = lax.all_gather(
            norm_rows(local_state, norm_gain[layer_index]), "tensor", axis=0, tiled=True
        )
        gate_pre = jnp.dot(normed, gate_weight, preferred_element_type=jnp.float32)
        up_value = jnp.dot(normed, up_weight, preferred_element_type=jnp.float32)
        hidden = (jax.nn.silu(gate_pre) * up_value).astype(jnp.bfloat16)
        stored.append(
            (
                local_state,
                whole_state,
                normed,
                gate_pre,
                up_value,
                hidden,
                gate_weight,
                up_weight,
                down_weight,
            )
        )
        if layer_index + 1 < LAYERS:
            summed = lax.psum_scatter(
                row_product(hidden, down_weight), "tensor", scatter_dimension=0, tiled=True
            )
            local_state = (local_state.astype(jnp.float32) + summed).astype(jnp.bfloat16)
    local_lengths = token_lengths(doc_lengths, first_row, shard_rows, micro_rows)
    cot_local = (out_grad.astype(jnp.float32) / local_lengths[:, None]).astype(jnp.bfloat16)
    cotangent = lax.all_gather(cot_local, "tensor", axis=0, tiled=True)
    gate_list = []
    up_list = []
    down_list = []
    result = cot_local
    for layer_index in reversed(range(LAYERS)):
        (
            state_rows,
            state_whole,
            normed,
            gate_pre,
            up_value,
            hidden,
            gate_weight,
            up_weight,
            down_weight,
        ) = stored[layer_index]
        gate_grad, up_grad = hidden_back(cotangent, gate_pre, up_value, down_weight)
        down_list.append(
            group_grad(
                down_codes[layer_index],
                down_zero[layer_index],
                jnp.dot(hidden.T, cotangent, preferred_element_type=jnp.float32),
            )
        )
        gate_list.append(
            group_grad(
                gate_codes[layer_index],
                gate_zero[layer_index],
                jnp.dot(normed.T, gate_grad, preferred_element_type=jnp.float32),
            )
        )
        up_list.append(
            group_grad(
                up_codes[layer_index],
                up_zero[layer_index],
                jnp.dot(normed.T, up_grad, preferred_element_type=jnp.float32),
            )
        )
        row_terms = input_product(gate_grad, up_grad, gate_weight, up_weight)
        if layer_index == 0:
            input_local = lax.psum_scatter(
                row_terms(jnp.int32(0), lax.axis_size("tensor") * shard_rows),
                "tensor",
                scatter_dimension=0,
                tiled=True,
            )
            result = (
                cot_local.astype(jnp.float32) + norm_back(state_rows, norm_gain[0], input_local)
            ).astype(jnp.bfloat16)
        else:
            input_local = lax.psum_scatter(
                row_terms(jnp.int32(0), lax.axis_size("tensor") * shard_rows),
                "tensor",
                scatter_dimension=0,
                tiled=True,
            )
            cot_local = (
                cot_local.astype(jnp.float32)
                + norm_back(state_rows, norm_gain[layer_index], input_local)
            ).astype(jnp.bfloat16)
            cotangent = lax.all_gather(cot_local, "tensor", axis=0, tiled=True)
    return (
        result,
        jnp.stack(gate_list[::-1]),
        jnp.stack(up_list[::-1]),
        jnp.stack(down_list[::-1]),
    )


def solution(mesh):
    placed = (
        P(("groups", "tensor"), None),
        P(),
        P(None, None, "tensor"),
        P(None, None, "tensor"),
        P(None, "tensor", None),
        P(None, None, "tensor"),
        P(None, None, "tensor"),
        P(None, "tensor", None),
        P(None, None, "tensor"),
        P(None, None, "tensor"),
        P(None, "tensor", None),
        P(("groups", "tensor"), None),
        P("groups", None),
    )
    return jax.shard_map(
        on_device,
        mesh=mesh,
        in_specs=placed,
        out_specs=(
            P(("groups", "tensor"), None),
            P("groups", None, "tensor"),
            P("groups", None, "tensor"),
            P("groups", "tensor", None),
        ),
        check_vma=False,
    )
```

profile of v0, /device:TPU:0, one launch (start us, length us, event | category | flops | bytes accessed | tf_op | source)
XLA Modules:
  0.0 1008.9 jit_solution(2541556975347687068)
XLA Ops:
  7.3 1.3 shift_right_arithmetic.178
  8.6 8.2 slice_bitcast_fusion
  16.7 11.6 %shift_right_arithmetic.175 = s32[2048,4,768]{2,1,0:T(4,128)} broadcast(s32[2048,768]{1,0:T(8,128)S(1)} %get-tuple-element.19), dimensions={0,2} | broadcast | bytes 31457280 | tf_op jit(solution)/shard_map/shift_right_arithmetic | solution.py:15
  28.4 29.1 %shift_right_arithmetic.176 = s32[8192,768]{1,0:T(8,128)} reshape(s32[2048,4,768]{2,1,0:T(4,128)} %shift_right_arithmetic.175) | data formatting | bytes 50331648 | tf_op jit(solution)/shard_map/shift_right_arithmetic | solution.py:15
  57.5 8.0 slice_bitcast_fusion.1
  65.5 11.6 %shift_right_arithmetic.182 = s32[2048,4,768]{2,1,0:T(4,128)} broadcast(s32[2048,768]{1,0:T(8,128)S(1)} %get-tuple-element.15), dimensions={0,2} | broadcast | bytes 31457280 | tf_op jit(solution)/shard_map/shift_right_arithmetic | solution.py:15
  77.1 29.0 %shift_right_arithmetic.183 = s32[8192,768]{1,0:T(8,128)} reshape(s32[2048,4,768]{2,1,0:T(4,128)} %shift_right_arithmetic.182) | data formatting | bytes 50331648 | tf_op jit(solution)/shard_map/shift_right_arithmetic | solution.py:15
  106.1 14.2 %shift_right_arithmetic.197 = s32[2048,4,768]{2,1,0:T(4,128)} broadcast(s32[2048,768]{1,0:T(8,128)} %get-tuple-element.14), dimensions={0,2} | broadcast | bytes 31457280 | tf_op jit(solution)/shard_map/shift_right_arithmetic | solution.py:15
  120.3 29.0 %shift_right_arithmetic.198 = s32[8192,768]{1,0:T(8,128)} reshape(s32[2048,4,768]{2,1,0:T(4,128)} %shift_right_arithmetic.197) | data formatting | bytes 50331648 | tf_op jit(solution)/shard_map/shift_right_arithmetic | solution.py:15
  149.4 14.2 %shift_right_arithmetic.201 = s32[2048,4,768]{2,1,0:T(4,128)} broadcast(s32[2048,768]{1,0:T(8,128)} %get-tuple-element.18), dimensions={0,2} | broadcast | bytes 31457280 | tf_op jit(solution)/shard_map/shift_right_arithmetic | solution.py:15
  163.6 29.1 %shift_right_arithmetic.202 = s32[8192,768]{1,0:T(8,128)} reshape(s32[2048,4,768]{2,1,0:T(4,128)} %shift_right_arithmetic.201) | data formatting | bytes 50331648 | tf_op jit(solution)/shard_map/shift_right_arithmetic | solution.py:15
  192.7 0.7 multiply_reduce_fusion.3
  194.2 46.2 %all-gather = bf16[32,1,8192]{2,1,0:T(2,128)(2,1)S(1)} all-gather(bf16[1,1,8192]{2,1,0:T(2,128)(2,1)S(1)} %convert_bitcast_fusion.2), channel_id=1, replica_groups=mesh['groups'=1,'tensor'=32] {'tensor'}, dimensions={0}, use_global_device_ids=true | all-gather | bytes 540672 | tf_op jit(solution)/shard_map/all_gather | solution.py:114
  240.3 1.4 copy.27
  241.7 1.7 fusion.47
  243.5 8.4 slice_bitcast_fusion.2
  251.9 12.5 %shift_right_arithmetic.186 = s32[192,4,8192]{2,1,0:T(4,128)} broadcast(s32[192,8192]{1,0:T(8,128)S(1)} %get-tuple-element.17), dimensions={0,2} | broadcast | bytes 31457280 | tf_op jit(solution)/shard_map/shift_right_arithmetic | solution.py:15
  264.4 28.8 %shift_right_arithmetic.187 = s32[768,8192]{1,0:T(8,128)} reshape(s32[192,4,8192]{2,1,0:T(4,128)} %shift_right_arithmetic.186) | data formatting | bytes 50331648 | tf_op jit(solution)/shard_map/shift_right_arithmetic | solution.py:15
  293.2 14.8 %shift_right_arithmetic.193 = s32[192,4,8192]{2,1,0:T(4,128)} broadcast(s32[192,8192]{1,0:T(8,128)} %get-tuple-element.16), dimensions={0,2} | broadcast | bytes 31457280 | tf_op jit(solution)/shard_map/shift_right_arithmetic | solution.py:15
  308.0 28.8 %shift_right_arithmetic.194 = s32[768,8192]{1,0:T(8,128)} reshape(s32[192,4,8192]{2,1,0:T(4,128)} %shift_right_arithmetic.193) | data formatting | bytes 50331648 | tf_op jit(solution)/shard_map/shift_right_arithmetic | solution.py:15
  336.8 0.8 fusion.46
  338.1 1.5 slice_bitcast_fusion.7
  339.6 1.9 slice_bitcast_fusion.6
  341.5 49.8 %fusion.2 = (bf16[8192,768]{1,0:T(8,128)(2,1)}, bf16[8192,768]{1,0:T(8,128)(2,1)}, bf16[8192,768]{1,0:T(8,128)(2,1)}, bf16[8192,768]{1,0:T(8,128)(2,1)}) fusion(s32[8192,768]{1,0:T(8,128)} %shift_right_arithmetic.198, f32[128,768]{1,0:T(8,128)S(1)} %get-tuple-element.45, s32[128,768]{1,0:T(8,128)S(1)} %get-tuple-element.47, s32[8192]{0:T(1024)} %shift_right_arithmetic.178, ...), kind=kLoop, calls=%fused_computation.9 | loop fusion | flops 150994944 | bytes 154173440 | tf_op jit(solution)/shard_map/convert_element_type | solution.py:24
  391.4 6.8 fusion.34
  398.3 7.5 multiply_convert_fusion.5
  405.7 0.5 copy_bitcast_fusion
  406.2 22.3 %fusion.4 = (bf16[768,8192]{1,0:T(8,128)(2,1)}, bf16[768,8192]{1,0:T(8,128)(2,1)S(1)}) fusion(s32[768,8192]{1,0:T(8,128)} %shift_right_arithmetic.194, f32[12,8192]{1,0:T(8,128)S(1)} %get-tuple-element.48, s32[12,8192]{1,0:T(8,128)S(1)} %bitcast.219, s32[768]{0:T(1024)S(1)} %shift_right_arithmetic.189, f32[12,8192]{1,0:T(8,128)S(1)} %get-tuple-element.49, ...), kind=kLoop, calls=%fused_computation.13 | loop fusion | flops 75497472 | bytes 77073408 | tf_op jit(solution)/shard_map/convert_element_type | solution.py:24
  428.5 4.5 copy-done
  433.1 3.3 fusion.48
  436.7 0.6 fusion.43
  438.1 40.3 %all-gather.1 = bf16[32,1,8192]{2,1,0:T(2,128)(2,1)S(1)} all-gather(bf16[1,1,8192]{2,1,0:T(2,128)(2,1)S(1)} %fusion.72), channel_id=1, replica_groups=mesh['groups'=1,'tensor'=32] {'tensor'}, dimensions={0}, use_global_device_ids=true | all-gather | bytes 540672 | tf_op jit(solution)/shard_map/all_gather | solution.py:140
  478.4 85.0 %all-reduce.7.cloned.1.call-done = f32[32,8192]{1,0:T(8,128)} async-done(((f32[32,8192]{1,0:T(8,128)}), f32[32,8192]{1,0:T(8,128)}) %all-reduce.7.cloned.1.call-update) | async-done | bytes 1048592
  563.4 1.6 multiply_reduce_fusion.2
  565.7 0.9 convert_bitcast_fusion.1
  566.6 42.4 %all-gather.2 = bf16[32,1,8192]{2,1,0:T(2,128)(2,1)S(1)} all-gather(bf16[1,1,8192]{2,1,0:T(2,128)(2,1)S(1)} %convert_bitcast_fusion.1), channel_id=1, replica_groups=mesh['groups'=1,'tensor'=32] {'tensor'}, dimensions={0}, use_global_device_ids=true | all-gather | bytes 540672 | tf_op jit(solution)/shard_map/all_gather | solution.py:114
  609.0 0.6 copy.29
  609.6 6.8 fusion.25
  616.4 6.9 fusion.23
  623.3 8.3 multiply_convert_fusion.3
  631.7 0.6 copy-done.21
  632.3 9.5 fusion.49
  641.9 6.0 convolution_add_fusion.1
  648.2 15.8 %fusion.15 = f32[768,8192]{1,0:T(8,128)} fusion(s32[768,8192]{1,0:T(8,128)} %shift_right_arithmetic.194, s32[12,8192]{1,0:T(8,128)S(1)} %bitcast.220, s32[768]{0:T(1024)S(1)} %shift_right_arithmetic.189, bf16[32,1,8192]{2,1,0:T(2,128)(2,1)S(1)} %all-gather.1, f32[32,768]{1,0:T(8,128)} %copy-done.15, f32[32,768]{1,0:T(8,128)} %copy-done.16), kind=kOutput, calls=%fused_computation.31 | convolution fusion | flops 434257920 | bytes 51448832 | tf_op jit(solution)/shard_map/dot_general | solution.py:162
  664.1 11.9 %bitcast_reduce_fusion = f32[128,768]{1,0:T(8,128)} fusion(s32[8192,768]{1,0:T(8,128)} %shift_right_arithmetic.198, s32[128,768]{1,0:T(8,128)} %copy-done.6, s32[8192]{0:T(1024)} %shift_right_arithmetic.178, bf16[32,768]{1,0:T(8,128)(2,1)} %copy-done.25, bf16[32,1,8192]{2,0,1:T(8,128)(2,1)S(1)} %copy.29), kind=kOutput, calls=%fused_computation | convolution fusion | flops 440303616 | bytes 26558464 | tf_op jit(solution)/shard_map/dot_general | solution.py:176
  676.0 12.0 %bitcast_reduce_fusion.2 = f32[128,768]{1,0:T(8,128)} fusion(s32[8192,768]{1,0:T(8,128)} %shift_right_arithmetic.202, s32[128,768]{1,0:T(8,128)S(1)} %copy-done.5, s32[8192]{0:T(1024)S(1)} %copy-done.11, bf16[32,768]{1,0:T(8,128)(2,1)S(1)} %copy-done.22, bf16[32,1,8192]{2,0,1:T(8,128)(2,1)S(1)} %copy.29), kind=kOutput, calls=%fused_computation.2 | convolution fusion | flops 440303616 | bytes 26558464 | tf_op jit(solution)/shard_map/dot_general | solution.py:169
  688.0 9.3 reduce_sum.127
  697.3 76.7 %all-reduce.9.cloned.1.call-done = f32[32,8192]{1,0:T(8,128)} async-done(((f32[32,8192]{1,0:T(8,128)}), f32[32,8192]{1,0:T(8,128)}) %all-reduce.9.cloned.1.call-update) | async-done | bytes 1048592
  774.1 1.7 multiply_reduce_fusion.1
  776.5 1.1 multiply_add_fusion
  777.6 42.7 %all-gather.3 = bf16[32,1,8192]{2,1,0:T(2,128)(2,1)S(1)} all-gather(bf16[1,1,8192]{2,1,0:T(2,128)(2,1)S(1)} %bitcast.227), channel_id=1, replica_groups=mesh['groups'=1,'tensor'=32] {'tensor'}, dimensions={0}, use_global_device_ids=true | all-gather | bytes 540672 | tf_op jit(solution)/shard_map/all_gather | solution.py:201
  820.3 20.4 %fusion.14 = f32[768,8192]{1,0:T(8,128)} fusion(s32[768,8192]{1,0:T(8,128)} %shift_right_arithmetic.187, bf16[32,768]{1,0:T(8,128)(2,1)S(1)} %copy-done.31, s32[12,8192]{1,0:T(8,128)S(1)} %bitcast.218, s32[768]{0:T(1024)S(1)} %shift_right_arithmetic.189, bf16[32,1,8192]{2,1,0:T(2,128)(2,1)S(1)} %all-gather.3), kind=kOutput, calls=%fused_computation.30 | convolution fusion | flops 434110464 | bytes 51301376 | tf_op jit(solution)/shard_map/dot_general | solution.py:162
  840.7 9.3 reduce_sum.126
  850.1 8.4 multiply_convert_fusion.1
  858.6 8.5 fusion.50
  867.1 4.7 convolution_add_fusion
  872.0 11.4 %bitcast_reduce_fusion.1 = f32[128,768]{1,0:T(8,128)S(1)} fusion(s32[8192,768]{1,0:T(8,128)} %shift_right_arithmetic.183, s32[128,768]{1,0:T(8,128)S(1)} %get-tuple-element.46, s32[8192]{0:T(1024)S(1)} %copy-done.12, bf16[32,768]{1,0:T(8,128)(2,1)} %copy-done.26, bf16[32,1,8192]{2,0,1:T(8,128)(2,1)S(1)} %copy-done.1), kind=kOutput, calls=%fused_computation.1 | convolution fusion | flops 440303616 | bytes 26558464 | tf_op jit(solution)/shard_map/dot_general | solution.py:176
  883.5 11.5 %bitcast_reduce_fusion.3 = f32[128,768]{1,0:T(8,128)S(1)} fusion(s32[8192,768]{1,0:T(8,128)} %shift_right_arithmetic.176, s32[128,768]{1,0:T(8,128)S(1)} %copy-done.3, s32[8192]{0:T(1024)S(1)} %copy-done.12, bf16[32,768]{1,0:T(8,128)(2,1)S(1)} %copy-done.24, bf16[32,1,8192]{2,0,1:T(8,128)(2,1)S(1)} %copy-done.1), kind=kOutput, calls=%fused_computation.3 | convolution fusion | flops 440303616 | bytes 26558464 | tf_op jit(solution)/shard_map/dot_general | solution.py:169
  895.0 1.5 copy.26
  896.5 0.9 pad_maximum_fusion.2
  897.4 0.9 pad_maximum_fusion.1
  898.4 99.6 %all-reduce.11.cloned.1.call-done = f32[32,8192]{1,0:T(8,128)} async-done(((f32[32,8192]{1,0:T(8,128)}), f32[32,8192]{1,0:T(8,128)}) %all-reduce.11.cloned.1.call-update) | async-done | bytes 1048592
  997.9 1.6 multiply_reduce_fusion
  1000.2 1.7 add_convert_fusion
  (110 shorter events, 1.7 us)
Async XLA Ops:
  7.2 556.2 %all-reduce.7.cloned.1.call-start = ((), (), s32[]{:S(2)}) async-start(), calls=%async_computation | async-start | bytes 2097152
  163.6 29.1 %copy-start.17 = (bf16[1,8192]{1,0:T(2,128)(2,1)S(1)}, bf16[1,8192]{1,0:T(2,128)(2,1)}, u32[]{:S(2)}) copy-start(bf16[1,8192]{1,0:T(2,128)(2,1)} %param.13) | copy-start | bytes 49156
  163.6 30.5 %copy-start.27 = (f32[2,8192]{1,0:T(2,128)S(1)}, f32[2,8192]{1,0:T(2,128)}, u32[]{:S(2)}) copy-start(f32[2,8192]{1,0:T(2,128)} %param.14) | copy-start | bytes 196612
  163.6 78.1 %copy-start.19 = (f32[2,12,8192]{2,0,1:T(2,128)S(1)}, f32[2,12,8192]{2,0,1:T(2,128)}, u32[]{:S(2)}) copy-start(f32[2,12,8192]{2,0,1:T(2,128)} %param.23) | copy-start | bytes 2359300
  308.0 28.8 %copy-start.20 = (s32[2,12,8192]{2,0,1:T(2,128)S(1)}, s32[2,12,8192]{2,0,1:T(2,128)}, u32[]{:S(2)}) copy-start(s32[2,12,8192]{2,0,1:T(2,128)} %param.20) | copy-start | bytes 2359300
  339.6 51.8 %copy-start.2 = (s32[128,768]{1,0:T(8,128)}, s32[128,768]{1,0:T(8,128)S(1)}, u32[]{:S(2)}) copy-start(s32[128,768]{1,0:T(8,128)S(1)} %get-tuple-element.29) | copy-start | bytes 1179652
  339.6 51.8 %copy-start.4 = (s32[128,768]{1,0:T(8,128)}, s32[128,768]{1,0:T(8,128)S(1)}, u32[]{:S(2)}) copy-start(s32[128,768]{1,0:T(8,128)S(1)} %get-tuple-element.28) | copy-start | bytes 1179652
  339.6 51.8 %copy-start.6 = (s32[128,768]{1,0:T(8,128)}, s32[128,768]{1,0:T(8,128)S(1)}, u32[]{:S(2)}) copy-start(s32[128,768]{1,0:T(8,128)S(1)} %get-tuple-element.47) | copy-start | bytes 1179652
  341.5 49.9 %copy-start.1 = (bf16[32,1,8192]{2,0,1:T(8,128)(2,1)S(1)}, bf16[32,1,8192]{2,0,1:T(8,128)(2,1)}, u32[]{:S(2)}) copy-start(bf16[32,1,8192]{2,0,1:T(8,128)(2,1)} %copy.27) | copy-start | bytes 1572868
  391.4 14.3 %copy-start.7 = (f32[1,12,8192]{2,0,1:T(1,128)S(1)}, f32[1,12,8192]{2,0,1:T(1,128)}, u32[]{:S(2)}) copy-start(f32[1,12,8192]{2,0,1:T(1,128)} %get-tuple-element.26) | copy-start | bytes 1179652
  391.4 14.3 %copy-start.8 = (f32[1,12,8192]{2,0,1:T(1,128)S(1)}, f32[1,12,8192]{2,0,1:T(1,128)}, u32[]{:S(2)}) copy-start(f32[1,12,8192]{2,0,1:T(1,128)} %get-tuple-element.27) | copy-start | bytes 1179652
  398.3 7.5 copy-start.13
  405.7 22.8 %copy-start.30 = (bf16[32,768]{1,0:T(8,128)(2,1)}, bf16[32,768]{1,0:T(8,128)(2,1)S(1)}, u32[]{:S(2)}) copy-start(bf16[32,768]{1,0:T(8,128)(2,1)S(1)} %get-tuple-element.42) | copy-start | bytes 147460
  406.2 30.3 %copy-start.39 = (s32[4,3]{1,0:T(4,128)S(1)}, s32[4,3]{1,0:T(4,128)}, u32[]{:S(2)}) copy-start(s32[4,3]{1,0:T(4,128)} %param.25) | copy-start | bytes 148
  406.2 31.8 %copy-start.37 = (bf16[1,8192]{1,0:T(2,128)(2,1)S(1)}, bf16[1,8192]{1,0:T(2,128)(2,1)}, u32[]{:S(2)}) copy-start(bf16[1,8192]{1,0:T(2,128)(2,1)} %param.24) | copy-start | bytes 49156
  428.5 4.6 copy-start
  436.4 337.7 %all-reduce.9.cloned.1.call-start = ((), (), s32[]{:S(2)}) async-start(), calls=%async_computation.1 | async-start | bytes 2097152
  565.0 1.6 copy-start.32
  616.4 6.9 copy-start.15
  616.4 25.5 %slice-start.3 = ((s8[12582912]{0:T(1024)(128)(4,1)}), s8[4194304]{0:T(1024)(128)(4,1)S(1)}, s32[]{:S(2)}) async-start(s8[12582912]{0:T(1024)(128)(4,1)} %bitcast.213), calls=%async_computation.6 | async-start | bytes 8388608
  616.4 25.5 %slice-start.4 = ((s8[12582912]{0:T(1024)(128)(4,1)}), s8[4194304]{0:T(1024)(128)(4,1)S(1)}, s32[]{:S(2)}) async-start(s8[12582912]{0:T(1024)(128)(4,1)} %bitcast.213), calls=%async_computation.7 | async-start | bytes 8388608
  623.3 8.4 copy-start.16
  631.7 0.6 copy-start.21
  631.7 10.2 %copy-start.25 = (bf16[32,768]{1,0:T(8,128)(2,1)}, bf16[32,768]{1,0:T(8,128)(2,1)S(1)}, u32[]{:S(2)}) copy-start(bf16[32,768]{1,0:T(8,128)(2,1)S(1)} %get-tuple-element.34) | copy-start | bytes 147460
  632.3 9.6 slice-start.5
  648.0 350.0 %all-reduce.11.cloned.1.call-start = ((), (), s32[]{:S(2)}) async-start(), calls=%async_computation.2 | async-start | bytes 2097152
  664.0 12.0 %copy-start.5 = (s32[128,768]{1,0:T(8,128)S(1)}, s32[128,768]{1,0:T(8,128)}, u32[]{:S(2)}) copy-start(s32[128,768]{1,0:T(8,128)} %copy-done.4) | copy-start | bytes 1179652
  664.0 12.0 %copy-start.11 = (s32[8192]{0:T(1024)S(1)}, s32[8192]{0:T(1024)}, u32[]{:S(2)}) copy-start(s32[8192]{0:T(1024)} %shift_right_arithmetic.178) | copy-start | bytes 98308
  664.0 12.0 %copy-start.22 = (bf16[32,768]{1,0:T(8,128)(2,1)S(1)}, bf16[32,768]{1,0:T(8,128)(2,1)}, u32[]{:S(2)}) copy-start(bf16[32,768]{1,0:T(8,128)(2,1)} %copy-done.21) | copy-start | bytes 147460
  676.0 98.0 %copy-start.28 = (f32[2,8192]{1,0:T(2,128)S(1)}, f32[2,8192]{1,0:T(2,128)}, u32[]{:S(2)}) copy-start(f32[2,8192]{1,0:T(2,128)} %param.14) | copy-start | bytes 196612
  676.0 98.0 %copy-start.33 = (f32[1,8192]{1,0:T(1,128)S(1)}, f32[1,8192]{1,0:T(1,128)}, u32[]{:S(2)}) copy-start(f32[1,8192]{1,0:T(1,128)} %copy-done.32) | copy-start | bytes 98308
  676.0 100.4 %copy-start.38 = (bf16[1,8192]{1,0:T(2,128)(2,1)S(1)}, bf16[1,8192]{1,0:T(2,128)(2,1)}, u32[]{:S(2)}) copy-start(bf16[1,8192]{1,0:T(2,128)(2,1)} %param.24) | copy-start | bytes 49156
  676.0 144.2 %copy-start.31 = (bf16[32,768]{1,0:T(8,128)(2,1)S(1)}, bf16[32,768]{1,0:T(8,128)(2,1)}, u32[]{:S(2)}) copy-start(bf16[32,768]{1,0:T(8,128)(2,1)} %copy-done.30) | copy-start | bytes 147460
  777.5 42.7 %copy-start.35 = (bf16[1,8192]{1,0:T(2,128)(2,1)}, bf16[1,8192]{1,0:T(2,128)(2,1)S(1)}, u32[]{:S(2)}) copy-start(bf16[1,8192]{1,0:T(2,128)(2,1)S(1)} %multiply_add_fusion) | copy-start | bytes 49156
  840.7 9.3 copy-start.14
  840.7 9.3 copy-start.34
  850.0 17.0 %slice-start = ((s8[12582912]{0:T(1024)(128)(4,1)}), s8[4194304]{0:T(1024)(128)(4,1)S(1)}, s32[]{:S(2)}) async-start(s8[12582912]{0:T(1024)(128)(4,1)} %bitcast.211), calls=%async_computation.3 | async-start | bytes 8388608
  850.1 17.0 %slice-start.1 = ((s8[12582912]{0:T(1024)(128)(4,1)}), s8[4194304]{0:T(1024)(128)(4,1)S(1)}, s32[]{:S(2)}) async-start(s8[12582912]{0:T(1024)(128)(4,1)} %bitcast.211), calls=%async_computation.4 | async-start | bytes 8388608
  858.5 8.5 copy-start.23
  858.5 8.5 copy-start.26
  858.5 13.4 %copy-start.12 = (s32[8192]{0:T(1024)S(1)}, s32[8192]{0:T(1024)}, u32[]{:S(2)}) copy-start(s32[8192]{0:T(1024)} %shift_right_arithmetic.178) | copy-start | bytes 98308
  858.5 8.5 slice-start.2
  867.1 16.3 %copy-start.3 = (s32[128,768]{1,0:T(8,128)S(1)}, s32[128,768]{1,0:T(8,128)}, u32[]{:S(2)}) copy-start(s32[128,768]{1,0:T(8,128)} %copy-done.2) | copy-start | bytes 1179652
  867.1 16.3 %copy-start.24 = (bf16[32,768]{1,0:T(8,128)(2,1)S(1)}, bf16[32,768]{1,0:T(8,128)(2,1)}, u32[]{:S(2)}) copy-start(bf16[32,768]{1,0:T(8,128)(2,1)} %copy-done.23) | copy-start | bytes 147460
  871.9 24.5 %copy-start.9 = (f32[128,768]{1,0:T(8,128)S(1)}, f32[128,768]{1,0:T(8,128)}, u32[]{:S(2)}) copy-start(f32[128,768]{1,0:T(8,128)} %bitcast_reduce_fusion) | copy-start | bytes 1179652
  872.0 25.5 %copy-start.10 = (f32[128,768]{1,0:T(8,128)S(1)}, f32[128,768]{1,0:T(8,128)}, u32[]{:S(2)}) copy-start(f32[128,768]{1,0:T(8,128)} %bitcast_reduce_fusion.2) | copy-start | bytes 1179652
  872.0 126.0 %copy-start.18 = (bf16[1,8192]{1,0:T(2,128)(2,1)S(1)}, bf16[1,8192]{1,0:T(2,128)(2,1)}, u32[]{:S(2)}) copy-start(bf16[1,8192]{1,0:T(2,128)(2,1)} %param.13) | copy-start | bytes 49156
  872.0 125.9 %copy-start.29 = (f32[2,8192]{1,0:T(2,128)S(1)}, f32[2,8192]{1,0:T(2,128)}, u32[]{:S(2)}) copy-start(f32[2,8192]{1,0:T(2,128)} %param.14) | copy-start | bytes 196612
  872.0 128.2 %copy-start.36 = (bf16[1,8192]{1,0:T(2,128)(2,1)S(1)}, bf16[1,8192]{1,0:T(2,128)(2,1)}, u32[]{:S(2)}) copy-start(bf16[1,8192]{1,0:T(2,128)(2,1)} %copy-done.35) | copy-start | bytes 49156
Sparse Core Ops, SparseCore 0:
  436.5 126.8 all-reduce.6
  648.1 125.9 all-reduce.8
  872.0 125.9 all-reduce.10
where the time goes:
time: 1020 us; the launch traced here: 1010 us
  local copies, waits for them, and re-layouts  294 us (29%)
  waiting for transfers between devices  261 us (26%)
  blocking collectives  172 us (17%)
  matrix products  160 us (16%)
  other arithmetic  103 us (10%)
  between operations  18.3 us (2%)
    shift_right_arithmetic x19, local copies, waits for them, and re-layouts, unpack(): jnp.right_shift(packed[:, None, :], shifts[None, :, None])  279 us
    unnamed x6, waiting for transfers between devices  261 us
    all_gather x2, blocking collectives, on_device(): lax.all_gather(norm_rows(local_state, norm_gain[layer_index]), 'tensor',...  88.6 us
    all_gather x2, blocking collectives, on_device(): cotangent = lax.all_gather(cot_local, 'tensor', axis=0, tiled=True)  83 us
    convert_element_type x2, other arithmetic, dequant(): (offsets_of(packed, zeros) * jnp.repeat(steps, GROUP, axis=0)).astype(jnp...  72.1 us
    dot_general x2, matrix products, on_device(): jnp.dot(hidden.T, cotangent, preferred_element_type=jnp.float32)  36.3 us
    dot_general x2, matrix products, on_device(): jnp.dot(normed.T, gate_grad, preferred_element_type=jnp.float32)  23.5 us
    dot_general x2, matrix products, on_device(): jnp.dot(normed.T, up_grad, preferred_element_type=jnp.float32)  23.4 us
  transfers between devices with their start and end apart: 3, of which 3 were waited for; matrix products, arithmetic and copies ran while one was open for 8% of the time, Pallas kernels for 0%

commit v1 on v0

v1 whole, which is shorter than its diff:
```python
import jax
import jax.numpy as jnp
import numpy as np
from jax import lax
from jax.experimental import pallas as pl
from jax.experimental.pallas import tpu as pltpu
from jax.sharding import PartitionSpec as P

GROUP = 64
WORDS = GROUP // 4
LAYERS = 2
norm_epsilon = 1e-05
BF16 = jnp.bfloat16
F32 = jnp.float32


def params(mib=48):
    return pltpu.CompilerParams(vmem_limit_bytes=mib * 2**20)


def cost(flops, bytes_accessed):
    return pl.CostEstimate(flops=int(flops), bytes_accessed=int(bytes_accessed), transcendentals=0)


def block_of(size, most):
    best = size
    if size > most:
        for candidate in range(128, most + 1, 128):
            if size % candidate == 0:
                best = candidate
    return best


def dequant_kernel(code_ref, zero_ref, step_ref, out_ref, planes):
    groups, width = zero_ref.shape
    lanes = planes.shape[-1]
    for group in range(groups):
        for lane in range(0, width, lanes):
            cols = slice(lane, lane + lanes)
            words = code_ref[group * WORDS : (group + 1) * WORDS, cols]
            zero = zero_ref[group : group + 1, cols]
            step = step_ref[group : group + 1, cols]
            for piece in range(4):
                offset = ((words >> (2 * piece)) & 3) - zero
                planes[pl.ds(piece, WORDS, stride=4), :] = offset.astype(F32) * step
            out_ref[group * GROUP : (group + 1) * GROUP, cols] = planes[...].astype(BF16)


def dequant(codes, zeros, steps, layer):
    _, words, width = codes.shape
    groups = zeros.shape[1]
    if width > words:
        row_block, col_block = words, block_of(width, 1024)
    else:
        row_block, col_block = min(words, 256), width
    group_block = row_block // WORDS
    lanes = 128 if col_block % 128 == 0 else 64
    return pl.pallas_call(
        dequant_kernel,
        grid=(words // row_block, width // col_block),
        in_specs=[
            pl.BlockSpec((None, row_block, col_block), lambda i, j: (layer, i, j)),
            pl.BlockSpec((None, group_block, col_block), lambda i, j: (layer, i, j)),
            pl.BlockSpec((None, group_block, col_block), lambda i, j: (layer, i, j)),
        ],
        out_specs=pl.BlockSpec((row_block * 4, col_block), lambda i, j: (i, j)),
        out_shape=jax.ShapeDtypeStruct((words * 4, width), BF16),
        scratch_shapes=[pltpu.VMEM((GROUP, lanes), F32)],
        compiler_params=params(),
        cost_estimate=cost(words * width * 40, words * width * 12),
    )(codes, zeros, steps)


def sigmoid(value):
    return 1.0 / (1.0 + jnp.exp(-value))


def forward_kernel(x_ref, gate_ref, up_ref, gate_out, up_out, hidden_out):
    index = pl.program_id(0)
    gate = jnp.dot(x_ref[...], gate_ref[...], preferred_element_type=F32)
    up = jnp.dot(x_ref[...], up_ref[...], preferred_element_type=F32)

    @pl.when(index == 0)
    def _():
        gate_out[...] = gate
        up_out[...] = up

    @pl.when(index > 0)
    def _():
        gate_out[...] += gate
        up_out[...] += up

    @pl.when(index == pl.num_programs(0) - 1)
    def _():
        gate_all = gate_out[...]
        hidden_out[...] = (gate_all * sigmoid(gate_all) * up_out[...]).astype(BF16)


def forward(normed, gate_weight, up_weight):
    tokens, depth = normed.shape
    width = gate_weight.shape[1]
    block = block_of(depth, 1024)
    return pl.pallas_call(
        forward_kernel,
        grid=(depth // block,),
        in_specs=[
            pl.BlockSpec((tokens, block), lambda i: (0, i)),
            pl.BlockSpec((block, width), lambda i: (i, 0)),
            pl.BlockSpec((block, width), lambda i: (i, 0)),
        ],
        out_specs=[pl.BlockSpec((tokens, width), lambda i: (0, 0))] * 3,
        out_shape=[
            jax.ShapeDtypeStruct((tokens, width), F32),
            jax.ShapeDtypeStruct((tokens, width), F32),
            jax.ShapeDtypeStruct((tokens, width), BF16),
        ],
        compiler_params=params(),
        cost_estimate=cost(4 * tokens * depth * width, 4 * depth * width),
    )(normed, gate_weight, up_weight)


def rows_kernel(x_ref, weight_ref, out_ref):
    out_ref[...] = jnp.dot(x_ref[...], weight_ref[...], preferred_element_type=F32)


def rows_product(x, weight):
    tokens, depth = x.shape
    width = weight.shape[1]
    block = block_of(width, 1024)
    return pl.pallas_call(
        rows_kernel,
        grid=(width // block,),
        in_specs=[
            pl.BlockSpec((tokens, depth), lambda i: (0, 0)),
            pl.BlockSpec((depth, block), lambda i: (0, i)),
        ],
        out_specs=pl.BlockSpec((tokens, block), lambda i: (0, i)),
        out_shape=jax.ShapeDtypeStruct((tokens, width), F32),
        compiler_params=params(),
        cost_estimate=cost(2 * tokens * depth * width, 2 * depth * width),
    )(x, weight)


def across(left, right):
    return lax.dot_general(left, right, (((1,), (1,)), ((), ())), preferred_element_type=F32)


def hidden_grad_kernel(cot_ref, weight_ref, out_ref):
    part = across(cot_ref[...], weight_ref[...])

    @pl.when(pl.program_id(0) == 0)
    def _():
        out_ref[...] = part

    @pl.when(pl.program_id(0) > 0)
    def _():
        out_ref[...] += part


def hidden_grad_of(cot, weight):
    tokens, width = cot.shape
    depth = weight.shape[0]
    block = block_of(width, 1024)
    return pl.pallas_call(
        hidden_grad_kernel,
        grid=(width // block,),
        in_specs=[
            pl.BlockSpec((tokens, block), lambda i: (0, i)),
            pl.BlockSpec((depth, block), lambda i: (0, i)),
        ],
        out_specs=pl.BlockSpec((tokens, depth), lambda i: (0, 0)),
        out_shape=jax.ShapeDtypeStruct((tokens, depth), F32),
        compiler_params=params(),
        cost_estimate=cost(2 * tokens * depth * width, 2 * depth * width),
    )(cot, weight)


def normed_grad_kernel(gate_grad_ref, up_grad_ref, gate_ref, up_ref, out_ref):
    out_ref[...] = across(gate_grad_ref[...], gate_ref[...]) + across(up_grad_ref[...], up_ref[...])


def normed_grad_of(gate_grad, up_grad, gate_weight, up_weight):
    tokens, width = gate_grad.shape
    depth = gate_weight.shape[0]
    block = block_of(depth, 1024)
    return pl.pallas_call(
        normed_grad_kernel,
        grid=(depth // block,),
        in_specs=[
            pl.BlockSpec((tokens, width), lambda i: (0, 0)),
            pl.BlockSpec((tokens, width), lambda i: (0, 0)),
            pl.BlockSpec((block, width), lambda i: (i, 0)),
            pl.BlockSpec((block, width), lambda i: (i, 0)),
        ],
        out_specs=pl.BlockSpec((tokens, block), lambda i: (0, i)),
        out_shape=jax.ShapeDtypeStruct((tokens, depth), F32),
        compiler_params=params(),
        cost_estimate=cost(4 * tokens * depth * width, 4 * depth * width),
    )(gate_grad, up_grad, gate_weight, up_weight)


def spread(x, groups):
    tokens, columns = x.shape
    tall = jnp.concatenate([x] * groups, axis=0)
    row_group = lax.broadcasted_iota(jnp.int32, tall.shape, 0) // tokens
    col_group = lax.broadcasted_iota(jnp.int32, tall.shape, 1) // GROUP
    return jnp.where(row_group == col_group, tall.astype(F32), 0.0).astype(BF16)


def step_grad_block(x, weight, upstream, step):
    tokens = x.shape[0]
    rows = []
    groups = weight.shape[0] // GROUP
    for first in range(0, groups, 4):
        count = min(4, groups - first)
        part = slice(first * GROUP, (first + count) * GROUP)
        product = jnp.dot(spread(x[:, part], count), weight[part, :], preferred_element_type=F32)
        for group in range(count):
            own = product[group * tokens : (group + 1) * tokens] * upstream
            rows.append(jnp.sum(own, axis=0, keepdims=True))
    return jnp.concatenate(rows, axis=0) / step


def step_grad_kernel(x_ref, weight_ref, upstream_ref, step_ref, *refs):
    refs[-1][...] = step_grad_block(
        x_ref[...], weight_ref[...], upstream_ref[...].astype(F32), step_ref[...]
    )


def step_grad(x, weight, upstream, steps, layer, earlier):
    tokens, depth = x.shape
    width = weight.shape[1]
    if width > depth:
        row_block, col_block = depth, block_of(width, 1024)
    else:
        row_block, col_block = block_of(depth, 1024), width
    group_block = row_block // GROUP
    operands = [x, weight, upstream, steps]
    in_specs = [
        pl.BlockSpec((tokens, row_block), lambda i, j: (0, i)),
        pl.BlockSpec((row_block, col_block), lambda i, j: (i, j)),
        pl.BlockSpec((tokens, col_block), lambda i, j: (0, j)),
        pl.BlockSpec((None, group_block, col_block), lambda i, j: (layer, i, j)),
    ]
    aliases = {}
    if earlier is not None:
        operands.append(earlier)
        in_specs.append(pl.BlockSpec(memory_space=pl.ANY))
        aliases = {4: 0}
    return pl.pallas_call(
        step_grad_kernel,
        grid=(depth // row_block, width // col_block),
        in_specs=in_specs,
        out_specs=pl.BlockSpec((None, group_block, col_block), lambda i, j: (layer, i, j)),
        out_shape=jax.ShapeDtypeStruct(steps.shape, F32),
        input_output_aliases=aliases,
        compiler_params=params(),
        cost_estimate=cost(8 * tokens * depth * width, 2 * depth * width),
    )(*operands)


def swap(value, bit):
    count = lax.axis_size("tensor")
    return lax.ppermute(value, "tensor", [(i, i ^ bit) for i in range(count)])


def own_bit(bit):
    return (lax.axis_index("tensor") // bit) % 2


def halve(value, bit, axis=0):
    half = value.shape[axis] // 2
    mine = own_bit(bit)
    kept = lax.dynamic_slice_in_dim(value, mine * half, half, axis)
    sent = lax.dynamic_slice_in_dim(value, (1 - mine) * half, half, axis)
    got = swap(sent.astype(BF16), bit)
    return kept.astype(F32) + got.astype(F32)


def add_up(value, bit):
    rounded = value.astype(BF16)
    return rounded.astype(F32) + swap(rounded, bit).astype(F32)


def double(value, bit, axis):
    other = swap(value, bit)
    mine = own_bit(bit) == 0
    return jnp.concatenate(
        [jnp.where(mine, value, other), jnp.where(mine, other, value)], axis=axis
    )


def inverse_rms(values):
    return lax.rsqrt(jnp.mean(values * values, axis=-1, keepdims=True) + norm_epsilon)


def norm_rows(state, gain):
    values = state.astype(F32)
    return (values * inverse_rms(values) * gain).astype(BF16)


def norm_back(state, gain, upstream):
    values = state.astype(F32)
    scale = inverse_rms(values)
    normal = values * scale
    inner = upstream * gain
    return scale * (inner - normal * jnp.mean(inner * normal, axis=-1, keepdims=True))


def token_lengths(doc_lengths, index_rows, micro_rows):
    batch_index = index_rows // micro_rows
    position = index_rows % micro_rows
    picked = batch_index[:, None] == jnp.arange(doc_lengths.shape[0], dtype=jnp.int32)[None, :]
    chosen = jnp.sum(jnp.where(picked[:, :, None], doc_lengths[None, :, :], 0), axis=1)
    ends = jnp.sum(
        jnp.where(
            jnp.arange(chosen.shape[1])[:, None] <= jnp.arange(chosen.shape[1])[None, :],
            chosen[:, :, None],
            0,
        ),
        axis=1,
    )
    starts = ends - chosen
    inside = (position[:, None] >= starts) & (position[:, None] < ends)
    return jnp.sum(jnp.where(inside, chosen, 0), axis=1).astype(F32)


def hidden_back(hidden_grad, gate_pre, up_value):
    gate_sigmoid = sigmoid(gate_pre)
    gate_grad = (
        hidden_grad * up_value * gate_sigmoid * (1.0 + gate_pre * (1.0 - gate_sigmoid))
    ).astype(BF16)
    up_grad = (hidden_grad * gate_pre * gate_sigmoid).astype(BF16)
    return gate_grad, up_grad


def on_device(
    tokens,
    norm_gain,
    gate_codes,
    up_codes,
    down_codes,
    gate_zero,
    up_zero,
    down_zero,
    gate_step,
    up_step,
    down_step,
    out_grad,
    doc_lengths,
):
    shard_rows, features = tokens.shape
    device_count = lax.axis_size("tensor")
    micro_rows = shard_rows * device_count // doc_lengths.shape[0]
    bits = [1 << k for k in range(device_count.bit_length() - 1)]
    near, far = bits[:-2], bits[-2:]

    far_count = 1 << len(far)
    far_index = np.arange(far_count)
    far_place = sum(((far_index >> k) & 1) << (len(far) - 1 - k) for k in range(len(far)))
    far_device = np.argsort(far_place)
    near_part = lax.axis_index("tensor") % (1 << len(near))
    device_ids = near_part + jnp.asarray(far_device << len(near), jnp.int32)
    row_ids = (
        device_ids[:, None] * shard_rows + jnp.arange(shard_rows, dtype=jnp.int32)[None, :]
    ).reshape(-1)
    lengths = token_lengths(doc_lengths, row_ids, micro_rows)

    weights = []
    for layer in range(LAYERS):
        weights.append(
            (
                dequant(gate_codes, gate_zero, gate_step, layer),
                dequant(up_codes, up_zero, up_step, layer),
                dequant(down_codes, down_zero, down_step, layer),
            )
        )

    pair = jnp.stack([tokens, out_grad])
    for bit in reversed(far):
        pair = double(pair, bit, 1)
    state_rows = [pair[0]]
    cot_rows = (pair[1].astype(F32) / lengths[:, None]).astype(BF16)
    pair = jnp.stack([norm_rows(pair[0], norm_gain[0]), cot_rows])
    for bit in reversed(near):
        pair = double(pair, bit, 1)
    normed, cotangent = pair[0], pair[1]

    stored = []
    for layer in range(LAYERS):
        gate_weight, up_weight, down_weight = weights[layer]
        gate_pre, up_value, hidden = forward(normed, gate_weight, up_weight)
        stored.append((normed, gate_pre, up_value, hidden))
        if layer + 1 < LAYERS:
            part = rows_product(hidden, down_weight)
            for bit in near:
                part = halve(part, bit)
            for bit in far:
                part = add_up(part, bit)
            state_rows.append((state_rows[layer].astype(F32) + part).astype(BF16))
            normed = norm_rows(state_rows[-1], norm_gain[layer + 1])
            for bit in reversed(near):
                normed = double(normed, bit, 0)

    gate_out = up_out = down_out = None
    result = None
    for layer in reversed(range(LAYERS)):
        normed, gate_pre, up_value, hidden = stored[layer]
        gate_weight, up_weight, down_weight = weights[layer]
        hidden_grad = hidden_grad_of(cotangent, down_weight)
        gate_grad, up_grad = hidden_back(hidden_grad, gate_pre, up_value)
        part = normed_grad_of(gate_grad, up_grad, gate_weight, up_weight)
        down_out = step_grad(hidden, down_weight, cotangent, down_step, layer, down_out)
        gate_out = step_grad(normed, gate_weight, gate_grad, gate_step, layer, gate_out)
        up_out = step_grad(normed, up_weight, up_grad, up_step, layer, up_out)
        for bit in near:
            part = halve(part, bit)
        if layer > 0:
            for bit in far:
                part = add_up(part, bit)
            cot_rows = (
                cot_rows.astype(F32) + norm_back(state_rows[layer], norm_gain[layer], part)
            ).astype(BF16)
            cotangent = cot_rows
            for bit in reversed(near):
                cotangent = double(cotangent, bit, 0)
        else:
            own_cot = cot_rows
            for bit in far:
                part = halve(part, bit)
                half = own_cot.shape[0] // 2
                own_cot = lax.dynamic_slice_in_dim(own_cot, own_bit(bit) * half, half, 0)
            result = (
                own_cot.astype(F32) + norm_back(tokens, norm_gain[0], part)
            ).astype(BF16)
    return result, gate_out, up_out, down_out


def solution(mesh):
    placed = (
        P(("groups", "tensor"), None),
        P(),
        P(None, None, "tensor"),
        P(None, None, "tensor"),
        P(None, "tensor", None),
        P(None, None, "tensor"),
        P(None, None, "tensor"),
        P(None, "tensor", None),
        P(None, None, "tensor"),
        P(None, None, "tensor"),
        P(None, "tensor", None),
        P(("groups", "tensor"), None),
        P("groups", None),
    )
    return jax.shard_map(
        on_device,
        mesh=mesh,
        in_specs=placed,
        out_specs=(
            P(("groups", "tensor"), None),
            P("groups", None, "tensor"),
            P("groups", None, "tensor"),
            P("groups", "tensor", None),
        ),
        check_vma=False,
    )
```

time: 1020 us -> 331 us (0.32)
  local copies, waits for them, and re-layouts: 294 us -> 16.2 us
  waiting for transfers between devices: 261 us -> 50.9 us
  Pallas kernels: 0 us -> 201 us
  blocking collectives: 172 us -> 0 us
  matrix products: 160 us -> 0 us
  other arithmetic: 103 us -> 16.8 us
  starting transfers between devices: 0.33 us -> 39.7 us
  between operations: 18.3 us -> 2.65 us
    shift_right_arithmetic x19 -> x0, local copies, waits for them, and re-layouts: 279 us -> none  [unpack(): jnp.right_shift(packed[:, None, :], shifts[None, :, None])]
    unnamed x6 -> x0, waiting for transfers between devices: 261 us -> none
    pallas_call x0 -> x19, Pallas kernels: none -> 201 us  [the longest x6 73.1 us: dequant(): pl.pallas_call(dequant_kernel, grid=(words // row_block, width // col_blo...]
    all_gather x4 -> x0, blocking collectives: 172 us -> none  [the longest x2 88.6 us: on_device(): lax.all_gather(norm_rows(local_state, norm_gain[layer_index]), 'tensor',...]
    dot_general x17 -> x0, matrix products: 160 us -> none  [the longest x2 36.3 us: on_device(): jnp.dot(hidden.T, cotangent, preferred_element_type=jnp.float32)]
    convert_element_type x4 -> x11, other arithmetic: 73.8 us -> 2.41 us  [the longest x4 1.16 us: add_up(): rounded = value.astype(BF16)]
    ppermute x0 -> x26, waiting for transfers between devices: none -> 50.9 us  [swap(): return lax.ppermute(value, 'tensor', [(i, i ^ bit) for i in range(count)])]
    ppermute x0 -> x26, starting transfers between devices: none -> 39.7 us  [swap(): return lax.ppermute(value, 'tensor', [(i, i ^ bit) for i in range(count)])]
  transfers between devices with their start and end apart: 3 -> 26, of which waited for: 3 -> 18; matrix products, arithmetic and copies ran while one was open for 8% -> 3% of each run, Pallas kernels for 0% -> 41%
where the time goes in v1:
time: 331 us; the launch traced here: 328 us
  Pallas kernels  201 us (61%)
  waiting for transfers between devices  50.9 us (15%)
  starting transfers between devices  39.7 us (12%)
  other arithmetic  16.8 us (5%)
  local copies, waits for them, and re-layouts  16.2 us (5%)
    pallas_call x6, Pallas kernels, dequant(): pl.pallas_call(dequant_kernel, grid=(words // row_block, width // col_blo...  73.1 us
    pallas_call x6, Pallas kernels, step_grad(): pl.pallas_call(step_grad_kernel, grid=(depth // row_block, width // col_b...  51.8 us
    ppermute x26, waiting for transfers between devices, swap(): return lax.ppermute(value, 'tensor', [(i, i ^ bit) for i in range(count)])  50.9 us
    ppermute x26, starting transfers between devices, swap(): return lax.ppermute(value, 'tensor', [(i, i ^ bit) for i in range(count)])  39.7 us
    pallas_call x2, Pallas kernels, normed_grad_of(): pl.pallas_call(normed_grad_kernel, grid=(depth // block,), in_specs=[pl.B...  26.5 us
    pallas_call x2, Pallas kernels, forward(): pl.pallas_call(forward_kernel, grid=(depth // block,), in_specs=[pl.Block...  24.1 us
    pallas_call x2, Pallas kernels, hidden_grad_of(): pl.pallas_call(hidden_grad_kernel, grid=(width // block,), in_specs=[pl.B...  17.8 us
    unnamed x60, local copies, waits for them, and re-layouts  12.8 us
  transfers between devices with their start and end apart: 26, of which 18 were waited for; matrix products, arithmetic and copies ran while one was open for 3% of the time, Pallas kernels for 41%

profile of v1, /device:TPU:0, one launch (start us, length us, event | category | flops | bytes accessed | tf_op | source)
XLA Modules:
  0.0 327.6 jit_solution(8857307804175185895)
XLA Ops:
  1.5 4.1 %collective-permute-start = (bf16[2,1,8192]{2,1,0:T(2,128)(2,1)S(1)}, bf16[2,1,8192]{2,1,0:T(2,128)(2,1)S(1)}, u32[]{:S(2)}, u32[]{:S(2)}) collective-permute-start(bf16[2,1,8192]{2,1,0:T(2,128)(2,1)S(1)} %pad_maximum_fusion.11), channel_id=1, source_target_pairs={{0,16},{1,17},{2,18},{3,19},{4,20},{5,21},{6,22},{7,23},{8,24},{9,... | collective-permute-start | bytes 98312 | tf_op jit(solution)/shard_map/ppermute | solution.py:264
  10.4 1.5 collective-permute-start.1
  11.9 2.8 collective-permute-done.1
  15.8 1.8 collective-permute-start.2
  17.6 3.2 collective-permute-done.2
  21.1 1.8 collective-permute-start.3
  22.9 4.7 %collective-permute-done.3 = bf16[2,8,8192]{2,1,0:T(8,128)(2,1)S(1)} collective-permute-done((bf16[2,8,8192]{2,1,0:T(8,128)(2,1)S(1)}, bf16[2,8,8192]{2,1,0:T(8,128)(2,1)S(1)}, u32[]{:S(2)}, u32[]{:S(2)}) %collective-permute-start.3) | collective-permute-done | bytes 262176 | tf_op jit(solution)/shard_map/ppermute | solution.py:264
  28.6 1.6 copy.33.step_ref
  30.2 1.6 copy.32.zero_ref
  31.8 1.5 copy-done.1
  34.4 11.9 %shard_map.165.gate_ref.weight_ref = bf16[8192,768]{1,0:T(8,128)(2,1)} custom-call(s32[2,2048,768]{2,1,0:T(8,128)} %code_ref.10, s32[2,128,768]{2,1,0:T(8,128)S(1)} %copy-done.10, f32[2,128,768]{2,1,0:T(8,128)S(1)} %copy-done.1), custom_call_target="tpu_custom_call" | custom-call | flops 62914560 | bytes 18874368 | tf_op jit(solution)/shard_map/pallas_call | solution.py:58
  46.4 11.8 %shard_map.166.up_ref.weight_ref = bf16[8192,768]{1,0:T(8,128)(2,1)} custom-call(s32[2,2048,768]{2,1,0:T(8,128)} %code_ref.11, s32[2,128,768]{2,1,0:T(8,128)S(1)} %copy-done.12, f32[2,128,768]{2,1,0:T(8,128)S(1)} %copy-done), custom_call_target="tpu_custom_call" | custom-call | flops 62914560 | bytes 18874368 | tf_op jit(solution)/shard_map/pallas_call | solution.py:58
  58.2 12.8 %shard_map.168.weight_ref = bf16[768,8192]{1,0:T(8,128)(2,1)} custom-call(s32[2,192,8192]{2,1,0:T(8,128)} %code_ref.9, s32[2,12,8192]{2,1,0:T(8,128)S(1)} %copy.32.zero_ref, f32[2,12,8192]{2,1,0:T(8,128)S(1)} %copy.33.step_ref), custom_call_target="tpu_custom_call" | custom-call | flops 62914560 | bytes 18874368 | tf_op jit(solution)/shard_map/pallas_call | solution.py:58
  71.1 1.2 broadcast_select_fusion
  72.4 12.2 %shard_map.167 = (f32[32,768]{1,0:T(8,128)S(1)}, f32[32,768]{1,0:T(8,128)S(1)}, bf16[32,768]{1,0:T(8,128)(2,1)S(1)}) custom-call(bf16[32,8192]{1,0:T(8,128)(2,1)S(1)} %get-tuple-element.33.x_ref, bf16[8192,768]{1,0:T(8,128)(2,1)} %shard_map.165.gate_ref.weight_ref, bf16[8192,768]{1,0:T(8,128)(2,1)} %shard_map.166.up_ref.weight_ref), custom_call_target="tpu_custom_call" | custom-call | flops 805306368 | bytes 25165824 | tf_op jit(solution)/shard_map/pallas_call | solution.py:103
  84.6 8.1 %shard_map.169 = f32[32,8192]{1,0:T(8,128)S(1)} custom-call(bf16[32,768]{1,0:T(8,128)(2,1)S(1)} %get-tuple-element.10.x_ref, bf16[768,8192]{1,0:T(8,128)(2,1)} %shard_map.168.weight_ref), custom_call_target="tpu_custom_call" | custom-call | flops 402653184 | bytes 12582912 | tf_op jit(solution)/shard_map/pallas_call | solution.py:130
  94.9 1.5 collective-permute-done.5
  96.4 1.2 convert_add_fusion.2
  99.1 1.7 collective-permute-start.6
  100.8 4.4 %collective-permute-done.6 = bf16[8,8192]{1,0:T(8,128)(2,1)} collective-permute-done((bf16[8,8192]{1,0:T(8,128)(2,1)}, bf16[8,8192]{1,0:T(8,128)(2,1)}, u32[]{:S(2)}, u32[]{:S(2)}) %collective-permute-start.6) | collective-permute-done | bytes 131104 | tf_op jit(solution)/shard_map/ppermute | solution.py:264
  107.6 1.7 collective-permute-start.7
  109.3 2.9 collective-permute-done.7
  113.2 1.5 collective-permute-start.8
  114.7 2.8 collective-permute-done.8
  117.6 2.0 collective-permute-start.9
  119.6 3.2 collective-permute-done.9
  123.1 1.8 collective-permute-start.10
  124.9 2.5 collective-permute-done.10
  127.7 1.8 collective-permute-start.11
  129.4 3.3 collective-permute-done.11
  134.1 11.8 %shard_map.172.gate_ref.weight_ref = bf16[8192,768]{1,0:T(8,128)(2,1)} custom-call(s32[2,2048,768]{2,1,0:T(8,128)} %code_ref.10, s32[2,128,768]{2,1,0:T(8,128)S(1)} %copy-done.11, f32[2,128,768]{2,1,0:T(8,128)S(1)} %copy-done.2), custom_call_target="tpu_custom_call" | custom-call | flops 62914560 | bytes 18874368 | tf_op jit(solution)/shard_map/pallas_call | solution.py:58
  145.9 11.9 %shard_map.173.up_ref.weight_ref = bf16[8192,768]{1,0:T(8,128)(2,1)} custom-call(s32[2,2048,768]{2,1,0:T(8,128)} %code_ref.11, s32[2,128,768]{2,1,0:T(8,128)S(1)} %copy-done.13, f32[2,128,768]{2,1,0:T(8,128)S(1)} %copy-done), custom_call_target="tpu_custom_call" | custom-call | flops 62914560 | bytes 18874368 | tf_op jit(solution)/shard_map/pallas_call | solution.py:58
  157.8 12.8 %shard_map.170.weight_ref = bf16[768,8192]{1,0:T(8,128)(2,1)} custom-call(s32[2,192,8192]{2,1,0:T(8,128)} %code_ref.9, s32[2,12,8192]{2,1,0:T(8,128)S(1)} %copy-done.4, f32[2,12,8192]{2,1,0:T(8,128)S(1)} %copy.33.step_ref), custom_call_target="tpu_custom_call" | custom-call | flops 62914560 | bytes 18874368 | tf_op jit(solution)/shard_map/pallas_call | solution.py:58
  170.6 8.9 %shard_map.171 = f32[32,768]{1,0:T(8,128)S(1)} custom-call(bf16[32,8192]{1,0:T(8,128)(2,1)S(1)} %get-tuple-element.32.cot_ref.upstream_ref, bf16[768,8192]{1,0:T(8,128)(2,1)} %shard_map.170.weight_ref), custom_call_target="tpu_custom_call" | custom-call | flops 402653184 | bytes 12582912 | tf_op jit(solution)/shard_map/pallas_call | solution.py:164
  179.6 11.9 %shard_map.174 = (f32[32,768]{1,0:T(8,128)S(1)}, f32[32,768]{1,0:T(8,128)S(1)}, bf16[32,768]{1,0:T(8,128)(2,1)S(1)}) custom-call(bf16[32,8192]{1,0:T(8,128)(2,1)S(1)} %pad_maximum_fusion.2.x_ref, bf16[8192,768]{1,0:T(8,128)(2,1)} %shard_map.172.gate_ref.weight_ref, bf16[8192,768]{1,0:T(8,128)(2,1)} %shard_map.173.up_ref.weight_ref), custom_call_target="tpu_custom_call" | custom-call | flops 805306368 | bytes 25165824 | tf_op jit(solution)/shard_map/pallas_call | solution.py:103
  191.6 13.3 %shard_map.175 = f32[32,8192]{1,0:T(8,128)S(1)} custom-call(bf16[32,768]{1,0:T(8,128)(2,1)S(1)} %get-tuple-element.51.gate_grad_ref.upstream_ref, bf16[32,768]{1,0:T(8,128)(2,1)S(1)} %get-tuple-element.50.up_grad_ref.upstream_ref, bf16[8192,768]{1,0:T(8,128)(2,1)} %shard_map.172.gate_ref.weight_ref, bf16[8192,768]{1,0:T(8,128)(2,1)} %shard_map.173.up_ref.weight_ref), custom_call_target="tpu_custom_call" | custom-call | flops 805306368 | bytes 25165824 | tf_op jit(solution)/shard_map/pallas_call | solution.py:186
  205.5 1.2 collective-permute-done.13
  206.7 1.8 collective-permute-start.14
  208.5 4.1 %collective-permute-done.14 = bf16[8,8192]{1,0:T(8,128)(2,1)S(1)} collective-permute-done((bf16[8,8192]{1,0:T(8,128)(2,1)S(1)}, bf16[8,8192]{1,0:T(8,128)(2,1)S(1)}, u32[]{:S(2)}, u32[]{:S(2)}) %collective-permute-start.14) | collective-permute-done | bytes 131104 | tf_op jit(solution)/shard_map/ppermute | solution.py:264
  212.6 1.8 collective-permute-start.15
  214.4 2.5 collective-permute-done.15
  217.0 1.5 collective-permute-start.16
  218.5 2.8 collective-permute-done.16
  221.4 2.1 collective-permute-start.17
  223.5 3.1 collective-permute-done.17
  227.1 1.8 collective-permute-start.18
  228.9 2.5 collective-permute-done.18
  231.6 1.8 collective-permute-start.19
  233.4 3.2 collective-permute-done.19
  238.1 1.4 multiply_reduce_fusion.1
  240.3 1.1 broadcast_select_fusion.3
  241.4 8.9 %shard_map.176 = f32[32,768]{1,0:T(8,128)S(1)} custom-call(bf16[32,8192]{1,0:T(8,128)(2,1)S(1)} %pad_maximum_fusion.3.cot_ref.upstream_ref, bf16[768,8192]{1,0:T(8,128)(2,1)} %shard_map.168.weight_ref), custom_call_target="tpu_custom_call" | custom-call | flops 402653184 | bytes 12582912 | tf_op jit(solution)/shard_map/pallas_call | solution.py:164
  250.4 13.2 %shard_map.177 = f32[32,8192]{1,0:T(8,128)S(1)} custom-call(bf16[32,768]{1,0:T(8,128)(2,1)S(1)} %get-tuple-element.49.gate_grad_ref.upstream_ref, bf16[32,768]{1,0:T(8,128)(2,1)S(1)} %get-tuple-element.48.up_grad_ref.upstream_ref, bf16[8192,768]{1,0:T(8,128)(2,1)} %shard_map.165.gate_ref.weight_ref, bf16[8192,768]{1,0:T(8,128)(2,1)} %shard_map.166.up_ref.weight_ref), custom_call_target="tpu_custom_call" | custom-call | flops 805306368 | bytes 25165824 | tf_op jit(solution)/shard_map/pallas_call | solution.py:186
  264.3 8.9 %shard_map.180.refs_0_ = f32[2,128,768]{2,1,0:T(8,128)} custom-call(bf16[32,8192]{1,0:T(8,128)(2,1)S(1)} %pad_maximum_fusion.2.x_ref, bf16[8192,768]{1,0:T(8,128)(2,1)} %shard_map.173.up_ref.weight_ref, bf16[32,768]{1,0:T(8,128)(2,1)S(1)} %get-tuple-element.50.up_grad_ref.upstream_ref, f32[2,128,768]{2,1,0:T(8,128)S(1)} %copy-done), custom_call_target="tpu_custom_call" | custom-call | flops 1610612736 | bytes 12582912 | tf_op jit(solution)/shard_map/pallas_call | solution.py:250
  273.1 8.9 %shard_map.178.refs_0_ = f32[2,128,768]{2,1,0:T(8,128)} custom-call(bf16[32,8192]{1,0:T(8,128)(2,1)S(1)} %pad_maximum_fusion.2.x_ref, bf16[8192,768]{1,0:T(8,128)(2,1)} %shard_map.172.gate_ref.weight_ref, bf16[32,768]{1,0:T(8,128)(2,1)S(1)} %get-tuple-element.51.gate_grad_ref.upstream_ref, f32[2,128,768]{2,1,0:T(8,128)S(1)} %copy-done.2), custom_call_target="tpu_custom_call" | custom-call | flops 1610612736 | bytes 12582912 | tf_op jit(solution)/shard_map/pallas_call | solution.py:250
  282.1 1.8 collective-permute-start.22
  283.9 8.2 %shard_map.182.refs_0_ = f32[2,12,8192]{2,1,0:T(8,128)S(1)} custom-call(bf16[32,768]{1,0:T(8,128)(2,1)S(1)} %get-tuple-element.15.x_ref, bf16[768,8192]{1,0:T(8,128)(2,1)} %shard_map.170.weight_ref, bf16[32,8192]{1,0:T(8,128)(2,1)S(1)} %copy-done.8, f32[2,12,8192]{2,1,0:T(8,128)S(1)} %copy.33.step_ref), custom_call_target="tpu_custom_call" | custom-call | flops 1610612736 | bytes 12582912 | tf_op jit(solution)/shard_map/pallas_call | solution.py:250
  292.2 1.6 collective-permute-start.23
  293.8 8.2 %shard_map.183 = f32[2,12,8192]{2,1,0:T(8,128)S(1)} custom-call(bf16[32,768]{1,0:T(8,128)(2,1)S(1)} %get-tuple-element.10.x_ref, bf16[768,8192]{1,0:T(8,128)(2,1)} %shard_map.168.weight_ref, bf16[32,8192]{1,0:T(8,128)(2,1)S(1)} %pad_maximum_fusion.3.cot_ref.upstream_ref, f32[2,12,8192]{2,1,0:T(8,128)S(1)} %copy.33.step_ref, ...), custom_call_target="tpu_custom_call", output_to_operand_aliasing={{}: (4, {})} | custom-call | flops 1610612736 | bytes 12582912 | tf_op jit(solution)/shard_map/pallas_call | solution.py:250
  302.1 1.3 collective-permute-start.24
  303.4 8.9 %shard_map.181 = f32[2,128,768]{2,1,0:T(8,128)} custom-call(bf16[32,8192]{1,0:T(8,128)(2,1)S(1)} %copy-done.6, bf16[8192,768]{1,0:T(8,128)(2,1)} %shard_map.166.up_ref.weight_ref, bf16[32,768]{1,0:T(8,128)(2,1)S(1)} %get-tuple-element.48.up_grad_ref.upstream_ref, f32[2,128,768]{2,1,0:T(8,128)S(1)} %copy-done, ...), custom_call_target="tpu_custom_call", output_to_operand_aliasing={{}: (4, {})} | custom-call | flops 1610612736 | bytes 12582912 | tf_op jit(solution)/shard_map/pallas_call | solution.py:250
  312.4 2.8 collective-permute-start.25
  315.2 8.9 %shard_map.179 = f32[2,128,768]{2,1,0:T(8,128)} custom-call(bf16[32,8192]{1,0:T(8,128)(2,1)S(1)} %copy-done.6, bf16[8192,768]{1,0:T(8,128)(2,1)} %shard_map.165.gate_ref.weight_ref, bf16[32,768]{1,0:T(8,128)(2,1)S(1)} %get-tuple-element.49.gate_grad_ref.upstream_ref, f32[2,128,768]{2,1,0:T(8,128)S(1)} %copy-done.2, ...), custom_call_target="tpu_custom_call", output_to_operand_aliasing={{}: (4, {})} | custom-call | flops 1610612736 | bytes 12582912 | tf_op jit(solution)/shard_map/pallas_call | solution.py:250
  324.1 1.5 copy.38
  (137 shorter events, 23.7 us)
Async XLA Ops:
  1.5 7.8 %collective-permute-start = (bf16[2,1,8192]{2,1,0:T(2,128)(2,1)S(1)}, bf16[2,1,8192]{2,1,0:T(2,128)(2,1)S(1)}, u32[]{:S(2)}, u32[]{:S(2)}) collective-permute-start(bf16[2,1,8192]{2,1,0:T(2,128)(2,1)S(1)} %pad_maximum_fusion.11), channel_id=1, source_target_pairs={{0,16},{1,17},{2,18},{3,19},{4,20},{5,21},{6,22},{7,23},{8,24},{9,... | collective-permute-start | bytes 98312 | tf_op jit(solution)/shard_map/ppermute | solution.py:264
  8.8 118.7 %copy-start.21 = (f32[1,8192]{1,0:T(1,128)}, f32[1,8192]{1,0:T(1,128)S(1)}, u32[]{:S(2)}) copy-start(f32[1,8192]{1,0:T(1,128)S(1)} %get-tuple-element.60) | copy-start | bytes 98308
  10.4 4.3 %collective-permute-start.1 = (bf16[2,2,8192]{2,1,0:T(2,128)(2,1)S(1)}, bf16[2,2,8192]{2,1,0:T(2,128)(2,1)S(1)}, u32[]{:S(2)}, u32[]{:S(2)}) collective-permute-start(bf16[2,2,8192]{2,1,0:T(2,128)(2,1)S(1)} %pad_maximum_fusion.12), channel_id=1, source_target_pairs={{0,8},{1,9},{2,10},{3,11},{4,12},{5,13},{6,14},{7,15},{8,0},{9,1},... | collective-permute-start | bytes 196616 | tf_op jit(solution)/shard_map/ppermute | solution.py:264
  14.9 0.6 copy-start.17
  14.9 0.8 copy-start.19
  15.8 5.0 %collective-permute-start.2 = (bf16[2,4,8192]{2,1,0:T(4,128)(2,1)S(1)}, bf16[2,4,8192]{2,1,0:T(4,128)(2,1)S(1)}, u32[]{:S(2)}, u32[]{:S(2)}) collective-permute-start(bf16[2,4,8192]{2,1,0:T(4,128)(2,1)S(1)} %pad_maximum_fusion.7), channel_id=1, source_target_pairs={{0,4},{1,5},{2,6},{3,7},{4,0},{5,1},{6,2},{7,3},{8,12},{9,13},{10,... | collective-permute-start | bytes 393224 | tf_op jit(solution)/shard_map/ppermute | solution.py:264
  21.1 6.4 %collective-permute-start.3 = (bf16[2,8,8192]{2,1,0:T(8,128)(2,1)S(1)}, bf16[2,8,8192]{2,1,0:T(8,128)(2,1)S(1)}, u32[]{:S(2)}, u32[]{:S(2)}) collective-permute-start(bf16[2,8,8192]{2,1,0:T(8,128)(2,1)S(1)} %pad_maximum_fusion.4), channel_id=1, source_target_pairs={{0,2},{1,3},{2,0},{3,1},{4,6},{5,7},{6,4},{7,5},{8,10},{9,11},{10,... | collective-permute-start | bytes 786440 | tf_op jit(solution)/shard_map/ppermute | solution.py:264
  28.6 42.5 %collective-permute-start.4 = (bf16[2,16,8192]{2,1,0:T(8,128)(2,1)}, bf16[2,16,8192]{2,1,0:T(8,128)(2,1)}, u32[]{:S(2)}, u32[]{:S(2)}) collective-permute-start(bf16[2,16,8192]{2,1,0:T(8,128)(2,1)} %pad_maximum_fusion.1), channel_id=1, source_target_pairs={{0,1},{1,0},{2,3},{3,2},{4,5},{5,4},{6,7},{7,6},{8,9},{9,8},{10,11... | collective-permute-start | bytes 1572872 | tf_op jit(solution)/shard_map/ppermute | solution.py:264
  31.8 26.5 %copy-start.3 = (s32[2,12,8192]{2,1,0:T(8,128)}, s32[2,12,8192]{2,1,0:T(8,128)S(1)}, u32[]{:S(2)}) copy-start(s32[2,12,8192]{2,1,0:T(8,128)S(1)} %copy.32.zero_ref) | copy-start | bytes 2359300
  31.8 1.5 copy-start.1
  33.3 1.1 copy-start.10
  34.4 12.0 %copy-start = (f32[2,128,768]{2,1,0:T(8,128)S(1)}, f32[2,128,768]{2,1,0:T(8,128)}, u32[]{:S(2)}) copy-start(f32[2,128,768]{2,1,0:T(8,128)} %step_ref.19) | copy-start | bytes 2359300
  34.4 12.0 %copy-start.12 = (s32[2,128,768]{2,1,0:T(8,128)S(1)}, s32[2,128,768]{2,1,0:T(8,128)}, u32[]{:S(2)}) copy-start(s32[2,128,768]{2,1,0:T(8,128)} %zero_ref.9) | copy-start | bytes 2359300
  72.4 12.3 %copy-start.5 = (bf16[32,8192]{1,0:T(8,128)(2,1)}, bf16[32,8192]{1,0:T(8,128)(2,1)S(1)}, u32[]{:S(2)}) copy-start(bf16[32,8192]{1,0:T(8,128)(2,1)S(1)} %get-tuple-element.33.x_ref) | copy-start | bytes 1572868
  72.4 98.2 %copy-start.7 = (bf16[32,8192]{1,0:T(8,128)(2,1)}, bf16[32,8192]{1,0:T(8,128)(2,1)S(1)}, u32[]{:S(2)}) copy-start(bf16[32,8192]{1,0:T(8,128)(2,1)S(1)} %get-tuple-element.32.cot_ref.upstream_ref) | copy-start | bytes 1572868
  84.6 48.3 %copy-start.2 = (f32[2,128,768]{2,1,0:T(8,128)S(1)}, f32[2,128,768]{2,1,0:T(8,128)}, u32[]{:S(2)}) copy-start(f32[2,128,768]{2,1,0:T(8,128)} %step_ref.17) | copy-start | bytes 2359300
  92.7 1.0 copy-start.9
  94.4 2.0 collective-permute-start.5
  97.6 0.8 copy-start.14
  99.1 6.1 %collective-permute-start.6 = (bf16[8,8192]{1,0:T(8,128)(2,1)}, bf16[8,8192]{1,0:T(8,128)(2,1)}, u32[]{:S(2)}, u32[]{:S(2)}) collective-permute-start(bf16[8,8192]{1,0:T(8,128)(2,1)} %dynamic-slice_convert_fusion.5), channel_id=1, source_target_pairs={{0,2},{1,3},{2,0},{3,1},{4,6},{5,7},{6,4},{7,5},{8,10},{9,11},{10,... | collective-permute-start | bytes 393224 | tf_op jit(solution)/shard_map/ppermute | solution.py:264
  106.2 0.7 copy-start.24
  107.6 4.6 %collective-permute-start.7 = (bf16[4,8192]{1,0:T(4,128)(2,1)}, bf16[4,8192]{1,0:T(4,128)(2,1)}, u32[]{:S(2)}, u32[]{:S(2)}) collective-permute-start(bf16[4,8192]{1,0:T(4,128)(2,1)} %dynamic-slice_convert_fusion.8), channel_id=1, source_target_pairs={{0,4},{1,5},{2,6},{3,7},{4,0},{5,1},{6,2},{7,3},{8,12},{9,13},{10,... | collective-permute-start | bytes 196616 | tf_op jit(solution)/shard_map/ppermute | solution.py:264
  113.2 4.3 %collective-permute-start.8 = (bf16[4,8192]{1,0:T(4,128)(2,1)S(1)}, bf16[4,8192]{1,0:T(4,128)(2,1)S(1)}, u32[]{:S(2)}, u32[]{:S(2)}) collective-permute-start(bf16[4,8192]{1,0:T(4,128)(2,1)S(1)} %add_convert_fusion.3), channel_id=1, source_target_pairs={{0,8},{1,9},{2,10},{3,11},{4,12},{5,13},{6,14},{7,15},{8,0},{9,1},... | collective-permute-start | bytes 196616 | tf_op jit(solution)/shard_map/ppermute | solution.py:264
  117.6 5.2 %collective-permute-start.9 = (bf16[4,8192]{1,0:T(4,128)(2,1)S(1)}, bf16[4,8192]{1,0:T(4,128)(2,1)S(1)}, u32[]{:S(2)}, u32[]{:S(2)}) collective-permute-start(bf16[4,8192]{1,0:T(4,128)(2,1)S(1)} %add_convert_fusion.2), channel_id=1, source_target_pairs={{0,16},{1,17},{2,18},{3,19},{4,20},{5,21},{6,22},{7,23},{8,24},{9,... | collective-permute-start | bytes 196616 | tf_op jit(solution)/shard_map/ppermute | solution.py:264
  123.1 4.3 %collective-permute-start.10 = (bf16[4,8192]{1,0:T(4,128)(2,1)S(1)}, bf16[4,8192]{1,0:T(4,128)(2,1)S(1)}, u32[]{:S(2)}, u32[]{:S(2)}) collective-permute-start(bf16[4,8192]{1,0:T(4,128)(2,1)S(1)} %fusion.8), channel_id=1, source_target_pairs={{0,4},{1,5},{2,6},{3,7},{4,0},{5,1},{6,2},{7,3},{8,12},{9,13},{10,... | collective-permute-start | bytes 196616 | tf_op jit(solution)/shard_map/ppermute | solution.py:264
  127.7 5.0 %collective-permute-start.11 = (bf16[8,8192]{1,0:T(8,128)(2,1)S(1)}, bf16[8,8192]{1,0:T(8,128)(2,1)S(1)}, u32[]{:S(2)}, u32[]{:S(2)}) collective-permute-start(bf16[8,8192]{1,0:T(8,128)(2,1)S(1)} %pad_maximum_fusion.8), channel_id=1, source_target_pairs={{0,2},{1,3},{2,0},{3,1},{4,6},{5,7},{6,4},{7,5},{8,10},{9,11},{10,... | collective-permute-start | bytes 393224 | tf_op jit(solution)/shard_map/ppermute | solution.py:264
  132.8 46.7 %collective-permute-start.12 = (bf16[16,8192]{1,0:T(8,128)(2,1)S(1)}, bf16[16,8192]{1,0:T(8,128)(2,1)S(1)}, u32[]{:S(2)}, u32[]{:S(2)}) collective-permute-start(bf16[16,8192]{1,0:T(8,128)(2,1)S(1)} %pad_maximum_fusion.5), channel_id=1, source_target_pairs={{0,1},{1,0},{2,3},{3,2},{4,5},{5,4},{6,7},{7,6},{8,9},{9,8},{10,11... | collective-permute-start | bytes 786440 | tf_op jit(solution)/shard_map/ppermute | solution.py:264
  132.9 1.1 copy-start.11
  134.1 11.8 %copy-start.13 = (s32[2,128,768]{2,1,0:T(8,128)S(1)}, s32[2,128,768]{2,1,0:T(8,128)}, u32[]{:S(2)}) copy-start(s32[2,128,768]{2,1,0:T(8,128)} %zero_ref.9) | copy-start | bytes 2359300
  145.9 11.9 %copy-start.4 = (s32[2,12,8192]{2,1,0:T(8,128)S(1)}, s32[2,12,8192]{2,1,0:T(8,128)}, u32[]{:S(2)}) copy-start(s32[2,12,8192]{2,1,0:T(8,128)} %copy-done.3) | copy-start | bytes 2359300
  191.6 35.0 %copy-start.22 = (f32[1,8192]{1,0:T(1,128)S(1)}, f32[1,8192]{1,0:T(1,128)}, u32[]{:S(2)}) copy-start(f32[1,8192]{1,0:T(1,128)} %copy-done.21) | copy-start | bytes 98308
  191.6 35.3 %copy-start.18 = (bf16[2,2,8192]{2,1,0:T(2,128)(2,1)S(1)}, bf16[2,2,8192]{2,1,0:T(2,128)(2,1)}, u32[]{:S(2)}) copy-start(bf16[2,2,8192]{2,1,0:T(2,128)(2,1)} %copy-done.17) | copy-start | bytes 196612
  191.6 35.3 %copy-start.20 = (bf16[2,2,8192]{2,1,0:T(2,128)(2,1)S(1)}, bf16[2,2,8192]{2,1,0:T(2,128)(2,1)}, u32[]{:S(2)}) copy-start(bf16[2,2,8192]{2,1,0:T(2,128)(2,1)} %copy-done.19) | copy-start | bytes 196612
  204.9 1.7 collective-permute-start.13
  206.7 5.8 %collective-permute-start.14 = (bf16[8,8192]{1,0:T(8,128)(2,1)S(1)}, bf16[8,8192]{1,0:T(8,128)(2,1)S(1)}, u32[]{:S(2)}, u32[]{:S(2)}) collective-permute-start(bf16[8,8192]{1,0:T(8,128)(2,1)S(1)} %dynamic-slice_convert_fusion.4), channel_id=1, source_target_pairs={{0,2},{1,3},{2,0},{3,1},{4,6},{5,7},{6,4},{7,5},{8,10},{9,11},{10,... | collective-permute-start | bytes 393224 | tf_op jit(solution)/shard_map/ppermute | solution.py:264
  212.6 4.3 %collective-permute-start.15 = (bf16[4,8192]{1,0:T(4,128)(2,1)S(1)}, bf16[4,8192]{1,0:T(4,128)(2,1)S(1)}, u32[]{:S(2)}, u32[]{:S(2)}) collective-permute-start(bf16[4,8192]{1,0:T(4,128)(2,1)S(1)} %dynamic-slice_convert_fusion.7), channel_id=1, source_target_pairs={{0,4},{1,5},{2,6},{3,7},{4,0},{5,1},{6,2},{7,3},{8,12},{9,13},{10,... | collective-permute-start | bytes 196616 | tf_op jit(solution)/shard_map/ppermute | solution.py:264
  217.0 4.3 %collective-permute-start.16 = (bf16[4,8192]{1,0:T(4,128)(2,1)S(1)}, bf16[4,8192]{1,0:T(4,128)(2,1)S(1)}, u32[]{:S(2)}, u32[]{:S(2)}) collective-permute-start(bf16[4,8192]{1,0:T(4,128)(2,1)S(1)} %add_convert_fusion.1), channel_id=1, source_target_pairs={{0,8},{1,9},{2,10},{3,11},{4,12},{5,13},{6,14},{7,15},{8,0},{9,1},... | collective-permute-start | bytes 196616 | tf_op jit(solution)/shard_map/ppermute | solution.py:264
  221.4 5.2 %collective-permute-start.17 = (bf16[4,8192]{1,0:T(4,128)(2,1)S(1)}, bf16[4,8192]{1,0:T(4,128)(2,1)S(1)}, u32[]{:S(2)}, u32[]{:S(2)}) collective-permute-start(bf16[4,8192]{1,0:T(4,128)(2,1)S(1)} %add_convert_fusion), channel_id=1, source_target_pairs={{0,16},{1,17},{2,18},{3,19},{4,20},{5,21},{6,22},{7,23},{8,24},{9,... | collective-permute-start | bytes 196616 | tf_op jit(solution)/shard_map/ppermute | solution.py:264
  227.1 6.3 %copy-start.25 = (bf16[4,8192]{1,0:T(4,128)(2,1)}, bf16[4,8192]{1,0:T(4,128)(2,1)S(1)}, u32[]{:S(2)}) copy-start(bf16[4,8192]{1,0:T(4,128)(2,1)S(1)} %fusion.13) | copy-start | bytes 196612
  227.1 4.3 %collective-permute-start.18 = (bf16[4,8192]{1,0:T(4,128)(2,1)S(1)}, bf16[4,8192]{1,0:T(4,128)(2,1)S(1)}, u32[]{:S(2)}, u32[]{:S(2)}) collective-permute-start(bf16[4,8192]{1,0:T(4,128)(2,1)S(1)} %fusion.13), channel_id=1, source_target_pairs={{0,4},{1,5},{2,6},{3,7},{4,0},{5,1},{6,2},{7,3},{8,12},{9,13},{10,... | collective-permute-start | bytes 196616 | tf_op jit(solution)/shard_map/ppermute | solution.py:264
  231.6 5.0 %collective-permute-start.19 = (bf16[8,8192]{1,0:T(8,128)(2,1)S(1)}, bf16[8,8192]{1,0:T(8,128)(2,1)S(1)}, u32[]{:S(2)}, u32[]{:S(2)}) collective-permute-start(bf16[8,8192]{1,0:T(8,128)(2,1)S(1)} %pad_maximum_fusion.9), channel_id=1, source_target_pairs={{0,2},{1,3},{2,0},{3,1},{4,6},{5,7},{6,4},{7,5},{8,10},{9,11},{10,... | collective-permute-start | bytes 393224 | tf_op jit(solution)/shard_map/ppermute | solution.py:264
  236.7 0.7 copy-start.15
  236.7 1.4 copy-start.16
  238.1 2.2 collective-permute-start.20
  263.7 20.2 %copy-start.8 = (bf16[32,8192]{1,0:T(8,128)(2,1)S(1)}, bf16[32,8192]{1,0:T(8,128)(2,1)}, u32[]{:S(2)}) copy-start(bf16[32,8192]{1,0:T(8,128)(2,1)} %copy-done.7) | copy-start | bytes 1572868
  263.7 18.3 %collective-permute-start.21 = (bf16[16,8192]{1,0:T(8,128)(2,1)S(1)}, bf16[16,8192]{1,0:T(8,128)(2,1)S(1)}, u32[]{:S(2)}, u32[]{:S(2)}) collective-permute-start(bf16[16,8192]{1,0:T(8,128)(2,1)S(1)} %dynamic-slice_convert_fusion), channel_id=1, source_target_pairs={{0,1},{1,0},{2,3},{3,2},{4,5},{5,4},{6,7},{7,6},{8,9},{9,8},{10,11... | collective-permute-start | bytes 786440 | tf_op jit(solution)/shard_map/ppermute | solution.py:264
  282.1 10.0 %collective-permute-start.22 = (bf16[8,8192]{1,0:T(8,128)(2,1)S(1)}, bf16[8,8192]{1,0:T(8,128)(2,1)S(1)}, u32[]{:S(2)}, u32[]{:S(2)}) collective-permute-start(bf16[8,8192]{1,0:T(8,128)(2,1)S(1)} %dynamic-slice_convert_fusion.3), channel_id=1, source_target_pairs={{0,2},{1,3},{2,0},{3,1},{4,6},{5,7},{6,4},{7,5},{8,10},{9,11},{10,... | collective-permute-start | bytes 393224 | tf_op jit(solution)/shard_map/ppermute | solution.py:264
  283.9 19.5 %copy-start.6 = (bf16[32,8192]{1,0:T(8,128)(2,1)S(1)}, bf16[32,8192]{1,0:T(8,128)(2,1)}, u32[]{:S(2)}) copy-start(bf16[32,8192]{1,0:T(8,128)(2,1)} %copy-done.5) | copy-start | bytes 1572868
  292.2 9.8 %collective-permute-start.23 = (bf16[4,8192]{1,0:T(4,128)(2,1)S(1)}, bf16[4,8192]{1,0:T(4,128)(2,1)S(1)}, u32[]{:S(2)}, u32[]{:S(2)}) collective-permute-start(bf16[4,8192]{1,0:T(4,128)(2,1)S(1)} %dynamic-slice_convert_fusion.6), channel_id=1, source_target_pairs={{0,4},{1,5},{2,6},{3,7},{4,0},{5,1},{6,2},{7,3},{8,12},{9,13},{10,... | collective-permute-start | bytes 196616 | tf_op jit(solution)/shard_map/ppermute | solution.py:264
  302.1 10.2 %collective-permute-start.24 = (bf16[2,8192]{1,0:T(2,128)(2,1)S(1)}, bf16[2,8192]{1,0:T(2,128)(2,1)S(1)}, u32[]{:S(2)}, u32[]{:S(2)}) collective-permute-start(bf16[2,8192]{1,0:T(2,128)(2,1)S(1)} %dynamic-slice_convert_fusion.9), channel_id=1, source_target_pairs={{0,8},{1,9},{2,10},{3,11},{4,12},{5,13},{6,14},{7,15},{8,0},{9,1},... | collective-permute-start | bytes 98312 | tf_op jit(solution)/shard_map/ppermute | solution.py:264
  312.3 13.3 %copy-start.23 = (bf16[1,8192]{1,0:T(2,128)(2,1)S(1)}, bf16[1,8192]{1,0:T(2,128)(2,1)}, u32[]{:S(2)}) copy-start(bf16[1,8192]{1,0:T(2,128)(2,1)} %param.14) | copy-start | bytes 49156
  312.3 13.3 %copy-start.27 = (f32[2,8192]{1,0:T(2,128)S(1)}, f32[2,8192]{1,0:T(2,128)}, u32[]{:S(2)}) copy-start(f32[2,8192]{1,0:T(2,128)} %param.15) | copy-start | bytes 196612
  312.3 14.6 %copy-start.26 = (bf16[4,8192]{1,0:T(4,128)(2,1)S(1)}, bf16[4,8192]{1,0:T(4,128)(2,1)}, u32[]{:S(2)}) copy-start(bf16[4,8192]{1,0:T(4,128)(2,1)} %copy-done.25) | copy-start | bytes 196612
  312.4 13.2 %collective-permute-start.25 = (bf16[1,8192]{1,0:T(2,128)(2,1)S(1)}, bf16[1,8192]{1,0:T(2,128)(2,1)S(1)}, u32[]{:S(2)}, u32[]{:S(2)}) collective-permute-start(bf16[1,8192]{1,0:T(2,128)(2,1)S(1)} %dynamic-slice_convert_fusion.10), channel_id=1, source_target_pairs={{0,16},{1,17},{2,18},{3,19},{4,20},{5,21},{6,22},{7,23},{8,24},{9,... | collective-permute-start | bytes 49160 | tf_op jit(solution)/shard_map/ppermute | solution.py:264

commit v2 on v1

v2 whole, which is shorter than its diff:
```python
import functools

import jax
import jax.numpy as jnp
import numpy as np
from jax import lax
from jax.experimental import pallas as pl
from jax.experimental.pallas import tpu as pltpu
from jax.sharding import PartitionSpec as P

GROUP = 64
WORDS = GROUP // 4
LAYERS = 2
norm_epsilon = 1e-05
BF16 = jnp.bfloat16
F32 = jnp.float32
OFFSET = jnp.float8_e4m3fn
ANYWHERE = pl.BlockSpec(memory_space=pl.ANY)
IN_HBM = pl.BlockSpec(memory_space=pltpu.HBM)


def params(mib=60):
    return pltpu.CompilerParams(vmem_limit_bytes=mib * 2**20)


def cost(flops, bytes_accessed):
    return pl.CostEstimate(flops=int(flops), bytes_accessed=int(bytes_accessed), transcendentals=0)


def block_of(size, most):
    best = size
    if size > most:
        for candidate in range(128, most + 1, 128):
            if size % candidate == 0:
                best = candidate
    return best


def copy_in(source, target, sem):
    copy = pltpu.make_async_copy(source, target, sem)
    copy.start()
    return copy


def row_chunk(chunk, size):
    return pl.ds(pl.multiple_of(chunk * size, size), size)


def one_row(ref, row, cols):
    if len(ref.shape) == 2:
        return ref[row : row + 1, cols]
    held = ref.shape[1]
    return ref[row // held, row % held : row % held + 1, cols]


COUNT = 8
AHEAD = 2


def stream(count, copies, work, before=None, last=None):
    for chunk in range(AHEAD):
        for copy in copies(chunk):
            copy.start()
    if before is not None:
        before()

    def step(chunk, _):
        for copy in copies(chunk):
            copy.wait()

        @pl.when(chunk + AHEAD < count)
        def _():
            for copy in copies(chunk + AHEAD):
                copy.start()

        if last is not None:
            @pl.when(chunk + AHEAD >= count)
            def _():
                last(chunk + AHEAD - count)

        work(chunk)
        return 0

    lax.fori_loop(0, count, step, 0)


def offsets_kernel(layer, along_rows, count, code_any, zero_any, out_any, code, zero, out, planes, sems):
    words, width = code.shape
    rows = words // count if along_rows else words
    lanes = width if along_rows else width // count
    tile = planes.shape[-1]
    slots = planes.shape[0]

    def code_part(chunk):
        if along_rows:
            return (row_chunk(chunk, rows), slice(None))
        return (slice(None), row_chunk(chunk, lanes))

    def out_part(chunk):
        if along_rows:
            return (row_chunk(chunk, rows * 4), slice(None))
        return (slice(None), row_chunk(chunk, lanes))

    def code_copy(chunk):
        part = code_part(chunk)
        return pltpu.make_async_copy(code_any.at[(layer,) + part], code.at[part], sems.at[chunk])

    def out_copy(chunk):
        part = out_part(chunk)
        return pltpu.make_async_copy(out.at[part], out_any.at[part], sems.at[count + chunk])

    zero_copy = pltpu.make_async_copy(zero_any.at[layer], zero, sems.at[2 * count])
    zero_copy.start()
    groups = rows // WORDS

    def work(chunk):
        def unit(held, zeros, place, cols, slot):
            for piece in range(4):
                offset = ((held >> (2 * piece)) & 3) - zeros
                planes[slot, pl.ds(piece, WORDS, stride=4), :] = offset.astype(F32)
            out[place, cols] = planes[slot].astype(OFFSET)

        if along_rows:

            def some_groups(block, _):
                first = chunk * groups + block * 8
                for index in range(width // tile):
                    cols = slice(index * tile, (index + 1) * tile)
                    zeros = zero[row_chunk(first // 8, 8), cols]
                    for group in range(8):
                        held = code[row_chunk(first + group, WORDS), cols]
                        place = row_chunk(first + group, GROUP)
                        unit(held, zeros[group : group + 1], place, cols, group)
                return 0

            lax.fori_loop(0, groups // 8, some_groups, 0)
        else:

            def some_lanes(index, _):
                cols = pl.ds(pl.multiple_of(chunk * lanes + index * tile, tile), tile)
                for group in range(groups):
                    held = code[group * WORDS : (group + 1) * WORDS, cols]
                    place = slice(group * GROUP, (group + 1) * GROUP)
                    unit(held, one_row(zero, group, cols), place, cols, group % slots)
                return 0

            lax.fori_loop(0, lanes // tile, some_lanes, 0)
        out_copy(chunk).start()

    stream(count, lambda chunk: [code_copy(chunk)], work, zero_copy.wait)
    for chunk in range(count):
        out_copy(chunk).wait()


def offsets_of(codes, zeros, layer):
    _, words, width = codes.shape
    along_rows = words >= width
    tile = 128 if width % 128 == 0 else 64
    count = COUNT
    return pl.pallas_call(
        functools.partial(offsets_kernel, layer, along_rows, count),
        in_specs=[IN_HBM, IN_HBM],
        out_specs=IN_HBM,
        out_shape=jax.ShapeDtypeStruct((words * 4, width), OFFSET),
        scratch_shapes=[
            pltpu.VMEM((words, width), jnp.int32),
            pltpu.VMEM(zeros.shape[1:], jnp.int32),
            pltpu.VMEM((words * 4, width), OFFSET),
            pltpu.VMEM((8, GROUP, tile), F32),
            pltpu.SemaphoreType.DMA((2 * count + 1,)),
        ],
        compiler_params=params(),
        cost_estimate=cost(words * width * 40, words * width * 8),
    )(codes, zeros)


def sigmoid(value):
    return 1.0 / (1.0 + jnp.exp(-value))


def across(left, right):
    return lax.dot_general(left, right, (((1,), (1,)), ((), ())), preferred_element_type=F32)


def weights_of(offsets, steps):
    parts = []
    for group, step in enumerate(steps):
        part = offsets[group * GROUP : (group + 1) * GROUP].astype(F32)
        parts.append((part * step).astype(BF16))
    return jnp.concatenate(parts, axis=0)


class Matrix:
    def __init__(self, layer, source, step_source, offsets, steps, sems, by_rows):
        self.layer, self.source, self.step_source = layer, source, step_source
        self.offsets, self.steps, self.sems, self.by_rows = offsets, steps, sems, by_rows
        self.count = COUNT
        self.size = offsets.shape[0 if by_rows else 1] // self.count

    def part(self, chunk):
        if self.by_rows:
            return (row_chunk(chunk, self.size), slice(None))
        return (slice(None), row_chunk(chunk, self.size))

    def step_copy(self):
        return pltpu.make_async_copy(
            self.step_source.at[self.layer], self.steps, self.sems.at[self.count]
        )

    def copy(self, chunk):
        part = self.part(chunk)
        return pltpu.make_async_copy(self.source.at[part], self.offsets.at[part], self.sems.at[chunk])

    def weights(self, chunk):
        offsets = self.offsets[self.part(chunk)]
        groups = offsets.shape[0] // GROUP
        if self.by_rows:
            held = self.steps[row_chunk(chunk, groups), :]
            steps = [held[group : group + 1] for group in range(groups)]
        else:
            cols = row_chunk(chunk, self.size)
            steps = [one_row(self.steps, group, cols) for group in range(groups)]
        return weights_of(offsets, steps)

    @staticmethod
    def scratch(offsets, steps):
        return [
            pltpu.VMEM(offsets.shape, OFFSET),
            pltpu.VMEM(steps.shape[1:], F32),
            pltpu.SemaphoreType.DMA((COUNT + 1,)),
        ]


def gate_up_forward(x, gate, up, gate_out, up_out, before, last=None):
    def work(chunk):
        rows = x[:, row_chunk(chunk, gate.size)]
        gate_out[...] += jnp.dot(rows, gate.weights(chunk), preferred_element_type=F32)
        up_out[...] += jnp.dot(rows, up.weights(chunk), preferred_element_type=F32)

    def ready():
        gate_out[...] = jnp.zeros_like(gate_out)
        up_out[...] = jnp.zeros_like(up_out)
        before()
        gate.step_copy().wait()
        up.step_copy().wait()

    gate.step_copy().start()
    up.step_copy().start()
    stream(gate.count, lambda chunk: [gate.copy(chunk), up.copy(chunk)], work, ready, last)
    gate_all = gate_out[...]
    return (gate_all * sigmoid(gate_all) * up_out[...]).astype(BF16)


def hidden_back(hidden_grad, gate_pre, up_value):
    gate_sigmoid = sigmoid(gate_pre)
    gate_grad = (
        hidden_grad * up_value * gate_sigmoid * (1.0 + gate_pre * (1.0 - gate_sigmoid))
    ).astype(BF16)
    up_grad = (hidden_grad * gate_pre * gate_sigmoid).astype(BF16)
    return gate_grad, up_grad


def gate_up_backward(gate_grad, up_grad, gate, up, out, chunk):
    part = across(gate_grad, gate.weights(chunk)) + across(up_grad, up.weights(chunk))
    out[:, row_chunk(chunk, gate.size)] = part.astype(BF16)


def cot_down(cot, down, out, before, last=None):
    def work(chunk):
        out[...] += across(cot[:, row_chunk(chunk, down.size)], down.weights(chunk))

    def ready():
        out[...] = jnp.zeros_like(out)
        before()
        down.step_copy().wait()

    down.step_copy().start()
    stream(down.count, lambda chunk: [down.copy(chunk)], work, ready, last)


def later(count, copies, work):
    def step(chunk, _):
        for copy in copies(chunk):
            copy.wait()

        @pl.when(chunk + AHEAD < count)
        def _():
            for copy in copies(chunk + AHEAD):
                copy.start()

        work(chunk)
        return 0

    lax.fori_loop(0, count, step, 0)


def first_forward_kernel(layer, x_any, gate_any, up_any, down_any, gs_any, us_any, ds_any, *refs):
    gate_out, up_out, hidden_out, part_out = refs[:4]
    x, sem = refs[4:6]
    gate = Matrix(layer, gate_any, gs_any, *refs[6:9], True)
    up = Matrix(layer, up_any, us_any, *refs[9:12], True)
    down = Matrix(layer, down_any, ds_any, *refs[12:15], False)
    x_copy = copy_in(x_any, x, sem.at[0])

    def last(chunk):
        down.copy(chunk).start()

    hidden = gate_up_forward(x, gate, up, gate_out, up_out, x_copy.wait, last)
    down.step_copy().start()
    hidden_out[...] = hidden
    down.step_copy().wait()

    def work(chunk):
        part = jnp.dot(hidden_out[...], down.weights(chunk), preferred_element_type=F32)
        part_out[:, row_chunk(chunk, down.size)] = part.astype(BF16)

    later(down.count, lambda chunk: [down.copy(chunk)], work)


def first_forward(layer, x, gate, up, down, gate_step, up_step, down_step):
    tokens, depth = x.shape
    width = gate.shape[1]
    return pl.pallas_call(
        functools.partial(first_forward_kernel, layer),
        in_specs=[ANYWHERE] + [IN_HBM] * 6,
        out_shape=[
            jax.ShapeDtypeStruct((tokens, width), F32),
            jax.ShapeDtypeStruct((tokens, width), F32),
            jax.ShapeDtypeStruct((tokens, width), BF16),
            jax.ShapeDtypeStruct((tokens, depth), BF16),
        ],
        scratch_shapes=[pltpu.VMEM(x.shape, BF16), pltpu.SemaphoreType.DMA((1,))]
        + Matrix.scratch(gate, gate_step)
        + Matrix.scratch(up, up_step)
        + Matrix.scratch(down, down_step),
        compiler_params=params(),
        cost_estimate=cost(6 * tokens * depth * width, 3 * depth * width),
    )(x, gate, up, down, gate_step, up_step, down_step)


def hidden_grad_kernel(layer, cot_any, down_any, ds_any, out, cot, sem, *refs):
    down = Matrix(layer, down_any, ds_any, *refs, False)
    cot_copy = copy_in(cot_any, cot, sem.at[0])
    cot_down(cot, down, out, cot_copy.wait)


def hidden_grad_of(layer, cot, down, down_step):
    tokens, features = cot.shape
    return pl.pallas_call(
        functools.partial(hidden_grad_kernel, layer),
        in_specs=[ANYWHERE] + [IN_HBM] * 2,
        out_shape=jax.ShapeDtypeStruct((tokens, down.shape[0]), F32),
        scratch_shapes=[pltpu.VMEM(cot.shape, BF16), pltpu.SemaphoreType.DMA((1,))]
        + Matrix.scratch(down, down_step),
        compiler_params=params(),
        cost_estimate=cost(2 * tokens * features * down.shape[0], features * down.shape[0]),
    )(cot, down, down_step)


def last_layer_kernel(layer, x_any, grad_any, gate_any, up_any, gs_any, us_any, *refs):
    hidden_out, gate_grad_out, up_grad_out, part_out = refs[:4]
    gate_pre, up_value, x, hidden_grad, sem = refs[4:9]
    gate = Matrix(layer, gate_any, gs_any, *refs[9:12], True)
    up = Matrix(layer, up_any, us_any, *refs[12:15], True)
    x_copy = copy_in(x_any, x, sem.at[0])
    grad_copy = copy_in(grad_any, hidden_grad, sem.at[1])
    hidden_out[...] = gate_up_forward(x, gate, up, gate_pre, up_value, x_copy.wait)
    grad_copy.wait()
    gate_grad, up_grad = hidden_back(hidden_grad[...], gate_pre[...], up_value[...])
    gate_grad_out[...] = gate_grad
    up_grad_out[...] = up_grad

    def work(chunk, _):
        gate_up_backward(gate_grad_out[...], up_grad_out[...], gate, up, part_out, chunk)
        return 0

    lax.fori_loop(0, gate.count, work, 0)


def last_layer(layer, x, hidden_grad, gate, up, gate_step, up_step):
    tokens, depth = x.shape
    width = gate.shape[1]
    small = jax.ShapeDtypeStruct((tokens, width), BF16)
    return pl.pallas_call(
        functools.partial(last_layer_kernel, layer),
        in_specs=[ANYWHERE] * 2 + [IN_HBM] * 4,
        out_shape=[small, small, small, jax.ShapeDtypeStruct((tokens, depth), BF16)],
        scratch_shapes=[
            pltpu.VMEM((tokens, width), F32),
            pltpu.VMEM((tokens, width), F32),
            pltpu.VMEM(x.shape, BF16),
            pltpu.VMEM((tokens, width), F32),
            pltpu.SemaphoreType.DMA((2,)),
        ]
        + Matrix.scratch(gate, gate_step)
        + Matrix.scratch(up, up_step),
        compiler_params=params(),
        cost_estimate=cost(8 * tokens * depth * width, 2 * depth * width),
    )(x, hidden_grad, gate, up, gate_step, up_step)


def backward_kernel(layer, cot_any, pre_any, value_any, gate_any, up_any, down_any, gs_any, us_any, ds_any, *refs):
    gate_grad_out, up_grad_out, part_out = refs[:3]
    cot, gate_pre, up_value, hidden_grad, sem = refs[3:8]
    gate = Matrix(layer, gate_any, gs_any, *refs[8:11], True)
    up = Matrix(layer, up_any, us_any, *refs[11:14], True)
    down = Matrix(layer, down_any, ds_any, *refs[14:17], False)
    cot_copy = copy_in(cot_any, cot, sem.at[0])
    pre_copy = copy_in(pre_any, gate_pre, sem.at[1])
    value_copy = copy_in(value_any, up_value, sem.at[2])

    def last(chunk):
        gate.copy(chunk).start()
        up.copy(chunk).start()

    cot_down(cot, down, hidden_grad, cot_copy.wait, last)
    gate.step_copy().start()
    up.step_copy().start()
    pre_copy.wait()
    value_copy.wait()
    gate_grad, up_grad = hidden_back(hidden_grad[...], gate_pre[...], up_value[...])
    gate_grad_out[...] = gate_grad
    up_grad_out[...] = up_grad
    gate.step_copy().wait()
    up.step_copy().wait()

    def work(chunk):
        gate_up_backward(gate_grad_out[...], up_grad_out[...], gate, up, part_out, chunk)

    later(gate.count, lambda chunk: [gate.copy(chunk), up.copy(chunk)], work)


def backward(layer, cot, gate_pre, up_value, gate, up, down, gate_step, up_step, down_step):
    tokens, depth = cot.shape
    width = gate.shape[1]
    small = jax.ShapeDtypeStruct((tokens, width), BF16)
    return pl.pallas_call(
        functools.partial(backward_kernel, layer),
        in_specs=[ANYWHERE] * 3 + [IN_HBM] * 6,
        out_shape=[small, small, jax.ShapeDtypeStruct((tokens, depth), BF16)],
        scratch_shapes=[
            pltpu.VMEM(cot.shape, BF16),
            pltpu.VMEM((tokens, width), F32),
            pltpu.VMEM((tokens, width), F32),
            pltpu.VMEM((tokens, width), F32),
            pltpu.SemaphoreType.DMA((3,)),
        ]
        + Matrix.scratch(gate, gate_step)
        + Matrix.scratch(up, up_step)
        + Matrix.scratch(down, down_step),
        compiler_params=params(),
        cost_estimate=cost(6 * tokens * depth * width, 3 * depth * width),
    )(cot, gate_pre, up_value, gate, up, down, gate_step, up_step, down_step)


def spread(x, groups):
    tokens = x.shape[0]
    tall = jnp.concatenate([x] * groups, axis=0)
    row_group = lax.broadcasted_iota(jnp.int32, tall.shape, 0) // tokens
    col_group = lax.broadcasted_iota(jnp.int32, tall.shape, 1) // GROUP
    return jnp.where(row_group == col_group, tall.astype(F32), 0.0).astype(BF16)


def step_grad_block(x, offsets, upstream):
    tokens = x.shape[0]
    rows = []
    groups = offsets.shape[0] // GROUP
    for first in range(0, groups, 4):
        count = min(4, groups - first)
        part = slice(first * GROUP, (first + count) * GROUP)
        product = jnp.dot(
            spread(x[:, part], count), offsets[part, :].astype(BF16), preferred_element_type=F32
        )
        for group in range(count):
            own = product[group * tokens : (group + 1) * tokens] * upstream
            rows.append(jnp.sum(own, axis=0, keepdims=True))
    return jnp.concatenate(rows, axis=0)


def step_grad_kernel(by_rows, x_any, off_any, grad_any, *refs):
    out, x, offsets, grad, sem, sems = refs[-6:]
    count = sems.shape[0]
    size = offsets.shape[0 if by_rows else 1] // count

    def copy(chunk):
        part = (row_chunk(chunk, size), slice(None)) if by_rows else (slice(None), row_chunk(chunk, size))
        return pltpu.make_async_copy(off_any.at[part], offsets.at[part], sems.at[chunk])

    x_copy = copy_in(x_any, x, sem.at[0])
    grad_copy = copy_in(grad_any, grad, sem.at[1])
    def ready():
        x_copy.wait()
        grad_copy.wait()

    def work(chunk):
        part = row_chunk(chunk, size)
        if by_rows:
            out[row_chunk(chunk, size // GROUP), :] = step_grad_block(
                x[:, part], offsets[part, :], grad[...].astype(F32)
            )
        else:
            found = step_grad_block(x[...], offsets[:, part], grad[:, part].astype(F32))
            held = out.shape[1]
            for place in range(out.shape[0]):
                out[place, :, part] = found[place * held : (place + 1) * held]

    stream(count, lambda chunk: [copy(chunk)], work, ready)


def step_grad(x, offsets, upstream, shape, layer, earlier):
    tokens, depth = x.shape
    width = offsets.shape[1]
    by_rows = depth >= width
    operands = [x, offsets, upstream]
    aliases = {}
    if earlier is not None:
        operands.append(earlier)
        aliases = {3: 0}
    return pl.pallas_call(
        functools.partial(step_grad_kernel, by_rows),
        grid=(1,),
        in_specs=[ANYWHERE, IN_HBM, ANYWHERE, IN_HBM][: len(operands)],
        out_specs=pl.BlockSpec((None,) + shape[1:], lambda i: (layer,) + (0,) * (len(shape) - 1)),
        out_shape=jax.ShapeDtypeStruct(shape, F32),
        scratch_shapes=[
            pltpu.VMEM(x.shape, BF16),
            pltpu.VMEM(offsets.shape, OFFSET),
            pltpu.VMEM(upstream.shape, BF16),
            pltpu.SemaphoreType.DMA((2,)),
            pltpu.SemaphoreType.DMA((COUNT,)),
        ],
        input_output_aliases=aliases,
        compiler_params=params(),
        cost_estimate=cost(8 * tokens * depth * width, depth * width),
    )(*operands)


class Side:
    def __init__(self):
        self.jobs = []

    def add(self, call, *operands):
        job = [call, operands, None]
        self.jobs.append(job)
        return job

    def skip(self):
        self.jobs.append(None)

    def swap(self, value, bit):
        count = lax.axis_size("tensor")
        pairs = [(i, i ^ bit) for i in range(count)]
        job = self.jobs.pop(0) if self.jobs else None
        if job is None:
            return lax.ppermute(value, "tensor", pairs)
        value, operands = lax.optimization_barrier((value, job[1]))
        got = lax.ppermute(value, "tensor", pairs)
        got, job[2] = lax.optimization_barrier((got, job[0](*operands)))
        return got

    def finish(self):
        for job in self.jobs:
            if job is not None:
                job[2] = job[0](*job[1])
        self.jobs = []


def own_bit(bit):
    return (lax.axis_index("tensor") // bit) % 2


def halve(side, value, bit):
    half = value.shape[0] // 2
    mine = own_bit(bit)
    kept = lax.dynamic_slice_in_dim(value, mine * half, half, 0)
    sent = lax.dynamic_slice_in_dim(value, (1 - mine) * half, half, 0)
    got = side.swap(sent.astype(BF16), bit)
    return kept.astype(F32) + got.astype(F32)


def add_up(side, value, bit):
    rounded = value.astype(BF16)
    return rounded.astype(F32) + side.swap(rounded, bit).astype(F32)


def double(side, value, bit, axis):
    other = side.swap(value, bit)
    mine = own_bit(bit) == 0
    return jnp.concatenate(
        [jnp.where(mine, value, other), jnp.where(mine, other, value)], axis=axis
    )


def inverse_rms(values):
    return lax.rsqrt(jnp.mean(values * values, axis=-1, keepdims=True) + norm_epsilon)


def norm_rows(state, gain):
    values = state.astype(F32)
    return (values * inverse_rms(values) * gain).astype(BF16)


def norm_back(state, gain, upstream):
    values = state.astype(F32)
    scale = inverse_rms(values)
    normal = values * scale
    inner = upstream * gain
    return scale * (inner - normal * jnp.mean(inner * normal, axis=-1, keepdims=True))


def token_lengths(doc_lengths, index_rows, micro_rows):
    batch_index = index_rows // micro_rows
    position = index_rows % micro_rows
    picked = batch_index[:, None] == jnp.arange(doc_lengths.shape[0], dtype=jnp.int32)[None, :]
    chosen = jnp.sum(jnp.where(picked[:, :, None], doc_lengths[None, :, :], 0), axis=1)
    ends = jnp.sum(
        jnp.where(
            jnp.arange(chosen.shape[1])[:, None] <= jnp.arange(chosen.shape[1])[None, :],
            chosen[:, :, None],
            0,
        ),
        axis=1,
    )
    starts = ends - chosen
    inside = (position[:, None] >= starts) & (position[:, None] < ends)
    return jnp.sum(jnp.where(inside, chosen, 0), axis=1).astype(F32)


def on_device(
    tokens,
    norm_gain,
    gate_codes,
    up_codes,
    down_codes,
    gate_zero,
    up_zero,
    down_zero,
    gate_step,
    up_step,
    down_step,
    out_grad,
    doc_lengths,
):
    shard_rows, features = tokens.shape
    device_count = lax.axis_size("tensor")
    micro_rows = shard_rows * device_count // doc_lengths.shape[0]
    bits = [1 << k for k in range(device_count.bit_length() - 1)]
    near, far = bits[:-2], bits[-2:]

    far_count = 1 << len(far)
    far_index = np.arange(far_count)
    far_place = sum(((far_index >> k) & 1) << (len(far) - 1 - k) for k in range(len(far)))
    far_device = np.argsort(far_place)
    near_part = lax.axis_index("tensor") % (1 << len(near))
    device_ids = near_part + jnp.asarray(far_device << len(near), jnp.int32)
    row_ids = (
        device_ids[:, None] * shard_rows + jnp.arange(shard_rows, dtype=jnp.int32)[None, :]
    ).reshape(-1)
    lengths = token_lengths(doc_lengths, row_ids, micro_rows)

    down_shape = down_step.shape
    held = 4 if down_shape[1] % 4 == 0 else down_shape[1]
    tiled = (down_shape[0], down_shape[1] // held, held, down_shape[2])
    down_step, down_zero = down_step.reshape(tiled), down_zero.reshape(tiled)

    def offsets_job(side, codes, zeros, layer):
        return side.add(lambda c, z: offsets_of(c, z, layer), codes, zeros)

    side = Side()
    gate_job = offsets_job(side, gate_codes, gate_zero, 0)
    up_job = offsets_job(side, up_codes, up_zero, 0)
    down_job = offsets_job(side, down_codes, down_zero, 0)
    pair = jnp.stack([tokens, out_grad])
    for bit in reversed(far):
        pair = double(side, pair, bit, 1)
    state_0 = pair[0]
    cot_rows = (pair[1].astype(F32) / lengths[:, None]).astype(BF16)
    pair = jnp.stack([norm_rows(state_0, norm_gain[0]), cot_rows])
    for bit in reversed(near):
        pair = double(side, pair, bit, 1)
    side.finish()
    normed_0, cotangent = pair[0], pair[1]
    gate_0, up_0, down_0 = gate_job[2], up_job[2], down_job[2]

    gate_pre, up_value, hidden_0, part = first_forward(
        0, normed_0, gate_0, up_0, down_0, gate_step, up_step, down_step
    )

    side = Side()
    side.skip()
    gate_job1 = offsets_job(side, gate_codes, gate_zero, 1)
    up_job1 = offsets_job(side, up_codes, up_zero, 1)
    down_job1 = offsets_job(side, down_codes, down_zero, 1)
    grad_job = side.add(
        lambda c, s: hidden_grad_of(1, c, down_job1[2], s), cotangent, down_step
    )
    for bit in near:
        part = halve(side, part, bit)
    for bit in far:
        part = add_up(side, part, bit)
    state_1 = (state_0.astype(F32) + part).astype(BF16)
    normed_1 = norm_rows(state_1, norm_gain[1])
    for bit in reversed(near):
        normed_1 = double(side, normed_1, bit, 0)
    side.finish()
    gate_1, up_1, down_1, hidden_grad = gate_job1[2], up_job1[2], down_job1[2], grad_job[2]

    hidden_1, gate_grad, up_grad, part = last_layer(
        1, normed_1, hidden_grad, gate_1, up_1, gate_step, up_step
    )
    side = Side()
    side.skip()
    down_out = side.add(lambda x, u: step_grad(x, down_1, u, tiled, 1, None), hidden_1, cotangent)
    gate_out = side.add(lambda x, u: step_grad(x, gate_1, u, gate_step.shape, 1, None), normed_1, gate_grad)
    up_out = side.add(lambda x, u: step_grad(x, up_1, u, up_step.shape, 1, None), normed_1, up_grad)
    for bit in near:
        part = halve(side, part, bit)
    for bit in far:
        part = add_up(side, part, bit)
    cot_rows = (cot_rows.astype(F32) + norm_back(state_1, norm_gain[1], part)).astype(BF16)
    cotangent = cot_rows
    for bit in reversed(near):
        cotangent = double(side, cotangent, bit, 0)
    side.finish()
    down_out, gate_out, up_out = down_out[2], gate_out[2], up_out[2]

    gate_grad, up_grad, part = backward(
        0, cotangent, gate_pre, up_value, gate_0, up_0, down_0, gate_step, up_step, down_step
    )
    side = Side()
    side.skip()
    down_job = side.add(
        lambda x, u, e: step_grad(x, down_0, u, tiled, 0, e), hidden_0, cotangent, down_out
    )
    gate_job = side.add(
        lambda x, u, e: step_grad(x, gate_0, u, gate_step.shape, 0, e), normed_0, gate_grad, gate_out
    )
    up_job = side.add(lambda x, u, e: step_grad(x, up_0, u, up_step.shape, 0, e), normed_0, up_grad, up_out)
    for bit in near:
        part = halve(side, part, bit)
    for bit in far:
        part = halve(side, part, bit)
        half = cot_rows.shape[0] // 2
        cot_rows = lax.dynamic_slice_in_dim(cot_rows, own_bit(bit) * half, half, 0)
    side.finish()
    result = (cot_rows.astype(F32) + norm_back(tokens, norm_gain[0], part)).astype(BF16)
    return result, gate_job[2], up_job[2], down_job[2].reshape(down_shape)


def solution(mesh):
    placed = (
        P(("groups", "tensor"), None),
        P(),
        P(None, None, "tensor"),
        P(None, None, "tensor"),
        P(None, "tensor", None),
        P(None, None, "tensor"),
        P(None, None, "tensor"),
        P(None, "tensor", None),
        P(None, None, "tensor"),
        P(None, None, "tensor"),
        P(None, "tensor", None),
        P(("groups", "tensor"), None),
        P("groups", None),
    )
    return jax.shard_map(
        on_device,
        mesh=mesh,
        in_specs=placed,
        out_specs=(
            P(("groups", "tensor"), None),
            P("groups", None, "tensor"),
            P("groups", None, "tensor"),
            P("groups", "tensor", None),
        ),
        check_vma=False,
    )
```

time: 331 us -> 234 us (0.71)
  Pallas kernels: 201 us -> 142 us
  waiting for transfers between devices: 50.9 us -> 31.3 us
  starting transfers between devices: 39.7 us -> 28.2 us
  local copies, waits for them, and re-layouts: 16.2 us -> 12.1 us
    pallas_call x19 -> x16, Pallas kernels: 201 us -> 142 us  [the longest x6 48 us: offsets_of(): pl.pallas_call(functools.partial(offsets_kernel, layer, along_rows, count...]
    ppermute x26, waiting for transfers between devices: 50.9 us -> 31.3 us  [the longest x13 31.3 us: swap(): return lax.ppermute(value, 'tensor', pairs)]
    unnamed x60 -> x13, local copies, waits for them, and re-layouts: 12.8 us -> 0.79 us
    ppermute x26, starting transfers between devices: 39.7 us -> 28.2 us  [the longest x13 16.4 us: swap(): got = lax.ppermute(value, 'tensor', pairs)]
    optimization_barrier x0 -> x4, local copies, waits for them, and re-layouts: none -> 5.65 us  [the longest x3 4.16 us: swap(): value, operands = lax.optimization_barrier((value, job[1]))]
  transfers between devices with their start and end apart: 26 -> 26, of which waited for: 18 -> 12; matrix products, arithmetic and copies ran while one was open for 3% -> 5% of each run, Pallas kernels for 41% -> 41%
where the time goes in v2:
time: 234 us; the launch traced here: 231 us
  Pallas kernels  142 us (61%)
  waiting for transfers between devices  31.3 us (13%)
  starting transfers between devices  28.2 us (12%)
  other arithmetic  14.6 us (6%)
  local copies, waits for them, and re-layouts  12.1 us (5%)
  between operations  2.6 us (1%)
    pallas_call x6, Pallas kernels, offsets_of(): pl.pallas_call(functools.partial(offsets_kernel, layer, along_rows, count...  48 us
    pallas_call x6, Pallas kernels, step_grad(): pl.pallas_call(functools.partial(step_grad_kernel, by_rows), grid=(1,), i...  39.2 us
    ppermute x13, waiting for transfers between devices, swap(): return lax.ppermute(value, 'tensor', pairs)  31.3 us
    pallas_call x1, Pallas kernels, last_layer(): pl.pallas_call(functools.partial(last_layer_kernel, layer), in_specs=[ANY...  17.1 us
    pallas_call x1, Pallas kernels, backward(): pl.pallas_call(functools.partial(backward_kernel, layer), in_specs=[ANYWH...  16.9 us
    ppermute x13, starting transfers between devices, swap(): got = lax.ppermute(value, 'tensor', pairs)  16.4 us
    pallas_call x1, Pallas kernels, first_forward(): pl.pallas_call(functools.partial(first_forward_kernel, layer), in_specs=[...  14.3 us
    ppermute x13, starting transfers between devices, swap(): return lax.ppermute(value, 'tensor', pairs)  11.8 us
  transfers between devices with their start and end apart: 26, of which 12 were waited for; matrix products, arithmetic and copies ran while one was open for 5% of the time, Pallas kernels for 41%

profile of v2, /device:TPU:0, one launch (start us, length us, event | category | flops | bytes accessed | tf_op | source)
XLA Modules:
  0.0 231.1 jit_solution(8498841936042235726)
XLA Ops:
  0.6 0.9 pad_maximum_fusion.11
  1.5 4.1 %collective-permute-start = (bf16[2,1,8192]{2,1,0:T(2,128)(2,1)S(1)}, bf16[2,1,8192]{2,1,0:T(2,128)(2,1)S(1)}, u32[]{:S(2)}, u32[]{:S(2)}) collective-permute-start(bf16[2,1,8192]{2,1,0:T(2,128)(2,1)S(1)} %pad_maximum_fusion.11), channel_id=1, source_target_pairs={{0,16},{1,17},{2,18},{3,19},{4,20},{5,21},{6,22},{7,23},{8,24},{9,... | collective-permute-start | bytes 98312 | tf_op jit(solution)/shard_map/ppermute | solution.py:557
  5.6 0.7 and_select_fusion.1
  6.3 0.7 and_select_fusion
  7.0 0.8 copy.30
  7.8 1.0 fusion.25
  9.1 7.9 %shard_map.165.gate_any.off_any = f8e4m3fn[8192,768]{1,0:T(32,128)(4,1)} custom-call(s32[2,2048,768]{2,1,0:T(8,128)} %code_any.3, s32[2,128,768]{2,1,0:T(8,128)} %zero_any.2), custom_call_target="tpu_custom_call" | custom-call | flops 62914560 | bytes 12582912 | tf_op jit(solution)/shard_map/pallas_call | solution.py:160
  17.4 1.6 collective-permute-start.1
  19.1 7.9 %shard_map.166.up_any.off_any = f8e4m3fn[8192,768]{1,0:T(32,128)(4,1)} custom-call(s32[2,2048,768]{2,1,0:T(8,128)} %code_any.4, s32[2,128,768]{2,1,0:T(8,128)} %zero_any.3), custom_call_target="tpu_custom_call" | custom-call | flops 62914560 | bytes 12582912 | tf_op jit(solution)/shard_map/pallas_call | solution.py:160
  27.7 1.6 collective-permute-start.2
  29.3 1.4 copy.34.zero_any
  30.7 8.2 %shard_map.167.down_any.off_any = f8e4m3fn[768,8192]{1,0:T(32,128)(4,1)} custom-call(s32[2,192,8192]{2,1,0:T(8,128)} %code_any.5, s32[2,3,4,8192]{3,2,1,0:T(4,128)} %copy.34.zero_any), custom_call_target="tpu_custom_call" | custom-call | flops 62914560 | bytes 12582912 | tf_op jit(solution)/shard_map/pallas_call | solution.py:160
  39.2 1.6 collective-permute-start.3
  40.8 5.7 %collective-permute-done.3 = bf16[2,8,8192]{2,1,0:T(8,128)(2,1)S(1)} collective-permute-done((bf16[2,8,8192]{2,1,0:T(8,128)(2,1)S(1)}, bf16[2,8,8192]{2,1,0:T(8,128)(2,1)S(1)}, u32[]{:S(2)}, u32[]{:S(2)}) %collective-permute-start.3) | collective-permute-done | bytes 262176 | tf_op jit(solution)/shard_map/ppermute | solution.py:555
  46.7 0.8 pad_maximum_fusion.1
  47.5 1.4 copy.35.ds_any
  48.9 0.7 collective-permute-done.4
  49.8 1.0 fusion.2
  50.8 14.3 %shard_map.168 = (f32[32,768]{1,0:T(8,128)}, f32[32,768]{1,0:T(8,128)}, bf16[32,768]{1,0:T(8,128)(2,1)}, bf16[32,8192]{1,0:T(8,128)(2,1)}) custom-call(bf16[32,8192]{1,0:T(8,128)(2,1)} %get-tuple-element.155.x_any, f8e4m3fn[8192,768]{1,0:T(32,128)(4,1)} %shard_map.165.gate_any.off_any, f8e4m3fn[8192,768]{1,0:T(32,128)(4,1)} %shard_map.166.up_any.off_any, ...), custom_call_target="tpu_custom_call" | custom-call | flops 1207959552 | bytes 18874368 | tf_op jit(solution)/shard_map/pallas_call | solution.py:323
  65.2 1.0 constant_dynamic-slice_fusion.2
  66.4 1.4 collective-permute-done.5
  67.8 1.0 convert_add_fusion.2
  68.8 1.6 collective-permute-start.6
  70.4 7.9 %shard_map.169.gate_any.off_any = f8e4m3fn[8192,768]{1,0:T(32,128)(4,1)} custom-call(s32[2,2048,768]{2,1,0:T(8,128)} %code_any.3, s32[2,128,768]{2,1,0:T(8,128)} %zero_any.2), custom_call_target="tpu_custom_call" | custom-call | flops 62914560 | bytes 12582912 | tf_op jit(solution)/shard_map/pallas_call | solution.py:160
  78.9 8.0 %shard_map.170.up_any.off_any = f8e4m3fn[8192,768]{1,0:T(32,128)(4,1)} custom-call(s32[2,2048,768]{2,1,0:T(8,128)} %code_any.4, s32[2,128,768]{2,1,0:T(8,128)} %zero_any.3), custom_call_target="tpu_custom_call" | custom-call | flops 62914560 | bytes 12582912 | tf_op jit(solution)/shard_map/pallas_call | solution.py:160
  87.5 1.4 copy.36.zero_any
  88.9 8.1 %shard_map.171.down_any.off_any = f8e4m3fn[768,8192]{1,0:T(32,128)(4,1)} custom-call(s32[2,192,8192]{2,1,0:T(8,128)} %code_any.5, s32[2,3,4,8192]{3,2,1,0:T(4,128)} %copy.36.zero_any), custom_call_target="tpu_custom_call" | custom-call | flops 62914560 | bytes 12582912 | tf_op jit(solution)/shard_map/pallas_call | solution.py:160
  97.4 1.4 copy.37.ds_any
  98.8 6.9 %shard_map.172.grad_any = f32[32,768]{1,0:T(8,128)} custom-call(bf16[32,8192]{1,0:T(8,128)(2,1)} %get-tuple-element.123.cot_any.grad_any, f8e4m3fn[768,8192]{1,0:T(32,128)(4,1)} %shard_map.171.down_any.off_any, f32[2,3,4,8192]{3,2,1,0:T(4,128)} %copy.37.ds_any), custom_call_target="tpu_custom_call" | custom-call | flops 402653184 | bytes 6291456 | tf_op jit(solution)/shard_map/pallas_call | solution.py:349
  106.0 1.6 collective-permute-start.10
  107.6 2.7 %collective-permute-done.10 = bf16[4,8192]{1,0:T(4,128)(2,1)S(1)} collective-permute-done((bf16[4,8192]{1,0:T(4,128)(2,1)S(1)}, bf16[4,8192]{1,0:T(4,128)(2,1)S(1)}, u32[]{:S(2)}, u32[]{:S(2)}) %collective-permute-start.10) | collective-permute-done | bytes 65568 | tf_op jit(solution)/shard_map/ppermute | solution.py:555
  111.2 4.4 %collective-permute-done.11 = bf16[8,8192]{1,0:T(8,128)(2,1)S(1)} collective-permute-done((bf16[8,8192]{1,0:T(8,128)(2,1)S(1)}, bf16[8,8192]{1,0:T(8,128)(2,1)S(1)}, u32[]{:S(2)}, u32[]{:S(2)}) %collective-permute-start.11) | collective-permute-done | bytes 131104 | tf_op jit(solution)/shard_map/ppermute | solution.py:555
  115.8 1.5 collective-permute-done.12
  117.4 0.8 pad_maximum_fusion.2.x_any
  118.3 17.1 %shard_map.173 = (bf16[32,768]{1,0:T(8,128)(2,1)}, bf16[32,768]{1,0:T(8,128)(2,1)}, bf16[32,768]{1,0:T(8,128)(2,1)}, bf16[32,8192]{1,0:T(8,128)(2,1)}) custom-call(bf16[32,8192]{1,0:T(8,128)(2,1)} %pad_maximum_fusion.2.x_any, f32[32,768]{1,0:T(8,128)} %shard_map.172.grad_any, f8e4m3fn[8192,768]{1,0:T(32,128)(4,1)} %shard_map.169.gate_any.off_any, ...), custom_call_target="tpu_custom_call" | custom-call | flops 1610612736 | bytes 12582912 | tf_op jit(solution)/shard_map/pallas_call | solution.py:384
  135.4 1.0 constant_dynamic-slice_fusion.1
  136.5 1.4 collective-permute-done.13
  137.9 1.0 convert_add_fusion.1
  139.0 0.6 collective-permute-start.14
  139.6 6.5 %shard_map.174.refs_0_ = f32[2,3,4,8192]{3,2,1,0:T(4,128)} custom-call(bf16[32,768]{1,0:T(8,128)(2,1)} %get-tuple-element.122.x_any, f8e4m3fn[768,8192]{1,0:T(32,128)(4,1)} %shard_map.171.down_any.off_any, bf16[32,8192]{1,0:T(8,128)(2,1)} %get-tuple-element.123.cot_any.grad_any), custom_call_target="tpu_custom_call" | custom-call | flops 1610612736 | bytes 6291456 | tf_op jit(solution)/shard_map/pallas_call | solution.py:519
  146.2 1.6 collective-permute-start.15
  147.8 6.5 %shard_map.175.refs_0_ = f32[2,128,768]{2,1,0:T(8,128)} custom-call(bf16[32,8192]{1,0:T(8,128)(2,1)} %pad_maximum_fusion.2.x_any, f8e4m3fn[8192,768]{1,0:T(32,128)(4,1)} %shard_map.169.gate_any.off_any, bf16[32,768]{1,0:T(8,128)(2,1)} %get-tuple-element.128.grad_any), custom_call_target="tpu_custom_call" | custom-call | flops 1610612736 | bytes 6291456 | tf_op jit(solution)/shard_map/pallas_call | solution.py:519
  154.4 1.6 collective-permute-start.16
  156.0 6.5 %shard_map.176.refs_0_ = f32[2,128,768]{2,1,0:T(8,128)} custom-call(bf16[32,8192]{1,0:T(8,128)(2,1)} %pad_maximum_fusion.2.x_any, f8e4m3fn[8192,768]{1,0:T(32,128)(4,1)} %shard_map.170.up_any.off_any, bf16[32,768]{1,0:T(8,128)(2,1)} %get-tuple-element.133.grad_any), custom_call_target="tpu_custom_call" | custom-call | flops 1610612736 | bytes 6291456 | tf_op jit(solution)/shard_map/pallas_call | solution.py:519
  162.6 2.7 %collective-permute-start.17 = (bf16[4,8192]{1,0:T(4,128)(2,1)S(1)}, bf16[4,8192]{1,0:T(4,128)(2,1)S(1)}, u32[]{:S(2)}, u32[]{:S(2)}) collective-permute-start(bf16[4,8192]{1,0:T(4,128)(2,1)S(1)} %add_convert_fusion), channel_id=1, source_target_pairs={{0,16},{1,17},{2,18},{3,19},{4,20},{5,21},{6,22},{7,23},{8,24},{9,... | collective-permute-start | bytes 196616 | tf_op jit(solution)/shard_map/ppermute | solution.py:555
  165.3 3.2 %collective-permute-done.17 = bf16[4,8192]{1,0:T(4,128)(2,1)S(1)} collective-permute-done((bf16[4,8192]{1,0:T(4,128)(2,1)S(1)}, bf16[4,8192]{1,0:T(4,128)(2,1)S(1)}, u32[]{:S(2)}, u32[]{:S(2)}) %collective-permute-start.17) | collective-permute-done | bytes 65568 | tf_op jit(solution)/shard_map/ppermute | solution.py:555
  169.4 3.8 %collective-permute-done.18 = bf16[4,8192]{1,0:T(4,128)(2,1)S(1)} collective-permute-done((bf16[4,8192]{1,0:T(4,128)(2,1)S(1)}, bf16[4,8192]{1,0:T(4,128)(2,1)S(1)}, u32[]{:S(2)}, u32[]{:S(2)}) %collective-permute-start.18) | collective-permute-done | bytes 65568 | tf_op jit(solution)/shard_map/ppermute | solution.py:555
  173.4 1.6 collective-permute-start.19
  174.9 3.5 %collective-permute-done.19 = bf16[8,8192]{1,0:T(8,128)(2,1)S(1)} collective-permute-done((bf16[8,8192]{1,0:T(8,128)(2,1)S(1)}, bf16[8,8192]{1,0:T(8,128)(2,1)S(1)}, u32[]{:S(2)}, u32[]{:S(2)}) %collective-permute-start.19) | collective-permute-done | bytes 131104 | tf_op jit(solution)/shard_map/ppermute | solution.py:555
  178.6 1.5 collective-permute-done.20
  180.2 0.8 pad_maximum_fusion.3.cot_any.grad_any
  181.1 16.9 %shard_map.177 = (bf16[32,768]{1,0:T(8,128)(2,1)}, bf16[32,768]{1,0:T(8,128)(2,1)}, bf16[32,8192]{1,0:T(8,128)(2,1)}) custom-call(bf16[32,8192]{1,0:T(8,128)(2,1)} %pad_maximum_fusion.3.cot_any.grad_any, f32[32,768]{1,0:T(8,128)} %get-tuple-element.135.pre_any, f32[32,768]{1,0:T(8,128)} %get-tuple-element.136.value_any, ...), custom_call_target="tpu_custom_call" | custom-call | flops 1207959552 | bytes 18874368 | tf_op jit(solution)/shard_map/pallas_call | solution.py:437
  197.9 1.0 constant_dynamic-slice_fusion
  199.1 1.4 collective-permute-done.21
  200.5 1.0 convert_add_fusion
  201.5 1.6 collective-permute-start.22
  203.1 6.5 %shard_map.178 = f32[2,3,4,8192]{3,2,1,0:T(4,128)} custom-call(bf16[32,768]{1,0:T(8,128)(2,1)} %get-tuple-element.141.x_any, f8e4m3fn[768,8192]{1,0:T(32,128)(4,1)} %shard_map.167.down_any.off_any, bf16[32,8192]{1,0:T(8,128)(2,1)} %pad_maximum_fusion.3.cot_any.grad_any, f32[2,3,4,8192]{3,2,1,0:T(4,128)} %shard_map.174.refs_0_), custom_call_target="tpu_custom_call", output_to_operand_aliasing={{}: (3, {})} | custom-call | flops 1610612736 | bytes 6291456 | tf_op jit(solution)/shard_map/pallas_call | solution.py:519
  210.3 6.5 %shard_map.179 = f32[2,128,768]{2,1,0:T(8,128)} custom-call(bf16[32,8192]{1,0:T(8,128)(2,1)} %get-tuple-element.155.x_any, f8e4m3fn[8192,768]{1,0:T(32,128)(4,1)} %shard_map.165.gate_any.off_any, bf16[32,768]{1,0:T(8,128)(2,1)} %get-tuple-element.149.grad_any, f32[2,128,768]{2,1,0:T(8,128)} %shard_map.175.refs_0_), custom_call_target="tpu_custom_call", output_to_operand_aliasing={{}: (3, {})} | custom-call | flops 1610612736 | bytes 6291456 | tf_op jit(solution)/shard_map/pallas_call | solution.py:519
  217.0 6.6 %shard_map.180 = f32[2,128,768]{2,1,0:T(8,128)} custom-call(bf16[32,8192]{1,0:T(8,128)(2,1)} %get-tuple-element.155.x_any, f8e4m3fn[8192,768]{1,0:T(32,128)(4,1)} %shard_map.166.up_any.off_any, bf16[32,768]{1,0:T(8,128)(2,1)} %get-tuple-element.156.grad_any, f32[2,128,768]{2,1,0:T(8,128)} %shard_map.176.refs_0_), custom_call_target="tpu_custom_call", output_to_operand_aliasing={{}: (3, {})} | custom-call | flops 1610612736 | bytes 6291456 | tf_op jit(solution)/shard_map/pallas_call | solution.py:519
  223.7 2.5 %collective-permute-start.25 = (bf16[1,8192]{1,0:T(2,128)(2,1)S(1)}, bf16[1,8192]{1,0:T(2,128)(2,1)S(1)}, u32[]{:S(2)}, u32[]{:S(2)}) collective-permute-start(bf16[1,8192]{1,0:T(2,128)(2,1)S(1)} %dynamic-slice_convert_fusion.7), channel_id=1, source_target_pairs={{0,16},{1,17},{2,18},{3,19},{4,20},{5,21},{6,22},{7,23},{8,24},{9,... | collective-permute-start | bytes 49160 | tf_op jit(solution)/shard_map/ppermute | solution.py:555
  226.2 0.7 multiply_reduce_fusion.1
  227.6 1.5 copy.39
  229.1 0.7 multiply_reduce_fusion
  230.4 0.7 add_convert_fusion.4
  (90 shorter events, 8.3 us)
Async XLA Ops:
  1.5 15.5 %collective-permute-start = (bf16[2,1,8192]{2,1,0:T(2,128)(2,1)S(1)}, bf16[2,1,8192]{2,1,0:T(2,128)(2,1)S(1)}, u32[]{:S(2)}, u32[]{:S(2)}) collective-permute-start(bf16[2,1,8192]{2,1,0:T(2,128)(2,1)S(1)} %pad_maximum_fusion.11), channel_id=1, source_target_pairs={{0,16},{1,17},{2,18},{3,19},{4,20},{5,21},{6,22},{7,23},{8,24},{9,... | collective-permute-start | bytes 98312 | tf_op jit(solution)/shard_map/ppermute | solution.py:557
  9.1 7.9 %copy-start.3 = (bf16[1,8192]{1,0:T(2,128)(2,1)S(1)}, bf16[1,8192]{1,0:T(2,128)(2,1)}, u32[]{:S(2)}) copy-start(bf16[1,8192]{1,0:T(2,128)(2,1)} %param.14) | copy-start | bytes 49156
  9.1 7.9 %copy-start.5 = (bf16[1,8192]{1,0:T(2,128)(2,1)S(1)}, bf16[1,8192]{1,0:T(2,128)(2,1)}, u32[]{:S(2)}) copy-start(bf16[1,8192]{1,0:T(2,128)(2,1)} %param.25) | copy-start | bytes 49156
  17.4 9.6 %collective-permute-start.1 = (bf16[2,2,8192]{2,1,0:T(2,128)(2,1)S(1)}, bf16[2,2,8192]{2,1,0:T(2,128)(2,1)S(1)}, u32[]{:S(2)}, u32[]{:S(2)}) collective-permute-start(bf16[2,2,8192]{2,1,0:T(2,128)(2,1)S(1)} %pad_maximum_fusion.12), channel_id=1, source_target_pairs={{0,8},{1,9},{2,10},{3,11},{4,12},{5,13},{6,14},{7,15},{8,0},{9,1},... | collective-permute-start | bytes 196616 | tf_op jit(solution)/shard_map/ppermute | solution.py:557
  19.1 10.2 %copy-start.1 = (s32[2,12,8192]{2,0,1:T(2,128)S(1)}, s32[2,12,8192]{2,0,1:T(2,128)}, u32[]{:S(2)}) copy-start(s32[2,12,8192]{2,0,1:T(2,128)} %param.21) | copy-start | bytes 2359300
  27.7 11.2 %collective-permute-start.2 = (bf16[2,4,8192]{2,1,0:T(4,128)(2,1)S(1)}, bf16[2,4,8192]{2,1,0:T(4,128)(2,1)S(1)}, u32[]{:S(2)}, u32[]{:S(2)}) collective-permute-start(bf16[2,4,8192]{2,1,0:T(4,128)(2,1)S(1)} %pad_maximum_fusion.7), channel_id=1, source_target_pairs={{0,4},{1,5},{2,6},{3,7},{4,0},{5,1},{6,2},{7,3},{8,12},{9,13},{10,... | collective-permute-start | bytes 393224 | tf_op jit(solution)/shard_map/ppermute | solution.py:557
  30.7 16.9 %copy-start.2 = (f32[2,12,8192]{2,0,1:T(2,128)S(1)}, f32[2,12,8192]{2,0,1:T(2,128)}, u32[]{:S(2)}) copy-start(f32[2,12,8192]{2,0,1:T(2,128)} %param.24) | copy-start | bytes 2359300
  39.2 7.3 %collective-permute-start.3 = (bf16[2,8,8192]{2,1,0:T(8,128)(2,1)S(1)}, bf16[2,8,8192]{2,1,0:T(8,128)(2,1)S(1)}, u32[]{:S(2)}, u32[]{:S(2)}) collective-permute-start(bf16[2,8,8192]{2,1,0:T(8,128)(2,1)S(1)} %pad_maximum_fusion.4), channel_id=1, source_target_pairs={{0,2},{1,3},{2,0},{3,1},{4,6},{5,7},{6,4},{7,5},{8,10},{9,11},{10,... | collective-permute-start | bytes 786440 | tf_op jit(solution)/shard_map/ppermute | solution.py:555
  47.5 2.1 collective-permute-start.4
  66.2 1.6 collective-permute-start.5
  68.8 9.4 %collective-permute-start.6 = (bf16[8,8192]{1,0:T(8,128)(2,1)S(1)}, bf16[8,8192]{1,0:T(8,128)(2,1)S(1)}, u32[]{:S(2)}, u32[]{:S(2)}) collective-permute-start(bf16[8,8192]{1,0:T(8,128)(2,1)S(1)} %dynamic-slice_convert_fusion.2), channel_id=1, source_target_pairs={{0,2},{1,3},{2,0},{3,1},{4,6},{5,7},{6,4},{7,5},{8,10},{9,11},{10,... | collective-permute-start | bytes 393224 | tf_op jit(solution)/shard_map/ppermute | solution.py:557
  78.3 8.5 %collective-permute-start.7 = (bf16[4,8192]{1,0:T(4,128)(2,1)S(1)}, bf16[4,8192]{1,0:T(4,128)(2,1)S(1)}, u32[]{:S(2)}, u32[]{:S(2)}) collective-permute-start(bf16[4,8192]{1,0:T(4,128)(2,1)S(1)} %dynamic-slice_convert_fusion.5), channel_id=1, source_target_pairs={{0,4},{1,5},{2,6},{3,7},{4,0},{5,1},{6,2},{7,3},{8,12},{9,13},{10,... | collective-permute-start | bytes 196616 | tf_op jit(solution)/shard_map/ppermute | solution.py:557
  87.0 10.0 %collective-permute-start.8 = (bf16[4,8192]{1,0:T(4,128)(2,1)S(1)}, bf16[4,8192]{1,0:T(4,128)(2,1)S(1)}, u32[]{:S(2)}, u32[]{:S(2)}) collective-permute-start(bf16[4,8192]{1,0:T(4,128)(2,1)S(1)} %add_convert_fusion.3), channel_id=1, source_target_pairs={{0,8},{1,9},{2,10},{3,11},{4,12},{5,13},{6,14},{7,15},{8,0},{9,1},... | collective-permute-start | bytes 196616 | tf_op jit(solution)/shard_map/ppermute | solution.py:557
  97.0 8.7 %collective-permute-start.9 = (bf16[4,8192]{1,0:T(4,128)(2,1)S(1)}, bf16[4,8192]{1,0:T(4,128)(2,1)S(1)}, u32[]{:S(2)}, u32[]{:S(2)}) collective-permute-start(bf16[4,8192]{1,0:T(4,128)(2,1)S(1)} %add_convert_fusion.2), channel_id=1, source_target_pairs={{0,16},{1,17},{2,18},{3,19},{4,20},{5,21},{6,22},{7,23},{8,24},{9,... | collective-permute-start | bytes 196616 | tf_op jit(solution)/shard_map/ppermute | solution.py:557
  106.0 4.3 %collective-permute-start.10 = (bf16[4,8192]{1,0:T(4,128)(2,1)S(1)}, bf16[4,8192]{1,0:T(4,128)(2,1)S(1)}, u32[]{:S(2)}, u32[]{:S(2)}) collective-permute-start(bf16[4,8192]{1,0:T(4,128)(2,1)S(1)} %fusion.8), channel_id=1, source_target_pairs={{0,4},{1,5},{2,6},{3,7},{4,0},{5,1},{6,2},{7,3},{8,12},{9,13},{10,... | collective-permute-start | bytes 196616 | tf_op jit(solution)/shard_map/ppermute | solution.py:555
  110.6 5.0 %collective-permute-start.11 = (bf16[8,8192]{1,0:T(8,128)(2,1)S(1)}, bf16[8,8192]{1,0:T(8,128)(2,1)S(1)}, u32[]{:S(2)}, u32[]{:S(2)}) collective-permute-start(bf16[8,8192]{1,0:T(8,128)(2,1)S(1)} %pad_maximum_fusion.8), channel_id=1, source_target_pairs={{0,2},{1,3},{2,0},{3,1},{4,6},{5,7},{6,4},{7,5},{8,10},{9,11},{10,... | collective-permute-start | bytes 393224 | tf_op jit(solution)/shard_map/ppermute | solution.py:555
  115.7 1.6 collective-permute-start.12
  136.3 1.6 collective-permute-start.13
  139.0 7.2 %collective-permute-start.14 = (bf16[8,8192]{1,0:T(8,128)(2,1)S(1)}, bf16[8,8192]{1,0:T(8,128)(2,1)S(1)}, u32[]{:S(2)}, u32[]{:S(2)}) collective-permute-start(bf16[8,8192]{1,0:T(8,128)(2,1)S(1)} %dynamic-slice_convert_fusion.1), channel_id=1, source_target_pairs={{0,2},{1,3},{2,0},{3,1},{4,6},{5,7},{6,4},{7,5},{8,10},{9,11},{10,... | collective-permute-start | bytes 393224 | tf_op jit(solution)/shard_map/ppermute | solution.py:557
  146.2 8.1 %collective-permute-start.15 = (bf16[4,8192]{1,0:T(4,128)(2,1)S(1)}, bf16[4,8192]{1,0:T(4,128)(2,1)S(1)}, u32[]{:S(2)}, u32[]{:S(2)}) collective-permute-start(bf16[4,8192]{1,0:T(4,128)(2,1)S(1)} %dynamic-slice_convert_fusion.4), channel_id=1, source_target_pairs={{0,4},{1,5},{2,6},{3,7},{4,0},{5,1},{6,2},{7,3},{8,12},{9,13},{10,... | collective-permute-start | bytes 196616 | tf_op jit(solution)/shard_map/ppermute | solution.py:557
  154.4 8.2 %collective-permute-start.16 = (bf16[4,8192]{1,0:T(4,128)(2,1)S(1)}, bf16[4,8192]{1,0:T(4,128)(2,1)S(1)}, u32[]{:S(2)}, u32[]{:S(2)}) collective-permute-start(bf16[4,8192]{1,0:T(4,128)(2,1)S(1)} %add_convert_fusion.1), channel_id=1, source_target_pairs={{0,8},{1,9},{2,10},{3,11},{4,12},{5,13},{6,14},{7,15},{8,0},{9,1},... | collective-permute-start | bytes 196616 | tf_op jit(solution)/shard_map/ppermute | solution.py:557
  162.6 5.8 %collective-permute-start.17 = (bf16[4,8192]{1,0:T(4,128)(2,1)S(1)}, bf16[4,8192]{1,0:T(4,128)(2,1)S(1)}, u32[]{:S(2)}, u32[]{:S(2)}) collective-permute-start(bf16[4,8192]{1,0:T(4,128)(2,1)S(1)} %add_convert_fusion), channel_id=1, source_target_pairs={{0,16},{1,17},{2,18},{3,19},{4,20},{5,21},{6,22},{7,23},{8,24},{9,... | collective-permute-start | bytes 196616 | tf_op jit(solution)/shard_map/ppermute | solution.py:555
  168.9 4.3 %collective-permute-start.18 = (bf16[4,8192]{1,0:T(4,128)(2,1)S(1)}, bf16[4,8192]{1,0:T(4,128)(2,1)S(1)}, u32[]{:S(2)}, u32[]{:S(2)}) collective-permute-start(bf16[4,8192]{1,0:T(4,128)(2,1)S(1)} %fusion.13), channel_id=1, source_target_pairs={{0,4},{1,5},{2,6},{3,7},{4,0},{5,1},{6,2},{7,3},{8,12},{9,13},{10,... | collective-permute-start | bytes 196616 | tf_op jit(solution)/shard_map/ppermute | solution.py:555
  173.4 5.0 %collective-permute-start.19 = (bf16[8,8192]{1,0:T(8,128)(2,1)S(1)}, bf16[8,8192]{1,0:T(8,128)(2,1)S(1)}, u32[]{:S(2)}, u32[]{:S(2)}) collective-permute-start(bf16[8,8192]{1,0:T(8,128)(2,1)S(1)} %pad_maximum_fusion.9), channel_id=1, source_target_pairs={{0,2},{1,3},{2,0},{3,1},{4,6},{5,7},{6,4},{7,5},{8,10},{9,11},{10,... | collective-permute-start | bytes 393224 | tf_op jit(solution)/shard_map/ppermute | solution.py:555
  178.5 1.6 collective-permute-start.20
  198.9 1.6 collective-permute-start.21
  201.5 8.1 %collective-permute-start.22 = (bf16[8,8192]{1,0:T(8,128)(2,1)S(1)}, bf16[8,8192]{1,0:T(8,128)(2,1)S(1)}, u32[]{:S(2)}, u32[]{:S(2)}) collective-permute-start(bf16[8,8192]{1,0:T(8,128)(2,1)S(1)} %dynamic-slice_convert_fusion), channel_id=1, source_target_pairs={{0,2},{1,3},{2,0},{3,1},{4,6},{5,7},{6,4},{7,5},{8,10},{9,11},{10,... | collective-permute-start | bytes 393224 | tf_op jit(solution)/shard_map/ppermute | solution.py:557
  209.7 7.1 %collective-permute-start.23 = (bf16[4,8192]{1,0:T(4,128)(2,1)S(1)}, bf16[4,8192]{1,0:T(4,128)(2,1)S(1)}, u32[]{:S(2)}, u32[]{:S(2)}) collective-permute-start(bf16[4,8192]{1,0:T(4,128)(2,1)S(1)} %dynamic-slice_convert_fusion.3), channel_id=1, source_target_pairs={{0,4},{1,5},{2,6},{3,7},{4,0},{5,1},{6,2},{7,3},{8,12},{9,13},{10,... | collective-permute-start | bytes 196616 | tf_op jit(solution)/shard_map/ppermute | solution.py:557
  216.8 10.8 %copy-start = (f32[2,3,4,8192]{3,2,1,0:T(4,128)S(1)}, f32[2,3,4,8192]{3,2,1,0:T(4,128)}, u32[]{:S(2)}) copy-start(f32[2,3,4,8192]{3,2,1,0:T(4,128)} %shard_map.178) | copy-start | bytes 2359300
  216.8 12.2 %copy-start.4 = (f32[2,8192]{1,0:T(2,128)S(1)}, f32[2,8192]{1,0:T(2,128)}, u32[]{:S(2)}) copy-start(f32[2,8192]{1,0:T(2,128)} %param.15) | copy-start | bytes 196612
  216.9 6.6 %collective-permute-start.24 = (bf16[2,8192]{1,0:T(2,128)(2,1)S(1)}, bf16[2,8192]{1,0:T(2,128)(2,1)S(1)}, u32[]{:S(2)}, u32[]{:S(2)}) collective-permute-start(bf16[2,8192]{1,0:T(2,128)(2,1)S(1)} %dynamic-slice_convert_fusion.6), channel_id=1, source_target_pairs={{0,8},{1,9},{2,10},{3,11},{4,12},{5,13},{6,14},{7,15},{8,0},{9,1},... | collective-permute-start | bytes 98312 | tf_op jit(solution)/shard_map/ppermute | solution.py:557
  223.7 5.4 %collective-permute-start.25 = (bf16[1,8192]{1,0:T(2,128)(2,1)S(1)}, bf16[1,8192]{1,0:T(2,128)(2,1)S(1)}, u32[]{:S(2)}, u32[]{:S(2)}) collective-permute-start(bf16[1,8192]{1,0:T(2,128)(2,1)S(1)} %dynamic-slice_convert_fusion.7), channel_id=1, source_target_pairs={{0,16},{1,17},{2,18},{3,19},{4,20},{5,21},{6,22},{7,23},{8,24},{9,... | collective-permute-start | bytes 49160 | tf_op jit(solution)/shard_map/ppermute | solution.py:555

commit v3 on v1

v3 whole, which is shorter than its diff:
```python
import functools

import jax
import jax.numpy as jnp
import numpy as np
from jax import lax
from jax.experimental import pallas as pl
from jax.experimental.pallas import tpu as pltpu
from jax.sharding import PartitionSpec as P

GROUP = 64
WORDS = GROUP // 4
LAYERS = 2
norm_epsilon = 1e-05
BF16 = jnp.bfloat16
F32 = jnp.float32
OFFSET = jnp.float8_e4m3fn
ANYWHERE = pl.BlockSpec(memory_space=pl.ANY)
IN_HBM = pl.BlockSpec(memory_space=pltpu.HBM)
SCALAR = pl.BlockSpec(memory_space=pltpu.SMEM)


def params(mib=60):
    return pltpu.CompilerParams(vmem_limit_bytes=mib * 2**20)


def cost(flops, bytes_accessed):
    return pl.CostEstimate(flops=int(flops), bytes_accessed=int(bytes_accessed), transcendentals=0)


def block_of(size, most):
    best = size
    if size > most:
        for candidate in range(128, most + 1, 128):
            if size % candidate == 0:
                best = candidate
    return best


def copy_in(source, target, sem):
    copy = pltpu.make_async_copy(source, target, sem)
    copy.start()
    return copy


def row_chunk(chunk, size):
    return pl.ds(pl.multiple_of(chunk * size, size), size)


def unpack(held, zeros, planes, slot):
    for piece in range(4):
        offset = ((held >> (2 * piece)) & 3) - zeros
        planes[slot, pl.ds(piece, WORDS, stride=4), :] = offset.astype(F32)


COUNT = 4
AHEAD = 2


def stream(count, copies, work, before=None, last=None, ahead=AHEAD):
    for chunk in range(min(ahead, count)):
        for copy in copies(chunk):
            copy.start()
    if before is not None:
        before()

    def step(chunk, _):
        for copy in copies(chunk):
            copy.wait()

        @pl.when(chunk + ahead < count)
        def _():
            for copy in copies(chunk + ahead):
                copy.start()

        if last is not None:
            @pl.when(chunk + ahead >= count)
            def _():
                last(chunk + ahead - count)

        work(chunk)
        return 0

    lax.fori_loop(0, count, step, 0)


def offsets_kernel(layer, half, *refs):
    code_any, zero_any = refs[:2]
    out_any, code, zero, out, planes, sems = refs[-6:]
    words, width = code.shape
    count = COUNT
    rows = words // count
    groups = rows // WORDS
    tile = planes.shape[-1]

    def code_copy(chunk):
        return pltpu.make_async_copy(
            code_any.at[layer, row_chunk(half * count + chunk, rows)],
            code.at[row_chunk(chunk, rows)],
            sems.at[chunk],
        )

    def out_copy(chunk):
        return pltpu.make_async_copy(
            out.at[row_chunk(chunk, rows * 4)],
            out_any.at[row_chunk(half * count + chunk, rows * 4)],
            sems.at[count + chunk],
        )

    own_groups = row_chunk(half, zero.shape[0])
    zero_copy = pltpu.make_async_copy(zero_any.at[layer, own_groups], zero, sems.at[2 * count])
    zero_copy.start()

    def work(chunk):
        def some_groups(block, _):
            first = chunk * groups + block * 8
            for index in range(width // tile):
                cols = slice(index * tile, (index + 1) * tile)
                zeros = zero[row_chunk(first // 8, 8), cols]
                for group in range(8):
                    held = code[row_chunk(first + group, WORDS), cols]
                    unpack(held, zeros[group : group + 1], planes, group)
                for group in range(8):
                    out[row_chunk(first + group, GROUP), cols] = planes[group].astype(OFFSET)
            return 0

        lax.fori_loop(0, groups // 8, some_groups, 0)
        out_copy(chunk).start()

    stream(count, lambda chunk: [code_copy(chunk)], work, zero_copy.wait)
    for chunk in range(count):
        out_copy(chunk).wait()


def offsets_of(codes, zeros, layer, earlier=None):
    _, words, width = codes.shape
    tile = 128 if width % 128 == 0 else 64
    operands = [codes, zeros] if earlier is None else [codes, zeros, earlier]
    return pl.pallas_call(
        functools.partial(offsets_kernel, layer, 0 if earlier is None else 1),
        in_specs=[IN_HBM] * len(operands),
        out_specs=IN_HBM,
        out_shape=jax.ShapeDtypeStruct((words * 4, width), OFFSET),
        scratch_shapes=[
            pltpu.VMEM((words // 2, width), jnp.int32),
            pltpu.VMEM((zeros.shape[1] // 2, width), jnp.int32),
            pltpu.VMEM((words * 2, width), OFFSET),
            pltpu.VMEM((8, GROUP, tile), F32),
            pltpu.SemaphoreType.DMA((2 * COUNT + 1,)),
        ],
        input_output_aliases={} if earlier is None else {2: 0},
        compiler_params=params(),
        cost_estimate=cost(words * width * 20, words * width * 4),
    )(*operands)


class DownCodes:
    def __init__(self, layer, code_any, zero_any, out_any, code, zero, out, planes, sems, half=0):
        self.half = half
        self.layer, self.code_any, self.zero_any, self.out_any = layer, code_any, zero_any, out_any
        self.code, self.zero, self.out, self.planes, self.sems = code, zero, out, planes, sems
        self.groups = code.shape[0] // WORDS
        self.lanes = code.shape[1] // COUNT
        self.tile = planes.shape[-1]
        self.tiles = self.lanes // self.tile

    def part(self, chunk):
        return (slice(None), row_chunk(chunk, self.lanes))

    def far_part(self, chunk):
        return self.part(self.half * COUNT + chunk)

    def zero_copy(self):
        own = row_chunk(self.half, self.zero.shape[-1])
        return pltpu.make_async_copy(
            self.zero_any.at[:, :, own], self.zero, self.sems.at[2 * COUNT]
        )

    def copy(self, chunk):
        return pltpu.make_async_copy(
            self.code_any.at[(self.layer,) + self.far_part(chunk)],
            self.code.at[self.part(chunk)],
            self.sems.at[chunk],
        )

    def out_copy(self, chunk):
        return pltpu.make_async_copy(
            self.out.at[self.part(chunk)],
            self.out_any.at[self.far_part(chunk)],
            self.sems.at[COUNT + chunk],
        )

    def tile_of(self, chunk, index):
        cols = pl.ds(pl.multiple_of(chunk * self.lanes + index * self.tile, self.tile), self.tile)
        for group in range(self.groups):
            held = self.code[group * WORDS : (group + 1) * WORDS, cols]
            zeros = self.zero[group, self.layer : self.layer + 1, cols]
            unpack(held, zeros, self.planes, group)
            self.out[group * GROUP : (group + 1) * GROUP, cols] = self.planes[group].astype(OFFSET)

    @staticmethod
    def scratch(codes, zeros, halves=1):
        _, words, width = codes.shape
        width = width // halves
        return [
            pltpu.VMEM((words, width), jnp.int32),
            pltpu.VMEM(zeros.shape[:2] + (width,), jnp.int32),
            pltpu.VMEM((words * 4, width), OFFSET),
            pltpu.VMEM((words // WORDS, GROUP, 128), F32),
            pltpu.SemaphoreType.DMA((2 * COUNT + 1,)),
        ]


def down_offsets_kernel(layer, half, *refs):
    code_any, zero_any = refs[:2]
    out_any, code, zero, out, planes, sems = refs[-6:]
    codes = DownCodes(layer, code_any, zero_any, out_any, code, zero, out, planes, sems, half)
    codes.zero_copy().start()

    def work(chunk):
        def tile(index, _):
            codes.tile_of(chunk, index)
            return 0

        lax.fori_loop(0, codes.tiles, tile, 0)
        codes.out_copy(chunk).start()

    stream(COUNT, lambda chunk: [codes.copy(chunk)], work, codes.zero_copy().wait)
    for chunk in range(COUNT):
        codes.out_copy(chunk).wait()


def down_offsets_of(codes, zeros, layer, earlier=None):
    _, words, width = codes.shape
    operands = [codes, zeros] if earlier is None else [codes, zeros, earlier]
    return pl.pallas_call(
        functools.partial(down_offsets_kernel, layer, 0 if earlier is None else 1),
        in_specs=[IN_HBM] * len(operands),
        out_specs=IN_HBM,
        out_shape=jax.ShapeDtypeStruct((words * 4, width), OFFSET),
        scratch_shapes=DownCodes.scratch(codes, zeros, 2),
        input_output_aliases={} if earlier is None else {2: 0},
        compiler_params=params(),
        cost_estimate=cost(words * width * 20, words * width * 4),
    )(*operands)


def sigmoid(value):
    return 1.0 / (1.0 + jnp.exp(-value))


def across(left, right):
    return lax.dot_general(left, right, (((1,), (1,)), ((), ())), preferred_element_type=F32)


def weights_of(offsets, steps):
    parts = []
    for group, step in enumerate(steps):
        part = offsets[group * GROUP : (group + 1) * GROUP].astype(F32)
        parts.append((part * step).astype(BF16))
    return jnp.concatenate(parts, axis=0)


def row_scale(value, step_most):
    top = jnp.max(jnp.abs(value), axis=1, keepdims=True) * step_most
    top = jnp.maximum(top, 1e-30)
    return 224.0 / top, top / 224.0


def across_offsets(scaled, offsets, steps):
    tokens = scaled.shape[0]
    found = []
    for first in range(0, len(steps), 4):
        count = min(4, len(steps) - first)
        high, low = [], []
        for step in steps[first : first + count]:
            part = scaled * step
            top = part.astype(OFFSET)
            high.append(top)
            low.append(((part - top.astype(F32)) * 16.0).astype(OFFSET))
        both = across(
            jnp.concatenate(high + low, axis=0),
            offsets[first * GROUP : (first + count) * GROUP, :],
        )
        rows = count * tokens
        both = both[:rows] + both[rows:] * (1.0 / 16.0)
        own = both[:tokens]
        lane_group = lax.broadcasted_iota(jnp.int32, own.shape, 1) // GROUP
        for group in range(1, count):
            own = jnp.where(lane_group == group, both[group * tokens : (group + 1) * tokens], own)
        found.append(own)
    return jnp.concatenate(found, axis=1)


class Matrix:
    def __init__(self, layer, source, step_source, offsets, steps, sems, by_rows):
        self.layer, self.source, self.step_source = layer, source, step_source
        self.offsets, self.steps, self.sems, self.by_rows = offsets, steps, sems, by_rows
        self.count = COUNT
        self.size = offsets.shape[0 if by_rows else 1] // self.count

    def part(self, chunk):
        if self.by_rows:
            return (row_chunk(chunk, self.size), slice(None))
        return (slice(None), row_chunk(chunk, self.size))

    def step_copy(self):
        source = self.step_source.at[self.layer] if self.by_rows else self.step_source
        return pltpu.make_async_copy(source, self.steps, self.sems.at[self.count])

    def copy(self, chunk):
        part = self.part(chunk)
        return pltpu.make_async_copy(self.source.at[part], self.offsets.at[part], self.sems.at[chunk])

    def weights(self, chunk):
        offsets = self.offsets[self.part(chunk)]
        groups = offsets.shape[0] // GROUP
        if self.by_rows:
            held = self.steps[row_chunk(chunk, groups), :]
            steps = [held[group : group + 1] for group in range(groups)]
        else:
            steps = self.step_rows(row_chunk(chunk, self.size))
        return weights_of(offsets, steps)

    def across(self, scaled, chunk):
        groups = self.size // GROUP
        held = self.steps[row_chunk(chunk, groups), :]
        steps = [held[group : group + 1] for group in range(groups)]
        return across_offsets(scaled, self.offsets[self.part(chunk)], steps)

    def step_rows(self, cols):
        layer = slice(self.layer, self.layer + 1)
        return [self.steps[group, layer, cols] for group in range(self.steps.shape[0])]

    def some_weights(self, chunk, piece, pieces):
        size = self.size // pieces
        if not self.by_rows:
            first = pl.multiple_of(chunk * self.size + piece * size, size)
            return weights_of(self.offsets[:, pl.ds(first, size)], self.step_rows(pl.ds(first, size)))
        groups = self.size // GROUP
        held = self.steps[row_chunk(chunk, groups), :]
        first = pl.multiple_of(chunk * self.size + piece * size, size)
        count = groups // pieces
        rows = range(piece * count, (piece + 1) * count)
        return weights_of(self.offsets[pl.ds(first, size), :], [held[row : row + 1] for row in rows])

    @staticmethod
    def scratch(offsets, steps):
        by_rows = offsets.shape[0] >= offsets.shape[1]
        return [
            pltpu.VMEM(offsets.shape, OFFSET),
            pltpu.VMEM(steps.shape[1:] if by_rows else steps.shape, F32),
            pltpu.SemaphoreType.DMA((COUNT + 1,)),
        ]


def gate_up_forward(x, gate, up, gate_out, up_out, before, beside=None, codes=None, after=None):
    pieces = 4

    def work(chunk):
        size = gate.size // pieces
        for piece in range(pieces):
            first = pl.multiple_of(chunk * gate.size + piece * size, size)
            rows = x[:, pl.ds(first, size)]
            for turn, (matrix, out) in enumerate(((gate, gate_out), (up, up_out))):
                weights = matrix.some_weights(chunk, piece, pieces)
                out[...] += jnp.dot(rows, weights, preferred_element_type=F32)
                if beside is not None:
                    beside(chunk, 2 * piece + turn, 2 * pieces)

    def ready():
        gate_out[...] = jnp.zeros_like(gate_out)
        up_out[...] = jnp.zeros_like(up_out)
        before()
        gate.step_copy().wait()
        up.step_copy().wait()

    gate.step_copy().start()
    up.step_copy().start()
    def copies(chunk):
        both = [gate.copy(chunk), up.copy(chunk)]
        return both if codes is None else both + [codes.copy(chunk)]

    def last(chunk):
        after.copy(chunk).start()

    stream(gate.count, copies, work, ready, None if after is None else last)
    gate_all = gate_out[...]
    return (gate_all * sigmoid(gate_all) * up_out[...]).astype(BF16)


def hidden_back(hidden_grad, gate_pre, up_value):
    gate_sigmoid = sigmoid(gate_pre)
    gate_grad = (
        hidden_grad * up_value * gate_sigmoid * (1.0 + gate_pre * (1.0 - gate_sigmoid))
    ).astype(BF16)
    up_grad = (hidden_grad * gate_pre * gate_sigmoid).astype(BF16)
    return gate_grad, up_grad


def gate_up_backward(gate_grad, up_grad, gate, up, scaled_gate, scaled_up):
    gate_value, up_value = gate_grad.astype(F32), up_grad.astype(F32)
    gate_factor, gate_back = row_scale(gate_value, jnp.max(gate.steps[...]))
    up_factor, up_back = row_scale(up_value, jnp.max(up.steps[...]))
    scaled_gate[...] = gate_value * gate_factor
    scaled_up[...] = up_value * up_factor

    def product(chunk):
        return (
            gate.across(scaled_gate[...], chunk) * gate_back
            + up.across(scaled_up[...], chunk) * up_back
        )

    return product


def cot_down(cot, down, out, pieces=4):
    most = jnp.max(down.steps[...])
    factor, back = row_scale(cot[...].astype(F32), most)
    size = down.size // pieces

    def work(chunk):
        for piece in range(pieces):
            cols = pl.ds(pl.multiple_of(chunk * down.size + piece * size, size), size)
            scaled = cot[:, cols].astype(F32) * factor
            out[...] += across_offsets(scaled, down.offsets[:, cols], down.step_rows(cols))

    return work, back


def halves_out(mine, part, kept_out, sent_out, cols):
    half = part.shape[0] // 2
    first, second = part[:half], part[half:]
    kept_out[:, cols] = jnp.where(mine == 0, first, second).astype(BF16)
    sent_out[:, cols] = jnp.where(mine == 0, second, first).astype(BF16)


def later(count, copies, work, last=None):
    def step(chunk, _):
        for copy in copies(chunk):
            copy.wait()

        @pl.when(chunk + AHEAD < count)
        def _():
            for copy in copies(chunk + AHEAD):
                copy.start()

        if last is not None:
            @pl.when(chunk + AHEAD >= count)
            def _():
                last(chunk + AHEAD - count)

        work(chunk)
        return 0

    lax.fori_loop(0, count, step, 0)


def first_forward_kernel(layer, mine, x_any, gate_any, up_any, code_any, zero_any, gs_any, us_any, ds_any, *refs):
    gate_out, up_out, hidden_out, kept_out, sent_out, off_any = refs[:6]
    x, sem = refs[6:8]
    gate = Matrix(layer, gate_any, gs_any, *refs[8:11], True)
    up = Matrix(layer, up_any, us_any, *refs[11:14], True)
    codes = DownCodes(layer, code_any, zero_any, off_any, *refs[14:19])
    down = Matrix(layer, off_any, ds_any, codes.out, *refs[19:21], False)
    x_copy = copy_in(x_any, x, sem.at[0])
    codes.zero_copy().start()
    down.step_copy().start()

    def before():
        x_copy.wait()
        codes.zero_copy().wait()

    def beside(chunk, turn, turns):
        for index in range(turn * codes.tiles // turns, (turn + 1) * codes.tiles // turns):
            codes.tile_of(chunk, index)

    hidden_out[...] = gate_up_forward(
        x, gate, up, gate_out, up_out, before, beside, codes
    )
    for chunk in range(COUNT):
        codes.out_copy(chunk).start()
    down.step_copy().wait()

    def work(chunk, _):
        part = jnp.dot(hidden_out[...], down.weights(chunk), preferred_element_type=F32)
        halves_out(mine[0], part, kept_out, sent_out, row_chunk(chunk, down.size))
        return 0

    lax.fori_loop(0, COUNT, work, 0)
    for chunk in range(COUNT):
        codes.out_copy(chunk).wait()


def first_forward(layer, mine, x, gate, up, down_codes, down_zero, gate_step, up_step, down_step):
    tokens, depth = x.shape
    width = gate.shape[1]
    return pl.pallas_call(
        functools.partial(first_forward_kernel, layer),
        in_specs=[SCALAR, ANYWHERE] + [IN_HBM] * 7,
        out_specs=[pl.BlockSpec(memory_space=pltpu.VMEM)] * 5 + [IN_HBM],
        out_shape=[
            jax.ShapeDtypeStruct((tokens, width), F32),
            jax.ShapeDtypeStruct((tokens, width), F32),
            jax.ShapeDtypeStruct((tokens, width), BF16),
            jax.ShapeDtypeStruct((tokens // 2, depth), BF16),
            jax.ShapeDtypeStruct((tokens // 2, depth), BF16),
            jax.ShapeDtypeStruct((width, depth), OFFSET),
        ],
        scratch_shapes=[pltpu.VMEM(x.shape, BF16), pltpu.SemaphoreType.DMA((1,))]
        + Matrix.scratch(gate, gate_step)
        + Matrix.scratch(up, up_step)
        + DownCodes.scratch(down_codes, down_zero)
        + [pltpu.VMEM(down_step.shape, F32), pltpu.SemaphoreType.DMA((COUNT + 1,))],
        compiler_params=params(),
        cost_estimate=cost(6 * tokens * depth * width, 4 * depth * width),
    )(mine, x, gate, up, down_codes, down_zero, gate_step, up_step, down_step)


def last_layer_kernel(layer, mine, x_any, cot_any, gate_any, up_any, down_any, gs_any, us_any, ds_any, *refs):
    hidden_out, gate_grad_out, up_grad_out, kept_out, sent_out = refs[:5]
    gate_pre, up_value, hidden_grad, scaled_gate, scaled_up, x, cot, sem = refs[5:13]
    gate = Matrix(layer, gate_any, gs_any, *refs[13:16], True)
    up = Matrix(layer, up_any, us_any, *refs[16:19], True)
    down = Matrix(layer, down_any, ds_any, *refs[19:22], False)
    x_copy = copy_in(x_any, x, sem.at[0])
    hidden_out[...] = gate_up_forward(x, gate, up, gate_pre, up_value, x_copy.wait, None, None, down)
    cot_copy = copy_in(cot_any, cot, sem.at[1])
    down.step_copy().start()
    cot_copy.wait()
    down.step_copy().wait()
    hidden_grad[...] = jnp.zeros_like(hidden_grad)
    down_work, back = cot_down(cot, down, hidden_grad)

    later(down.count, lambda chunk: [down.copy(chunk)], down_work)
    gate_grad, up_grad = hidden_back(hidden_grad[...] * back, gate_pre[...], up_value[...])
    gate_grad_out[...] = gate_grad
    up_grad_out[...] = up_grad
    product = gate_up_backward(gate_grad, up_grad, gate, up, scaled_gate, scaled_up)

    def work(chunk, _):
        halves_out(mine[0], product(chunk), kept_out, sent_out, row_chunk(chunk, gate.size))
        return 0

    lax.fori_loop(0, COUNT, work, 0)


def last_layer(layer, mine, x, cot, gate, up, down, gate_step, up_step, down_step):
    tokens, depth = x.shape
    width = gate.shape[1]
    small = jax.ShapeDtypeStruct((tokens, width), BF16)
    return pl.pallas_call(
        functools.partial(last_layer_kernel, layer),
        in_specs=[SCALAR] + [ANYWHERE] * 2 + [IN_HBM] * 6,
        out_shape=[
            small,
            small,
            small,
            jax.ShapeDtypeStruct((tokens // 2, depth), BF16),
            jax.ShapeDtypeStruct((tokens // 2, depth), BF16),
        ],
        scratch_shapes=[pltpu.VMEM((tokens, width), F32)] * 5
        + [
            pltpu.VMEM(x.shape, BF16),
            pltpu.VMEM(cot.shape, BF16),
            pltpu.SemaphoreType.DMA((2,)),
        ]
        + Matrix.scratch(gate, gate_step)
        + Matrix.scratch(up, up_step)
        + Matrix.scratch(down, down_step),
        compiler_params=params(),
        cost_estimate=cost(10 * tokens * depth * width, 4 * depth * width),
    )(mine, x, cot, gate, up, down, gate_step, up_step, down_step)


def backward_kernel(layer, mine, cot_any, pre_any, value_any, gate_any, up_any, down_any, gs_any, us_any, ds_any, *refs):
    gate_grad_out, up_grad_out, kept_out, sent_out = refs[:4]
    gate_pre, up_value, hidden_grad, scaled_gate, scaled_up, cot, sem = refs[4:11]
    gate = Matrix(layer, gate_any, gs_any, *refs[11:14], True)
    up = Matrix(layer, up_any, us_any, *refs[14:17], True)
    down = Matrix(layer, down_any, ds_any, *refs[17:20], False)
    cot_copy = copy_in(cot_any, cot, sem.at[0])
    down.step_copy().start()
    for chunk in range(AHEAD):
        down.copy(chunk).start()
    pre_copy = copy_in(pre_any, gate_pre, sem.at[1])
    value_copy = copy_in(value_any, up_value, sem.at[2])
    hidden_grad[...] = jnp.zeros_like(hidden_grad)
    cot_copy.wait()
    down.step_copy().wait()
    down_work, back = cot_down(cot, down, hidden_grad)

    def last(chunk):
        gate.copy(chunk).start()
        up.copy(chunk).start()

    later(down.count, lambda chunk: [down.copy(chunk)], down_work, last)
    gate.step_copy().start()
    up.step_copy().start()
    pre_copy.wait()
    value_copy.wait()
    gate_grad, up_grad = hidden_back(hidden_grad[...] * back, gate_pre[...], up_value[...])
    gate_grad_out[...] = gate_grad
    up_grad_out[...] = up_grad
    gate.step_copy().wait()
    up.step_copy().wait()
    product = gate_up_backward(gate_grad, up_grad, gate, up, scaled_gate, scaled_up)

    def work(chunk):
        halves_out(mine[0], product(chunk), kept_out, sent_out, row_chunk(chunk, gate.size))

    later(gate.count, lambda chunk: [gate.copy(chunk), up.copy(chunk)], work)


def backward(layer, mine, cot, gate_pre, up_value, gate, up, down, gate_step, up_step, down_step):
    tokens, depth = cot.shape
    width = gate.shape[1]
    small = jax.ShapeDtypeStruct((tokens, width), BF16)
    return pl.pallas_call(
        functools.partial(backward_kernel, layer),
        in_specs=[SCALAR] + [ANYWHERE] * 3 + [IN_HBM] * 6,
        out_shape=[small, small] + [jax.ShapeDtypeStruct((tokens // 2, depth), BF16)] * 2,
        scratch_shapes=[pltpu.VMEM((tokens, width), F32)] * 5
        + [pltpu.VMEM(cot.shape, BF16), pltpu.SemaphoreType.DMA((3,))]
        + Matrix.scratch(gate, gate_step)
        + Matrix.scratch(up, up_step)
        + Matrix.scratch(down, down_step),
        compiler_params=params(),
        cost_estimate=cost(6 * tokens * depth * width, 3 * depth * width),
    )(mine, cot, gate_pre, up_value, gate, up, down, gate_step, up_step, down_step)


def spread(x, groups):
    tokens = x.shape[0]
    tall = jnp.concatenate([x] * groups, axis=0)
    row_group = lax.broadcasted_iota(jnp.int32, tall.shape, 0) // tokens
    col_group = lax.broadcasted_iota(jnp.int32, tall.shape, 1) // GROUP
    return jnp.where(row_group == col_group, tall.astype(F32), 0.0).astype(BF16)


def step_grad_block(x, offsets, upstream):
    tokens = x.shape[0]
    rows = []
    groups = offsets.shape[0] // GROUP
    for first in range(0, groups, 4):
        count = min(4, groups - first)
        part = slice(first * GROUP, (first + count) * GROUP)
        product = jnp.dot(
            spread(x[:, part], count), offsets[part, :].astype(BF16), preferred_element_type=F32
        )
        for group in range(count):
            own = product[group * tokens : (group + 1) * tokens] * upstream
            rows.append(jnp.sum(own, axis=0, keepdims=True))
    return jnp.concatenate(rows, axis=0)


def step_grad_kernel(by_rows, half, halves, x_any, off_any, grad_any, *refs):
    out, x, offsets, grad, sem, sems = refs[-6:]
    count = COUNT // halves
    size = offsets.shape[0 if by_rows else 1] // count

    def places(chunk):
        chunk = row_chunk(chunk, size)
        return (chunk, slice(None)) if by_rows else (slice(None), chunk)

    def copy(chunk):
        return pltpu.make_async_copy(
            off_any.at[places(half * count + chunk)], offsets.at[places(chunk)], sems.at[chunk]
        )

    if by_rows:
        own = row_chunk(half, x.shape[1])
        x_copy = copy_in(x_any.at[:, own], x, sem.at[0])
        grad_copy = copy_in(grad_any, grad, sem.at[1])
    else:
        own = row_chunk(half, grad.shape[1])
        x_copy = copy_in(x_any, x, sem.at[0])
        grad_copy = copy_in(grad_any.at[:, own], grad, sem.at[1])
    def ready():
        x_copy.wait()
        grad_copy.wait()

    def work(chunk):
        part = row_chunk(chunk, size)
        if by_rows:
            out[row_chunk(chunk, size // GROUP), :] = step_grad_block(
                x[:, part], offsets[part, :], grad[...].astype(F32)
            )
        else:
            found = step_grad_block(x[...], offsets[:, part], grad[:, part].astype(F32))
            if len(out.shape) == 2:
                out[:, part] = found
            else:
                other = refs[0][:, part]
                for place in range(out.shape[0]):
                    out[place, 0:1, part] = found[place : place + 1]
                    out[place, 1:2, part] = other[place : place + 1]

    stream(count, lambda chunk: [copy(chunk)], work, ready)


def step_grad(x, offsets, upstream, layer, half, halves, earlier, last=None):
    tokens, depth = x.shape
    width = offsets.shape[1]
    groups = depth // GROUP
    by_rows = depth >= width
    operands = [x, offsets, upstream]
    in_specs = [ANYWHERE, IN_HBM, ANYWHERE]
    scratch = [x.shape, offsets.shape, upstream.shape]
    if by_rows:
        shape = (LAYERS, groups, width)
        out_spec = pl.BlockSpec((None, groups // halves, width), lambda i: (layer, half, 0))
        scratch[0] = (tokens, depth // halves)
        scratch[1] = (depth // halves, width)
    else:
        shape = (groups, width) if last is None else (groups, LAYERS, width)
        block = shape[:-1] + (width // halves,)
        out_spec = pl.BlockSpec(block, lambda i: (0,) * (len(shape) - 1) + (half,))
        scratch[1] = (depth, width // halves)
        scratch[2] = (tokens, width // halves)
    if last is not None:
        operands.append(last)
        in_specs.append(pl.BlockSpec((groups, width // halves), lambda i: (0, half)))
    aliases = {}
    if earlier is not None:
        aliases = {len(operands): 0}
        operands.append(earlier)
        in_specs.append(IN_HBM)
    return pl.pallas_call(
        functools.partial(step_grad_kernel, by_rows, half, halves),
        grid=(1,),
        in_specs=in_specs,
        out_specs=out_spec,
        out_shape=jax.ShapeDtypeStruct(shape, F32),
        scratch_shapes=[
            pltpu.VMEM(scratch[0], BF16),
            pltpu.VMEM(scratch[1], OFFSET),
            pltpu.VMEM(scratch[2], BF16),
            pltpu.SemaphoreType.DMA((2,)),
            pltpu.SemaphoreType.DMA((COUNT,)),
        ],
        input_output_aliases=aliases,
        compiler_params=params(),
        cost_estimate=cost(8 * tokens * depth * width // halves, depth * width // halves),
    )(*operands)


class Side:
    def __init__(self, *jobs):
        self.jobs = list(jobs)

    def swap(self, value, bit):
        count = lax.axis_size("tensor")
        pairs = [(i, i ^ bit) for i in range(count)]
        job = self.jobs.pop(0) if self.jobs else None
        if job is None:
            return lax.ppermute(value, "tensor", pairs)
        call, operands, results = job
        value, operands = lax.optimization_barrier((value, operands))
        got = lax.ppermute(value, "tensor", pairs)
        found = call(*operands, results.get("value"))
        got, results["value"] = lax.optimization_barrier((got, found))
        return got


def own_bit(bit):
    return (lax.axis_index("tensor") // bit) % 2


def halve_first(side, kept, sent, bit):
    return kept.astype(F32) + side.swap(sent, bit).astype(F32)


def halve(side, value, bit):
    half = value.shape[0] // 2
    mine = own_bit(bit)
    kept = lax.dynamic_slice_in_dim(value, mine * half, half, 0)
    sent = lax.dynamic_slice_in_dim(value, (1 - mine) * half, half, 0)
    got = side.swap(sent.astype(BF16), bit)
    return kept.astype(F32) + got.astype(F32)


def add_up(side, value, bit):
    rounded = value.astype(BF16)
    return rounded.astype(F32) + side.swap(rounded, bit).astype(F32)


def double(side, value, bit, axis):
    other = side.swap(value, bit)
    mine = own_bit(bit) == 0
    return jnp.concatenate(
        [jnp.where(mine, value, other), jnp.where(mine, other, value)], axis=axis
    )


def inverse_rms(values):
    return lax.rsqrt(jnp.mean(values * values, axis=-1, keepdims=True) + norm_epsilon)


def norm_rows(state, gain):
    values = state.astype(F32)
    return (values * inverse_rms(values) * gain).astype(BF16)


def norm_back(state, gain, upstream):
    values = state.astype(F32)
    scale = inverse_rms(values)
    normal = values * scale
    inner = upstream * gain
    return scale * (inner - normal * jnp.mean(inner * normal, axis=-1, keepdims=True))


def token_lengths(doc_lengths, index_rows, micro_rows):
    batch_index = index_rows // micro_rows
    position = index_rows % micro_rows
    picked = batch_index[:, None] == jnp.arange(doc_lengths.shape[0], dtype=jnp.int32)[None, :]
    chosen = jnp.sum(jnp.where(picked[:, :, None], doc_lengths[None, :, :], 0), axis=1)
    ends = jnp.sum(
        jnp.where(
            jnp.arange(chosen.shape[1])[:, None] <= jnp.arange(chosen.shape[1])[None, :],
            chosen[:, :, None],
            0,
        ),
        axis=1,
    )
    starts = ends - chosen
    inside = (position[:, None] >= starts) & (position[:, None] < ends)
    return jnp.sum(jnp.where(inside, chosen, 0), axis=1).astype(F32)


def on_device(
    tokens,
    norm_gain,
    gate_codes,
    up_codes,
    down_codes,
    gate_zero,
    up_zero,
    down_zero,
    gate_step,
    up_step,
    down_step,
    out_grad,
    doc_lengths,
):
    shard_rows, features = tokens.shape
    device_count = lax.axis_size("tensor")
    micro_rows = shard_rows * device_count // doc_lengths.shape[0]
    bits = [1 << k for k in range(device_count.bit_length() - 1)]
    near, far = bits[:-2], bits[-2:]

    far_count = 1 << len(far)
    far_index = np.arange(far_count)
    far_place = sum(((far_index >> k) & 1) << (len(far) - 1 - k) for k in range(len(far)))
    far_device = np.argsort(far_place)
    near_part = lax.axis_index("tensor") % (1 << len(near))
    device_ids = near_part + jnp.asarray(far_device << len(near), jnp.int32)
    row_ids = (
        device_ids[:, None] * shard_rows + jnp.arange(shard_rows, dtype=jnp.int32)[None, :]
    ).reshape(-1)
    lengths = token_lengths(doc_lengths, row_ids, micro_rows)

    down_step, down_zero = down_step.transpose(1, 0, 2), down_zero.transpose(1, 0, 2)

    def offsets_jobs(codes, zeros, layer, unpack_half=offsets_of):
        results = {}
        call = lambda c, z, earlier: unpack_half(c, z, layer, earlier)
        return [(call, (codes, zeros), results)] * 2, results

    gate_jobs, gate_0 = offsets_jobs(gate_codes, gate_zero, 0)
    up_jobs, up_0 = offsets_jobs(up_codes, up_zero, 0)
    side = Side(*gate_jobs, *up_jobs)
    pair = jnp.stack([tokens, out_grad])
    for bit in reversed(far):
        pair = double(side, pair, bit, 1)
    state_0 = pair[0]
    cot_rows = (pair[1].astype(F32) / lengths[:, None]).astype(BF16)
    pair = jnp.stack([norm_rows(pair[0], norm_gain[0]), cot_rows])
    for bit in reversed(near):
        pair = double(side, pair, bit, 1)
    normed_0, cotangent = pair[0], pair[1]
    gate_0, up_0 = gate_0["value"], up_0["value"]

    mine = own_bit(near[0]).reshape(1).astype(jnp.int32)
    gate_pre, up_value, hidden_0, kept, sent, down_0 = first_forward(
        0, mine, normed_0, gate_0, up_0, down_codes, down_zero, gate_step, up_step, down_step
    )

    gate_jobs, gate_1 = offsets_jobs(gate_codes, gate_zero, 1)
    up_jobs, up_1 = offsets_jobs(up_codes, up_zero, 1)
    down_jobs, down_1 = offsets_jobs(down_codes, down_zero, 1, down_offsets_of)
    side = Side(None, gate_jobs[0], *down_jobs, gate_jobs[1], *up_jobs)
    part = halve_first(side, kept, sent, near[0])
    for bit in near[1:]:
        part = halve(side, part, bit)
    for bit in far:
        part = add_up(side, part, bit)
    state_1 = (state_0.astype(F32) + part).astype(BF16)
    normed_1 = norm_rows(state_1, norm_gain[1])
    for bit in reversed(near):
        normed_1 = double(side, normed_1, bit, 0)
    gate_1, up_1, down_1 = gate_1["value"], up_1["value"], down_1["value"]

    hidden_1, gate_grad, up_grad, kept, sent = last_layer(
        1, mine, normed_1, cotangent, gate_1, up_1, down_1, gate_step, up_step, down_step
    )

    down_out, gate_out, up_out = {}, {}, {}

    def half_jobs(x, offsets, upstream, results):
        return [
            (
                lambda x, u, earlier, half=half: step_grad(x, offsets, u, 1, half, 2, earlier),
                (x, upstream),
                results,
            )
            for half in range(2)
        ]

    side = Side(
        None,
        *half_jobs(hidden_1, down_1, cotangent, down_out),
        *half_jobs(normed_1, gate_1, gate_grad, gate_out),
        *half_jobs(normed_1, up_1, up_grad, up_out),
    )
    part = halve_first(side, kept, sent, near[0])
    for bit in near[1:]:
        part = halve(side, part, bit)
    for bit in far:
        part = add_up(side, part, bit)
    cot_rows = (cot_rows.astype(F32) + norm_back(state_1, norm_gain[1], part)).astype(BF16)
    cotangent = cot_rows
    for bit in reversed(near):
        cotangent = double(side, cotangent, bit, 0)

    gate_grad, up_grad, kept, sent = backward(
        0,
        mine,
        cotangent,
        gate_pre,
        up_value,
        gate_0,
        up_0,
        down_0,
        gate_step,
        up_step,
        down_step,
    )
    last = down_out["value"]
    down_out = {}
    side = Side(
        None,
        (
            lambda x, u, earlier: step_grad(x, down_0, u, 0, 0, 1, earlier, last),
            (hidden_0, cotangent),
            down_out,
        ),
        (
            lambda x, u, earlier: step_grad(x, gate_0, u, 0, 0, 1, earlier),
            (normed_0, gate_grad),
            gate_out,
        ),
        (
            lambda x, u, earlier: step_grad(x, up_0, u, 0, 0, 1, earlier),
            (normed_0, up_grad),
            up_out,
        ),
    )
    part = halve_first(side, kept, sent, near[0])
    for bit in near[1:]:
        part = halve(side, part, bit)
    for bit in far:
        part = halve(side, part, bit)
        half = cot_rows.shape[0] // 2
        cot_rows = lax.dynamic_slice_in_dim(cot_rows, own_bit(bit) * half, half, 0)
    result = (cot_rows.astype(F32) + norm_back(tokens, norm_gain[0], part)).astype(BF16)
    return result, gate_out["value"], up_out["value"], down_out["value"].transpose(1, 0, 2)


def solution(mesh):
    placed = (
        P(("groups", "tensor"), None),
        P(),
        P(None, None, "tensor"),
        P(None, None, "tensor"),
        P(None, "tensor", None),
        P(None, None, "tensor"),
        P(None, None, "tensor"),
        P(None, "tensor", None),
        P(None, None, "tensor"),
        P(None, None, "tensor"),
        P(None, "tensor", None),
        P(("groups", "tensor"), None),
        P("groups", None),
    )
    return jax.shard_map(
        on_device,
        mesh=mesh,
        in_specs=placed,
        out_specs=(
            P(("groups", "tensor"), None),
            P("groups", None, "tensor"),
            P("groups", None, "tensor"),
            P("groups", "tensor", None),
        ),
        check_vma=False,
    )
```

time: 331 us -> 201 us (0.61)
  Pallas kernels: 201 us -> 139 us
  waiting for transfers between devices: 50.9 us -> 13.6 us
  local copies, waits for them, and re-layouts: 16.2 us -> 2.1 us
  starting transfers between devices: 39.7 us -> 28.7 us
    pallas_call x19 -> x22, Pallas kernels: 201 us -> 139 us  [the longest x8 38.2 us: offsets_of(): pl.pallas_call(functools.partial(offsets_kernel, layer, 0 if earlier is N...]
    ppermute x26, waiting for transfers between devices: 50.9 us -> 13.6 us  [the longest x7 11.6 us: swap(): return lax.ppermute(value, 'tensor', pairs)]
    unnamed x60 -> x7, local copies, waits for them, and re-layouts: 12.8 us -> 0.78 us
    ppermute x26, starting transfers between devices: 39.7 us -> 28.7 us  [the longest x19 26.2 us: swap(): got = lax.ppermute(value, 'tensor', pairs)]
  transfers between devices with their start and end apart: 26 -> 26, of which waited for: 18 -> 12; matrix products, arithmetic and copies ran while one was open for 3% -> 2% of each run, Pallas kernels for 41% -> 43%
where the time goes in v3:
time: 201 us; the launch traced here: 200 us
  Pallas kernels  139 us (69%)
  starting transfers between devices  28.7 us (14%)
  other arithmetic  13.9 us (7%)
  waiting for transfers between devices  13.6 us (7%)
  between operations  2.63 us (1%)
  local copies, waits for them, and re-layouts  2.1 us (1%)
    pallas_call x8, Pallas kernels, offsets_of(): pl.pallas_call(functools.partial(offsets_kernel, layer, 0 if earlier is N...  38.2 us
    pallas_call x9, Pallas kernels, step_grad(): pl.pallas_call(functools.partial(step_grad_kernel, by_rows, half, halves)...  38 us
    ppermute x19, starting transfers between devices, swap(): got = lax.ppermute(value, 'tensor', pairs)  26.2 us
    pallas_call x1, Pallas kernels, last_layer(): pl.pallas_call(functools.partial(last_layer_kernel, layer), in_specs=[SCA...  20.6 us
    pallas_call x1, Pallas kernels, first_forward(): pl.pallas_call(functools.partial(first_forward_kernel, layer), in_specs=[...  17.1 us
    pallas_call x1, Pallas kernels, backward(): pl.pallas_call(functools.partial(backward_kernel, layer), in_specs=[SCALA...  14.6 us
    ppermute x7, waiting for transfers between devices, swap(): return lax.ppermute(value, 'tensor', pairs)  11.6 us
    pallas_call x2, Pallas kernels, down_offsets_of(): pl.pallas_call(functools.partial(down_offsets_kernel, layer, 0 if earlier...  10.5 us
  transfers between devices with their start and end apart: 26, of which 12 were waited for; matrix products, arithmetic and copies ran while one was open for 2% of the time, Pallas kernels for 43%

profile of v3, /device:TPU:0, one launch (start us, length us, event | category | flops | bytes accessed | tf_op | source)
XLA Modules:
  0.0 199.9 jit_solution(6293758856121760552)
XLA Ops:
  0.6 0.9 pad_maximum_fusion.11
  1.5 4.1 %collective-permute-start = (bf16[2,1,8192]{2,1,0:T(2,128)(2,1)S(1)}, bf16[2,1,8192]{2,1,0:T(2,128)(2,1)S(1)}, u32[]{:S(2)}, u32[]{:S(2)}) collective-permute-start(bf16[2,1,8192]{2,1,0:T(2,128)(2,1)S(1)} %pad_maximum_fusion.11), channel_id=1, source_target_pairs={{0,16},{1,17},{2,18},{3,19},{4,20},{5,21},{6,22},{7,23},{8,24},{9,... | collective-permute-start | bytes 98312 | tf_op jit(solution)/shard_map/ppermute | solution.py:760
  5.6 0.7 and_select_fusion.1
  6.3 0.7 and_select_fusion
  7.0 0.8 copy.28
  7.8 1.0 fusion.25
  9.1 4.8 %shard_map.165.refs_2_ = f8e4m3fn[8192,768]{1,0:T(32,128)(4,1)} custom-call(s32[2,2048,768]{2,1,0:T(8,128)} %refs_0_.7, s32[2,128,768]{2,1,0:T(8,128)} %refs_1_.5), custom_call_target="tpu_custom_call" | custom-call | flops 31457280 | bytes 6291456 | tf_op jit(solution)/shard_map/pallas_call | solution.py:139
  14.3 1.6 collective-permute-start.1
  15.9 4.7 %shard_map.166.gate_any.off_any = f8e4m3fn[8192,768]{1,0:T(32,128)(4,1)} custom-call(s32[2,2048,768]{2,1,0:T(8,128)} %refs_0_.7, s32[2,128,768]{2,1,0:T(8,128)} %refs_1_.5, f8e4m3fn[8192,768]{1,0:T(32,128)(4,1)} %shard_map.165.refs_2_), custom_call_target="tpu_custom_call", output_to_operand_aliasing={{}: (2, {})} | custom-call | flops 31457280 | bytes 6291456 | tf_op jit(solution)/shard_map/pallas_call | solution.py:139
  21.4 1.6 collective-permute-start.2
  22.9 4.8 %shard_map.167.refs_2_ = f8e4m3fn[8192,768]{1,0:T(32,128)(4,1)} custom-call(s32[2,2048,768]{2,1,0:T(8,128)} %refs_0_.9, s32[2,128,768]{2,1,0:T(8,128)} %refs_1_.7), custom_call_target="tpu_custom_call" | custom-call | flops 31457280 | bytes 6291456 | tf_op jit(solution)/shard_map/pallas_call | solution.py:139
  28.0 1.6 collective-permute-start.3
  29.6 4.9 %shard_map.168.up_any.off_any = f8e4m3fn[8192,768]{1,0:T(32,128)(4,1)} custom-call(s32[2,2048,768]{2,1,0:T(8,128)} %refs_0_.9, s32[2,128,768]{2,1,0:T(8,128)} %refs_1_.7, f8e4m3fn[8192,768]{1,0:T(32,128)(4,1)} %shard_map.167.refs_2_), custom_call_target="tpu_custom_call", output_to_operand_aliasing={{}: (2, {})} | custom-call | flops 31457280 | bytes 6291456 | tf_op jit(solution)/shard_map/pallas_call | solution.py:139
  34.5 0.8 collective-permute-done.3
  35.6 1.9 collective-permute-done.4
  37.7 1.0 fusion.2
  38.7 17.1 %shard_map.169 = (f32[32,768]{1,0:T(8,128)}, f32[32,768]{1,0:T(8,128)}, bf16[32,768]{1,0:T(8,128)(2,1)}, bf16[16,8192]{1,0:T(8,128)(2,1)}, bf16[16,8192]{1,0:T(8,128)(2,1)}, /*index=5*/f8e4m3fn[768,8192]{1,0:T(32,128)(4,1)}) custom-call(s32[1]{0:T(128)} %bitcast.4.mine, bf16[32,8192]{1,0:T(8,128)(2,1)} %get-tuple-element.217.x_any, ...), custom_call_target="tpu_custom_call" | custom-call | flops 1207959552 | bytes 25165824 | tf_op jit(solution)/shard_map/pallas_call | solution.py:498
  56.1 1.6 collective-permute-done.5
  57.7 1.0 convert_add_fusion.2
  58.7 1.6 collective-permute-start.6
  60.3 4.8 %shard_map.170.refs_2_ = f8e4m3fn[8192,768]{1,0:T(32,128)(4,1)} custom-call(s32[2,2048,768]{2,1,0:T(8,128)} %refs_0_.7, s32[2,128,768]{2,1,0:T(8,128)} %refs_1_.5), custom_call_target="tpu_custom_call" | custom-call | flops 31457280 | bytes 6291456 | tf_op jit(solution)/shard_map/pallas_call | solution.py:139
  65.2 0.6 collective-permute-start.7
  65.8 5.3 %shard_map.171.refs_2_ = f8e4m3fn[768,8192]{1,0:T(32,128)(4,1)} custom-call(s32[2,192,8192]{2,1,0:T(8,128)} %refs_0_.6, s32[12,2,8192]{2,1,0:T(2,128)} %bitcast.32), custom_call_target="tpu_custom_call" | custom-call | flops 31457280 | bytes 6291456 | tf_op jit(solution)/shard_map/pallas_call | solution.py:236
  71.1 0.5 collective-permute-start.8
  71.6 5.2 %shard_map.172.down_any.off_any = f8e4m3fn[768,8192]{1,0:T(32,128)(4,1)} custom-call(s32[2,192,8192]{2,1,0:T(8,128)} %refs_0_.6, s32[12,2,8192]{2,1,0:T(2,128)} %bitcast.33, f8e4m3fn[768,8192]{1,0:T(32,128)(4,1)} %shard_map.171.refs_2_), custom_call_target="tpu_custom_call", output_to_operand_aliasing={{}: (2, {})} | custom-call | flops 31457280 | bytes 6291456 | tf_op jit(solution)/shard_map/pallas_call | solution.py:236
  77.3 4.7 %shard_map.173.gate_any.off_any = f8e4m3fn[8192,768]{1,0:T(32,128)(4,1)} custom-call(s32[2,2048,768]{2,1,0:T(8,128)} %refs_0_.7, s32[2,128,768]{2,1,0:T(8,128)} %refs_1_.5, f8e4m3fn[8192,768]{1,0:T(32,128)(4,1)} %shard_map.170.refs_2_), custom_call_target="tpu_custom_call", output_to_operand_aliasing={{}: (2, {})} | custom-call | flops 31457280 | bytes 6291456 | tf_op jit(solution)/shard_map/pallas_call | solution.py:139
  82.5 1.6 collective-permute-start.10
  84.1 4.7 %shard_map.174.refs_2_ = f8e4m3fn[8192,768]{1,0:T(32,128)(4,1)} custom-call(s32[2,2048,768]{2,1,0:T(8,128)} %refs_0_.9, s32[2,128,768]{2,1,0:T(8,128)} %refs_1_.7), custom_call_target="tpu_custom_call" | custom-call | flops 31457280 | bytes 6291456 | tf_op jit(solution)/shard_map/pallas_call | solution.py:139
  89.0 0.7 collective-permute-start.11
  89.8 4.8 %shard_map.175.up_any.off_any = f8e4m3fn[8192,768]{1,0:T(32,128)(4,1)} custom-call(s32[2,2048,768]{2,1,0:T(8,128)} %refs_0_.9, s32[2,128,768]{2,1,0:T(8,128)} %refs_1_.7, f8e4m3fn[8192,768]{1,0:T(32,128)(4,1)} %shard_map.174.refs_2_), custom_call_target="tpu_custom_call", output_to_operand_aliasing={{}: (2, {})} | custom-call | flops 31457280 | bytes 6291456 | tf_op jit(solution)/shard_map/pallas_call | solution.py:139
  94.8 1.5 collective-permute-done.12
  96.4 0.8 pad_maximum_fusion.2.x_any
  97.2 20.6 %shard_map.176 = (bf16[32,768]{1,0:T(8,128)(2,1)}, bf16[32,768]{1,0:T(8,128)(2,1)}, bf16[32,768]{1,0:T(8,128)(2,1)}, bf16[16,8192]{1,0:T(8,128)(2,1)}, bf16[16,8192]{1,0:T(8,128)(2,1)}) custom-call(s32[1]{0:T(128)} %bitcast.4.mine, bf16[32,8192]{1,0:T(8,128)(2,1)} %pad_maximum_fusion.2.x_any, bf16[32,8192]{1,0:T(8,128)(2,1)} %get-tuple-element.175.cot_any.grad_any, ...), custom_call_target="tpu_custom_call" | custom-call | flops 2013265920 | bytes 25165824 | tf_op jit(solution)/shard_map/pallas_call | solution.py:552
  118.1 1.6 collective-permute-done.13
  119.7 1.0 convert_add_fusion.1
  120.7 1.4 collective-permute-start.14
  122.1 3.5 %shard_map.177.refs_0_ = f32[12,8192]{1,0:T(8,128)} custom-call(bf16[32,768]{1,0:T(8,128)(2,1)} %get-tuple-element.174.x_any, f8e4m3fn[768,8192]{1,0:T(32,128)(4,1)} %shard_map.172.down_any.off_any, bf16[32,8192]{1,0:T(8,128)(2,1)} %get-tuple-element.175.cot_any.grad_any), custom_call_target="tpu_custom_call" | custom-call | flops 805306368 | bytes 3145728 | tf_op jit(solution)/shard_map/pallas_call | solution.py:729
  125.6 0.7 collective-permute-done.14
  126.4 0.6 collective-permute-start.15
  127.0 3.5 %shard_map.178.refs_0_ = f32[12,8192]{1,0:T(8,128)} custom-call(bf16[32,768]{1,0:T(8,128)(2,1)} %get-tuple-element.174.x_any, f8e4m3fn[768,8192]{1,0:T(32,128)(4,1)} %shard_map.172.down_any.off_any, bf16[32,8192]{1,0:T(8,128)(2,1)} %get-tuple-element.175.cot_any.grad_any, f32[12,8192]{1,0:T(8,128)} %shard_map.177.refs_0_), custom_call_target="tpu_custom_call", output_to_operand_aliasing={{}: (3, {})} | custom-call | flops 805306368 | bytes 3145728 | tf_op jit(solution)/shard_map/pallas_call | solution.py:729
  130.8 1.6 collective-permute-start.16
  132.4 3.5 %shard_map.179.refs_0_ = f32[2,128,768]{2,1,0:T(8,128)} custom-call(bf16[32,8192]{1,0:T(8,128)(2,1)} %pad_maximum_fusion.2.x_any, f8e4m3fn[8192,768]{1,0:T(32,128)(4,1)} %shard_map.173.gate_any.off_any, bf16[32,768]{1,0:T(8,128)(2,1)} %get-tuple-element.185.grad_any), custom_call_target="tpu_custom_call" | custom-call | flops 805306368 | bytes 3145728 | tf_op jit(solution)/shard_map/pallas_call | solution.py:729
  136.0 2.6 %collective-permute-start.17 = (bf16[4,8192]{1,0:T(4,128)(2,1)S(1)}, bf16[4,8192]{1,0:T(4,128)(2,1)S(1)}, u32[]{:S(2)}, u32[]{:S(2)}) collective-permute-start(bf16[4,8192]{1,0:T(4,128)(2,1)S(1)} %add_convert_fusion), channel_id=1, source_target_pairs={{0,16},{1,17},{2,18},{3,19},{4,20},{5,21},{6,22},{7,23},{8,24},{9,... | collective-permute-start | bytes 196616 | tf_op jit(solution)/shard_map/ppermute | solution.py:760
  138.6 3.5 %shard_map.180.refs_0_ = f32[2,128,768]{2,1,0:T(8,128)} custom-call(bf16[32,8192]{1,0:T(8,128)(2,1)} %pad_maximum_fusion.2.x_any, f8e4m3fn[8192,768]{1,0:T(32,128)(4,1)} %shard_map.173.gate_any.off_any, bf16[32,768]{1,0:T(8,128)(2,1)} %get-tuple-element.185.grad_any, f32[2,128,768]{2,1,0:T(8,128)} %shard_map.179.refs_0_), custom_call_target="tpu_custom_call", output_to_operand_aliasing={{}: (3, {})} | custom-call | flops 805306368 | bytes 3145728 | tf_op jit(solution)/shard_map/pallas_call | solution.py:729
  142.6 1.3 collective-permute-start.18
  143.9 3.5 %shard_map.181.refs_0_ = f32[2,128,768]{2,1,0:T(8,128)} custom-call(bf16[32,8192]{1,0:T(8,128)(2,1)} %pad_maximum_fusion.2.x_any, f8e4m3fn[8192,768]{1,0:T(32,128)(4,1)} %shard_map.175.up_any.off_any, bf16[32,768]{1,0:T(8,128)(2,1)} %get-tuple-element.195.grad_any), custom_call_target="tpu_custom_call" | custom-call | flops 805306368 | bytes 3145728 | tf_op jit(solution)/shard_map/pallas_call | solution.py:729
  147.6 1.4 collective-permute-start.19
  149.0 3.5 %shard_map.182.refs_0_ = f32[2,128,768]{2,1,0:T(8,128)} custom-call(bf16[32,8192]{1,0:T(8,128)(2,1)} %pad_maximum_fusion.2.x_any, f8e4m3fn[8192,768]{1,0:T(32,128)(4,1)} %shard_map.175.up_any.off_any, bf16[32,768]{1,0:T(8,128)(2,1)} %get-tuple-element.195.grad_any, f32[2,128,768]{2,1,0:T(8,128)} %shard_map.181.refs_0_), custom_call_target="tpu_custom_call", output_to_operand_aliasing={{}: (3, {})} | custom-call | flops 805306368 | bytes 3145728 | tf_op jit(solution)/shard_map/pallas_call | solution.py:729
  152.9 1.5 collective-permute-done.20
  154.5 0.8 pad_maximum_fusion.3.cot_any.grad_any
  155.3 14.6 %shard_map.183 = (bf16[32,768]{1,0:T(8,128)(2,1)}, bf16[32,768]{1,0:T(8,128)(2,1)}, bf16[16,8192]{1,0:T(8,128)(2,1)}, bf16[16,8192]{1,0:T(8,128)(2,1)}) custom-call(s32[1]{0:T(128)} %bitcast.4.mine, bf16[32,8192]{1,0:T(8,128)(2,1)} %pad_maximum_fusion.3.cot_any.grad_any, f32[32,768]{1,0:T(8,128)} %get-tuple-element.198.pre_any, ...), custom_call_target="tpu_custom_call" | custom-call | flops 1207959552 | bytes 18874368 | tf_op jit(solution)/shard_map/pallas_call | solution.py:619
  170.1 1.6 collective-permute-done.21
  171.7 1.0 convert_add_fusion
  172.7 1.4 collective-permute-start.22
  174.1 6.5 %shard_map.184 = f32[12,2,8192]{2,1,0:T(2,128)} custom-call(bf16[32,768]{1,0:T(8,128)(2,1)} %get-tuple-element.205.x_any, f8e4m3fn[768,8192]{1,0:T(32,128)(4,1)} %get-tuple-element.200.down_any.off_any, bf16[32,8192]{1,0:T(8,128)(2,1)} %pad_maximum_fusion.3.cot_any.grad_any, f32[12,8192]{1,0:T(8,128)} %shard_map.178.refs_0_), custom_call_target="tpu_custom_call" | custom-call | flops 1610612736 | bytes 6291456 | tf_op jit(solution)/shard_map/pallas_call | solution.py:729
  180.7 0.8 collective-permute-start.23
  181.5 5.2 %shard_map.185 = f32[2,128,768]{2,1,0:T(8,128)} custom-call(bf16[32,8192]{1,0:T(8,128)(2,1)} %get-tuple-element.217.x_any, f8e4m3fn[8192,768]{1,0:T(32,128)(4,1)} %shard_map.166.gate_any.off_any, bf16[32,768]{1,0:T(8,128)(2,1)} %get-tuple-element.212.grad_any, f32[2,128,768]{2,1,0:T(8,128)} %shard_map.180.refs_0_), custom_call_target="tpu_custom_call", output_to_operand_aliasing={{}: (3, {})} | custom-call | flops 1610612736 | bytes 6291456 | tf_op jit(solution)/shard_map/pallas_call | solution.py:729
  186.8 0.8 collective-permute-start.24
  187.6 5.2 %shard_map.186 = f32[2,128,768]{2,1,0:T(8,128)} custom-call(bf16[32,8192]{1,0:T(8,128)(2,1)} %get-tuple-element.217.x_any, f8e4m3fn[8192,768]{1,0:T(32,128)(4,1)} %shard_map.168.up_any.off_any, bf16[32,768]{1,0:T(8,128)(2,1)} %get-tuple-element.218.grad_any, f32[2,128,768]{2,1,0:T(8,128)} %shard_map.182.refs_0_), custom_call_target="tpu_custom_call", output_to_operand_aliasing={{}: (3, {})} | custom-call | flops 1610612736 | bytes 6291456 | tf_op jit(solution)/shard_map/pallas_call | solution.py:729
  192.9 1.7 collective-permute-start.25
  194.6 0.7 multiply_reduce_fusion.1
  196.0 1.8 collective-permute-done.25
  197.8 0.7 multiply_reduce_fusion
  199.1 0.7 add_convert_fusion.4
  (82 shorter events, 6.0 us)
Async XLA Ops:
  1.5 12.4 %collective-permute-start = (bf16[2,1,8192]{2,1,0:T(2,128)(2,1)S(1)}, bf16[2,1,8192]{2,1,0:T(2,128)(2,1)S(1)}, u32[]{:S(2)}, u32[]{:S(2)}) collective-permute-start(bf16[2,1,8192]{2,1,0:T(2,128)(2,1)S(1)} %pad_maximum_fusion.11), channel_id=1, source_target_pairs={{0,16},{1,17},{2,18},{3,19},{4,20},{5,21},{6,22},{7,23},{8,24},{9,... | collective-permute-start | bytes 98312 | tf_op jit(solution)/shard_map/ppermute | solution.py:760
  9.1 4.8 %copy-start = (bf16[1,8192]{1,0:T(2,128)(2,1)S(1)}, bf16[1,8192]{1,0:T(2,128)(2,1)}, u32[]{:S(2)}) copy-start(bf16[1,8192]{1,0:T(2,128)(2,1)} %param.14) | copy-start | bytes 49156
  9.1 4.8 %copy-start.2 = (bf16[1,8192]{1,0:T(2,128)(2,1)S(1)}, bf16[1,8192]{1,0:T(2,128)(2,1)}, u32[]{:S(2)}) copy-start(bf16[1,8192]{1,0:T(2,128)(2,1)} %param.25) | copy-start | bytes 49156
  14.3 6.4 %collective-permute-start.1 = (bf16[2,2,8192]{2,1,0:T(2,128)(2,1)S(1)}, bf16[2,2,8192]{2,1,0:T(2,128)(2,1)S(1)}, u32[]{:S(2)}, u32[]{:S(2)}) collective-permute-start(bf16[2,2,8192]{2,1,0:T(2,128)(2,1)S(1)} %pad_maximum_fusion.12), channel_id=1, source_target_pairs={{0,8},{1,9},{2,10},{3,11},{4,12},{5,13},{6,14},{7,15},{8,0},{9,1},... | collective-permute-start | bytes 196616 | tf_op jit(solution)/shard_map/ppermute | solution.py:760
  21.4 6.4 %collective-permute-start.2 = (bf16[2,4,8192]{2,1,0:T(4,128)(2,1)S(1)}, bf16[2,4,8192]{2,1,0:T(4,128)(2,1)S(1)}, u32[]{:S(2)}, u32[]{:S(2)}) collective-permute-start(bf16[2,4,8192]{2,1,0:T(4,128)(2,1)S(1)} %pad_maximum_fusion.7), channel_id=1, source_target_pairs={{0,4},{1,5},{2,6},{3,7},{4,0},{5,1},{6,2},{7,3},{8,12},{9,13},{10,... | collective-permute-start | bytes 393224 | tf_op jit(solution)/shard_map/ppermute | solution.py:760
  28.0 7.3 %collective-permute-start.3 = (bf16[2,8,8192]{2,1,0:T(8,128)(2,1)S(1)}, bf16[2,8,8192]{2,1,0:T(8,128)(2,1)S(1)}, u32[]{:S(2)}, u32[]{:S(2)}) collective-permute-start(bf16[2,8,8192]{2,1,0:T(8,128)(2,1)S(1)} %pad_maximum_fusion.4), channel_id=1, source_target_pairs={{0,2},{1,3},{2,0},{3,1},{4,6},{5,7},{6,4},{7,5},{8,10},{9,11},{10,... | collective-permute-start | bytes 786440 | tf_op jit(solution)/shard_map/ppermute | solution.py:760
  35.5 2.0 collective-permute-start.4
  55.9 1.8 collective-permute-start.5
  58.7 6.4 %collective-permute-start.6 = (bf16[8,8192]{1,0:T(8,128)(2,1)S(1)}, bf16[8,8192]{1,0:T(8,128)(2,1)S(1)}, u32[]{:S(2)}, u32[]{:S(2)}) collective-permute-start(bf16[8,8192]{1,0:T(8,128)(2,1)S(1)} %dynamic-slice_convert_fusion.2), channel_id=1, source_target_pairs={{0,2},{1,3},{2,0},{3,1},{4,6},{5,7},{6,4},{7,5},{8,10},{9,11},{10,... | collective-permute-start | bytes 393224 | tf_op jit(solution)/shard_map/ppermute | solution.py:760
  65.2 5.8 %collective-permute-start.7 = (bf16[4,8192]{1,0:T(4,128)(2,1)S(1)}, bf16[4,8192]{1,0:T(4,128)(2,1)S(1)}, u32[]{:S(2)}, u32[]{:S(2)}) collective-permute-start(bf16[4,8192]{1,0:T(4,128)(2,1)S(1)} %dynamic-slice_convert_fusion.5), channel_id=1, source_target_pairs={{0,4},{1,5},{2,6},{3,7},{4,0},{5,1},{6,2},{7,3},{8,12},{9,13},{10,... | collective-permute-start | bytes 196616 | tf_op jit(solution)/shard_map/ppermute | solution.py:760
  71.1 5.7 %collective-permute-start.8 = (bf16[4,8192]{1,0:T(4,128)(2,1)S(1)}, bf16[4,8192]{1,0:T(4,128)(2,1)S(1)}, u32[]{:S(2)}, u32[]{:S(2)}) collective-permute-start(bf16[4,8192]{1,0:T(4,128)(2,1)S(1)} %add_convert_fusion.3), channel_id=1, source_target_pairs={{0,8},{1,9},{2,10},{3,11},{4,12},{5,13},{6,14},{7,15},{8,0},{9,1},... | collective-permute-start | bytes 196616 | tf_op jit(solution)/shard_map/ppermute | solution.py:760
  76.9 5.3 %collective-permute-start.9 = (bf16[4,8192]{1,0:T(4,128)(2,1)S(1)}, bf16[4,8192]{1,0:T(4,128)(2,1)S(1)}, u32[]{:S(2)}, u32[]{:S(2)}) collective-permute-start(bf16[4,8192]{1,0:T(4,128)(2,1)S(1)} %add_convert_fusion.2), channel_id=1, source_target_pairs={{0,16},{1,17},{2,18},{3,19},{4,20},{5,21},{6,22},{7,23},{8,24},{9,... | collective-permute-start | bytes 196616 | tf_op jit(solution)/shard_map/ppermute | solution.py:760
  82.5 6.3 %collective-permute-start.10 = (bf16[4,8192]{1,0:T(4,128)(2,1)S(1)}, bf16[4,8192]{1,0:T(4,128)(2,1)S(1)}, u32[]{:S(2)}, u32[]{:S(2)}) collective-permute-start(bf16[4,8192]{1,0:T(4,128)(2,1)S(1)} %fusion.8), channel_id=1, source_target_pairs={{0,4},{1,5},{2,6},{3,7},{4,0},{5,1},{6,2},{7,3},{8,12},{9,13},{10,... | collective-permute-start | bytes 196616 | tf_op jit(solution)/shard_map/ppermute | solution.py:760
  89.0 5.5 %collective-permute-start.11 = (bf16[8,8192]{1,0:T(8,128)(2,1)S(1)}, bf16[8,8192]{1,0:T(8,128)(2,1)S(1)}, u32[]{:S(2)}, u32[]{:S(2)}) collective-permute-start(bf16[8,8192]{1,0:T(8,128)(2,1)S(1)} %pad_maximum_fusion.8), channel_id=1, source_target_pairs={{0,2},{1,3},{2,0},{3,1},{4,6},{5,7},{6,4},{7,5},{8,10},{9,11},{10,... | collective-permute-start | bytes 393224 | tf_op jit(solution)/shard_map/ppermute | solution.py:760
  94.7 1.6 collective-permute-start.12
  117.9 1.8 collective-permute-start.13
  120.7 5.6 %collective-permute-start.14 = (bf16[8,8192]{1,0:T(8,128)(2,1)S(1)}, bf16[8,8192]{1,0:T(8,128)(2,1)S(1)}, u32[]{:S(2)}, u32[]{:S(2)}) collective-permute-start(bf16[8,8192]{1,0:T(8,128)(2,1)S(1)} %dynamic-slice_convert_fusion.1), channel_id=1, source_target_pairs={{0,2},{1,3},{2,0},{3,1},{4,6},{5,7},{6,4},{7,5},{8,10},{9,11},{10,... | collective-permute-start | bytes 393224 | tf_op jit(solution)/shard_map/ppermute | solution.py:760
  126.4 4.3 %collective-permute-start.15 = (bf16[4,8192]{1,0:T(4,128)(2,1)S(1)}, bf16[4,8192]{1,0:T(4,128)(2,1)S(1)}, u32[]{:S(2)}, u32[]{:S(2)}) collective-permute-start(bf16[4,8192]{1,0:T(4,128)(2,1)S(1)} %dynamic-slice_convert_fusion.4), channel_id=1, source_target_pairs={{0,4},{1,5},{2,6},{3,7},{4,0},{5,1},{6,2},{7,3},{8,12},{9,13},{10,... | collective-permute-start | bytes 196616 | tf_op jit(solution)/shard_map/ppermute | solution.py:760
  130.8 5.2 %collective-permute-start.16 = (bf16[4,8192]{1,0:T(4,128)(2,1)S(1)}, bf16[4,8192]{1,0:T(4,128)(2,1)S(1)}, u32[]{:S(2)}, u32[]{:S(2)}) collective-permute-start(bf16[4,8192]{1,0:T(4,128)(2,1)S(1)} %add_convert_fusion.1), channel_id=1, source_target_pairs={{0,8},{1,9},{2,10},{3,11},{4,12},{5,13},{6,14},{7,15},{8,0},{9,1},... | collective-permute-start | bytes 196616 | tf_op jit(solution)/shard_map/ppermute | solution.py:760
  136.0 6.1 %collective-permute-start.17 = (bf16[4,8192]{1,0:T(4,128)(2,1)S(1)}, bf16[4,8192]{1,0:T(4,128)(2,1)S(1)}, u32[]{:S(2)}, u32[]{:S(2)}) collective-permute-start(bf16[4,8192]{1,0:T(4,128)(2,1)S(1)} %add_convert_fusion), channel_id=1, source_target_pairs={{0,16},{1,17},{2,18},{3,19},{4,20},{5,21},{6,22},{7,23},{8,24},{9,... | collective-permute-start | bytes 196616 | tf_op jit(solution)/shard_map/ppermute | solution.py:760
  142.6 4.9 %collective-permute-start.18 = (bf16[4,8192]{1,0:T(4,128)(2,1)S(1)}, bf16[4,8192]{1,0:T(4,128)(2,1)S(1)}, u32[]{:S(2)}, u32[]{:S(2)}) collective-permute-start(bf16[4,8192]{1,0:T(4,128)(2,1)S(1)} %fusion.13), channel_id=1, source_target_pairs={{0,4},{1,5},{2,6},{3,7},{4,0},{5,1},{6,2},{7,3},{8,12},{9,13},{10,... | collective-permute-start | bytes 196616 | tf_op jit(solution)/shard_map/ppermute | solution.py:760
  147.6 5.0 %collective-permute-start.19 = (bf16[8,8192]{1,0:T(8,128)(2,1)S(1)}, bf16[8,8192]{1,0:T(8,128)(2,1)S(1)}, u32[]{:S(2)}, u32[]{:S(2)}) collective-permute-start(bf16[8,8192]{1,0:T(8,128)(2,1)S(1)} %pad_maximum_fusion.9), channel_id=1, source_target_pairs={{0,2},{1,3},{2,0},{3,1},{4,6},{5,7},{6,4},{7,5},{8,10},{9,11},{10,... | collective-permute-start | bytes 393224 | tf_op jit(solution)/shard_map/ppermute | solution.py:760
  152.8 1.6 collective-permute-start.20
  169.9 1.8 collective-permute-start.21
  172.7 7.9 %collective-permute-start.22 = (bf16[8,8192]{1,0:T(8,128)(2,1)S(1)}, bf16[8,8192]{1,0:T(8,128)(2,1)S(1)}, u32[]{:S(2)}, u32[]{:S(2)}) collective-permute-start(bf16[8,8192]{1,0:T(8,128)(2,1)S(1)} %dynamic-slice_convert_fusion), channel_id=1, source_target_pairs={{0,2},{1,3},{2,0},{3,1},{4,6},{5,7},{6,4},{7,5},{8,10},{9,11},{10,... | collective-permute-start | bytes 393224 | tf_op jit(solution)/shard_map/ppermute | solution.py:760
  180.7 6.0 %collective-permute-start.23 = (bf16[4,8192]{1,0:T(4,128)(2,1)S(1)}, bf16[4,8192]{1,0:T(4,128)(2,1)S(1)}, u32[]{:S(2)}, u32[]{:S(2)}) collective-permute-start(bf16[4,8192]{1,0:T(4,128)(2,1)S(1)} %dynamic-slice_convert_fusion.3), channel_id=1, source_target_pairs={{0,4},{1,5},{2,6},{3,7},{4,0},{5,1},{6,2},{7,3},{8,12},{9,13},{10,... | collective-permute-start | bytes 196616 | tf_op jit(solution)/shard_map/ppermute | solution.py:760
  186.7 11.1 %copy-start.1 = (f32[2,8192]{1,0:T(2,128)S(1)}, f32[2,8192]{1,0:T(2,128)}, u32[]{:S(2)}) copy-start(f32[2,8192]{1,0:T(2,128)} %param.15) | copy-start | bytes 196612
  186.8 6.0 %collective-permute-start.24 = (bf16[2,8192]{1,0:T(2,128)(2,1)S(1)}, bf16[2,8192]{1,0:T(2,128)(2,1)S(1)}, u32[]{:S(2)}, u32[]{:S(2)}) collective-permute-start(bf16[2,8192]{1,0:T(2,128)(2,1)S(1)} %dynamic-slice_convert_fusion.6), channel_id=1, source_target_pairs={{0,8},{1,9},{2,10},{3,11},{4,12},{5,13},{6,14},{7,15},{8,0},{9,1},... | collective-permute-start | bytes 98312 | tf_op jit(solution)/shard_map/ppermute | solution.py:760
  192.9 4.9 %collective-permute-start.25 = (bf16[1,8192]{1,0:T(2,128)(2,1)S(1)}, bf16[1,8192]{1,0:T(2,128)(2,1)S(1)}, u32[]{:S(2)}, u32[]{:S(2)}) collective-permute-start(bf16[1,8192]{1,0:T(2,128)(2,1)S(1)} %dynamic-slice_convert_fusion.7), channel_id=1, source_target_pairs={{0,16},{1,17},{2,18},{3,19},{4,20},{5,21},{6,22},{7,23},{8,24},{9,... | collective-permute-start | bytes 49160 | tf_op jit(solution)/shard_map/ppermute | solution.py:757

commit v4 on v3

--- a/solution.py
+++ b/solution.py
@@ -84,11 +84,11 @@
     lax.fori_loop(0, count, step, 0)
 
 
-def offsets_kernel(layer, half, *refs):
+def offsets_kernel(layer, half, halves, *refs):
     code_any, zero_any = refs[:2]
     out_any, code, zero, out, planes, sems = refs[-6:]
     words, width = code.shape
-    count = COUNT
+    count = 2 * COUNT // halves
     rows = words // count
     groups = rows // WORDS
     tile = planes.shape[-1]
@@ -132,25 +132,25 @@
         out_copy(chunk).wait()
 
 
-def offsets_of(codes, zeros, layer, earlier=None):
+def offsets_of(codes, zeros, layer, earlier=None, halves=2):
     _, words, width = codes.shape
     tile = 128 if width % 128 == 0 else 64
     operands = [codes, zeros] if earlier is None else [codes, zeros, earlier]
     return pl.pallas_call(
-        functools.partial(offsets_kernel, layer, 0 if earlier is None else 1),
+        functools.partial(offsets_kernel, layer, 0 if earlier is None else 1, halves),
         in_specs=[IN_HBM] * len(operands),
         out_specs=IN_HBM,
         out_shape=jax.ShapeDtypeStruct((words * 4, width), OFFSET),
         scratch_shapes=[
-            pltpu.VMEM((words // 2, width), jnp.int32),
-            pltpu.VMEM((zeros.shape[1] // 2, width), jnp.int32),
-            pltpu.VMEM((words * 2, width), OFFSET),
+            pltpu.VMEM((words // halves, width), jnp.int32),
+            pltpu.VMEM((zeros.shape[1] // halves, width), jnp.int32),
+            pltpu.VMEM((words * 4 // halves, width), OFFSET),
             pltpu.VMEM((8, GROUP, tile), F32),
-            pltpu.SemaphoreType.DMA((2 * COUNT + 1,)),
+            pltpu.SemaphoreType.DMA((4 * COUNT // halves + 1,)),
         ],
         input_output_aliases={} if earlier is None else {2: 0},
         compiler_params=params(),
-        cost_estimate=cost(words * width * 20, words * width * 4),
+        cost_estimate=cost(words * width * 40 // halves, words * width * 8 // halves),
     )(*operands)
 
 
@@ -256,8 +256,8 @@
 def weights_of(offsets, steps):
     parts = []
     for group, step in enumerate(steps):
-        part = offsets[group * GROUP : (group + 1) * GROUP].astype(F32)
-        parts.append((part * step).astype(BF16))
+        part = offsets[group * GROUP : (group + 1) * GROUP].astype(BF16)
+        parts.append(part * jnp.broadcast_to(step, part.shape).astype(BF16))
     return jnp.concatenate(parts, axis=0)
 
 
@@ -768,16 +768,22 @@
 
 
 def halve_first(side, kept, sent, bit):
-    return kept.astype(F32) + side.swap(sent, bit).astype(F32)
-
-
-def halve(side, value, bit):
-    half = value.shape[0] // 2
+    return kept, side.swap(sent, bit)
+
+
+def halve(side, terms, bit):
+    half = terms[0].shape[0] // 2
     mine = own_bit(bit)
-    kept = lax.dynamic_slice_in_dim(value, mine * half, half, 0)
-    sent = lax.dynamic_slice_in_dim(value, (1 - mine) * half, half, 0)
-    got = side.swap(sent.astype(BF16), bit)
-    return kept.astype(F32) + got.astype(F32)
+
+    def part(place):
+        one, other = (lax.dynamic_slice_in_dim(term, place * half, half, 0) for term in terms)
+        return one.astype(F32) + other.astype(F32)
+
+    return part(mine), side.swap(part(1 - mine).astype(BF16), bit)
+
+
+def total(terms):
+    return terms[0].astype(F32) + terms[1].astype(F32)
 
 
 def add_up(side, value, bit):
@@ -867,9 +873,10 @@
         call = lambda c, z, earlier: unpack_half(c, z, layer, earlier)
         return [(call, (codes, zeros), results)] * 2, results
 
+    whole = functools.partial(offsets_of, halves=1)
     gate_jobs, gate_0 = offsets_jobs(gate_codes, gate_zero, 0)
-    up_jobs, up_0 = offsets_jobs(up_codes, up_zero, 0)
-    side = Side(*gate_jobs, *up_jobs)
+    up_jobs, up_0 = offsets_jobs(up_codes, up_zero, 0, whole)
+    side = Side(None, *gate_jobs, up_jobs[0])
     pair = jnp.stack([tokens, out_grad])
     for bit in reversed(far):
         pair = double(side, pair, bit, 1)
@@ -893,6 +900,7 @@
     part = halve_first(side, kept, sent, near[0])
     for bit in near[1:]:
         part = halve(side, part, bit)
+    part = total(part)
     for bit in far:
         part = add_up(side, part, bit)
     state_1 = (state_0.astype(F32) + part).astype(BF16)
@@ -926,6 +934,7 @@
     part = halve_first(side, kept, sent, near[0])
     for bit in near[1:]:
         part = halve(side, part, bit)
+    part = total(part)
     for bit in far:
         part = add_up(side, part, bit)
     cot_rows = (cot_rows.astype(F32) + norm_back(state_1, norm_gain[1], part)).astype(BF16)
@@ -960,11 +969,14 @@
             (normed_0, gate_grad),
             gate_out,
         ),
-        (
-            lambda x, u, earlier: step_grad(x, up_0, u, 0, 0, 1, earlier),
-            (normed_0, up_grad),
-            up_out,
-        ),
+        *[
+            (
+                lambda x, u, earlier, half=half: step_grad(x, up_0, u, 0, half, 2, earlier),
+                (normed_0, up_grad),
+                up_out,
+            )
+            for half in range(2)
+        ],
     )
     part = halve_first(side, kept, sent, near[0])
     for bit in near[1:]:
@@ -973,6 +985,7 @@
         part = halve(side, part, bit)
         half = cot_rows.shape[0] // 2
         cot_rows = lax.dynamic_slice_in_dim(cot_rows, own_bit(bit) * half, half, 0)
+    part = total(part)
     result = (cot_rows.astype(F32) + norm_back(tokens, norm_gain[0], part)).astype(BF16)
     return result, gate_out["value"], up_out["value"], down_out["value"].transpose(1, 0, 2)
 

time: 201 us -> 196 us (0.975)
  starting transfers between devices: 28.7 us -> 25.4 us
    ppermute x19, starting transfers between devices: 26.2 us -> 20.5 us  [swap(): got = lax.ppermute(value, 'tensor', pairs)]
    convert_element_type x0 -> x7, other arithmetic: none -> 3.39 us  [halve(): return (part(mine), side.swap(part(1 - mine).astype(BF16), bit))]
    add x8 -> x1, other arithmetic: 3.18 us -> 0.12 us  [part(): return one.astype(F32) + other.astype(F32)]
    ppermute x7, waiting for transfers between devices: 11.6 us -> 8.53 us  [swap(): return lax.ppermute(value, 'tensor', pairs)]
    ppermute x19, waiting for transfers between devices: 2.05 us -> 4.83 us  [swap(): got = lax.ppermute(value, 'tensor', pairs)]
    ppermute x7, starting transfers between devices: 2.5 us -> 4.92 us  [swap(): return lax.ppermute(value, 'tensor', pairs)]
    pallas_call x8 -> x7, Pallas kernels: 38.2 us -> 36 us  [offsets_of(): pl.pallas_call(functools.partial(offsets_kernel, layer, 0 if earlier is N...]
    pallas_call x9 -> x10, Pallas kernels: 38 us -> 39.8 us  [step_grad(): pl.pallas_call(functools.partial(step_grad_kernel, by_rows, half, halves)...]
  transfers between devices with their start and end apart: 26 -> 26, of which waited for: 12 -> 14; matrix products, arithmetic and copies ran while one was open for 2% -> 2% of each run, Pallas kernels for 43% -> 44%
where the time goes in v4:
time: 196 us; the launch traced here: 195 us
  Pallas kernels  137 us (70%)
  starting transfers between devices  25.4 us (13%)
  other arithmetic  15.1 us (8%)
  waiting for transfers between devices  13.4 us (7%)
  between operations  2.55 us (1%)
    pallas_call x10, Pallas kernels, step_grad(): pl.pallas_call(functools.partial(step_grad_kernel, by_rows, half, halves)...  39.8 us
    pallas_call x7, Pallas kernels, offsets_of(): pl.pallas_call(functools.partial(offsets_kernel, layer, 0 if earlier is N...  36 us
    ppermute x19, starting transfers between devices, swap(): got = lax.ppermute(value, 'tensor', pairs)  20.5 us
    pallas_call x1, Pallas kernels, last_layer(): pl.pallas_call(functools.partial(last_layer_kernel, layer), in_specs=[SCA...  20.1 us
    pallas_call x1, Pallas kernels, first_forward(): pl.pallas_call(functools.partial(first_forward_kernel, layer), in_specs=[...  16 us
    pallas_call x1, Pallas kernels, backward(): pl.pallas_call(functools.partial(backward_kernel, layer), in_specs=[SCALA...  14.6 us
    pallas_call x2, Pallas kernels, down_offsets_of(): pl.pallas_call(functools.partial(down_offsets_kernel, layer, 0 if earlier...  10.4 us
    ppermute x7, waiting for transfers between devices, swap(): return lax.ppermute(value, 'tensor', pairs)  8.53 us
  transfers between devices with their start and end apart: 26, of which 14 were waited for; matrix products, arithmetic and copies ran while one was open for 2% of the time, Pallas kernels for 44%

profile of v4, /device:TPU:0, one launch (start us, length us, event | category | flops | bytes accessed | tf_op | source)
XLA Modules:
  0.0 195.2 jit_solution(11411877810144528509)
XLA Ops:
  0.6 0.9 pad_maximum_fusion.11
  1.5 4.1 %collective-permute-start = (bf16[2,1,8192]{2,1,0:T(2,128)(2,1)S(1)}, bf16[2,1,8192]{2,1,0:T(2,128)(2,1)S(1)}, u32[]{:S(2)}, u32[]{:S(2)}) collective-permute-start(bf16[2,1,8192]{2,1,0:T(2,128)(2,1)S(1)} %pad_maximum_fusion.11), channel_id=1, source_target_pairs={{0,16},{1,17},{2,18},{3,19},{4,20},{5,21},{6,22},{7,23},{8,24},{9,... | collective-permute-start | bytes 98312 | tf_op jit(solution)/shard_map/ppermute | solution.py:757
  5.6 0.7 and_select_fusion.1
  6.3 0.7 and_select_fusion
  7.0 0.8 copy.28
  7.8 1.0 fusion.25
  9.3 1.0 broadcast_select_fusion.15
  10.4 1.5 collective-permute-start.1
  11.9 4.8 %shard_map.165.refs_2_ = f8e4m3fn[8192,768]{1,0:T(32,128)(4,1)} custom-call(s32[2,2048,768]{2,1,0:T(8,128)} %refs_0_.6, s32[2,128,768]{2,1,0:T(8,128)} %refs_1_.4), custom_call_target="tpu_custom_call" | custom-call | flops 31457280 | bytes 6291456 | tf_op jit(solution)/shard_map/pallas_call | solution.py:139
  17.4 1.6 collective-permute-start.2
  18.9 4.8 %shard_map.166.gate_any.off_any = f8e4m3fn[8192,768]{1,0:T(32,128)(4,1)} custom-call(s32[2,2048,768]{2,1,0:T(8,128)} %refs_0_.6, s32[2,128,768]{2,1,0:T(8,128)} %refs_1_.4, f8e4m3fn[8192,768]{1,0:T(32,128)(4,1)} %shard_map.165.refs_2_), custom_call_target="tpu_custom_call", output_to_operand_aliasing={{}: (2, {})} | custom-call | flops 31457280 | bytes 6291456 | tf_op jit(solution)/shard_map/pallas_call | solution.py:139
  24.1 1.6 collective-permute-start.3
  25.6 7.4 %shard_map.167.up_any.off_any = f8e4m3fn[8192,768]{1,0:T(32,128)(4,1)} custom-call(s32[2,2048,768]{2,1,0:T(8,128)} %refs_0_.8, s32[2,128,768]{2,1,0:T(8,128)} %refs_1_.6), custom_call_target="tpu_custom_call" | custom-call | flops 62914560 | bytes 12582912 | tf_op jit(solution)/shard_map/pallas_call | solution.py:139
  33.4 1.9 collective-permute-done.4
  35.5 1.0 fusion.2
  36.5 16.0 %shard_map.168 = (f32[32,768]{1,0:T(8,128)}, f32[32,768]{1,0:T(8,128)}, bf16[32,768]{1,0:T(8,128)(2,1)}, bf16[16,8192]{1,0:T(8,128)(2,1)}, bf16[16,8192]{1,0:T(8,128)(2,1)}, /*index=5*/f8e4m3fn[768,8192]{1,0:T(32,128)(4,1)}) custom-call(s32[1]{0:T(128)} %bitcast.4.mine, bf16[32,8192]{1,0:T(8,128)(2,1)} %get-tuple-element.217.x_any, ...), custom_call_target="tpu_custom_call" | custom-call | flops 1207959552 | bytes 25165824 | tf_op jit(solution)/shard_map/pallas_call | solution.py:498
  52.7 1.6 collective-permute-done.5
  54.4 1.0 add_convert_fusion.2
  55.4 0.6 collective-permute-start.6
  56.0 4.8 %shard_map.169.refs_2_ = f8e4m3fn[8192,768]{1,0:T(32,128)(4,1)} custom-call(s32[2,2048,768]{2,1,0:T(8,128)} %refs_0_.6, s32[2,128,768]{2,1,0:T(8,128)} %refs_1_.4), custom_call_target="tpu_custom_call" | custom-call | flops 31457280 | bytes 6291456 | tf_op jit(solution)/shard_map/pallas_call | solution.py:139
  61.1 0.6 collective-permute-start.7
  61.6 5.2 %shard_map.170.refs_2_ = f8e4m3fn[768,8192]{1,0:T(32,128)(4,1)} custom-call(s32[2,192,8192]{2,1,0:T(8,128)} %refs_0_.5, s32[12,2,8192]{2,1,0:T(2,128)} %bitcast.32), custom_call_target="tpu_custom_call" | custom-call | flops 31457280 | bytes 6291456 | tf_op jit(solution)/shard_map/pallas_call | solution.py:236
  67.0 0.9 collective-permute-start.8
  67.8 5.2 %shard_map.171.down_any.off_any = f8e4m3fn[768,8192]{1,0:T(32,128)(4,1)} custom-call(s32[2,192,8192]{2,1,0:T(8,128)} %refs_0_.5, s32[12,2,8192]{2,1,0:T(2,128)} %bitcast.33, f8e4m3fn[768,8192]{1,0:T(32,128)(4,1)} %shard_map.170.refs_2_), custom_call_target="tpu_custom_call", output_to_operand_aliasing={{}: (2, {})} | custom-call | flops 31457280 | bytes 6291456 | tf_op jit(solution)/shard_map/pallas_call | solution.py:236
  73.1 1.8 collective-permute-start.9
  74.9 4.7 %shard_map.172.gate_any.off_any = f8e4m3fn[8192,768]{1,0:T(32,128)(4,1)} custom-call(s32[2,2048,768]{2,1,0:T(8,128)} %refs_0_.6, s32[2,128,768]{2,1,0:T(8,128)} %refs_1_.4, f8e4m3fn[8192,768]{1,0:T(32,128)(4,1)} %shard_map.169.refs_2_), custom_call_target="tpu_custom_call", output_to_operand_aliasing={{}: (2, {})} | custom-call | flops 31457280 | bytes 6291456 | tf_op jit(solution)/shard_map/pallas_call | solution.py:139
  80.0 1.6 collective-permute-start.10
  81.5 4.7 %shard_map.173.refs_2_ = f8e4m3fn[8192,768]{1,0:T(32,128)(4,1)} custom-call(s32[2,2048,768]{2,1,0:T(8,128)} %refs_0_.8, s32[2,128,768]{2,1,0:T(8,128)} %refs_1_.6), custom_call_target="tpu_custom_call" | custom-call | flops 31457280 | bytes 6291456 | tf_op jit(solution)/shard_map/pallas_call | solution.py:139
  86.5 1.3 collective-permute-start.11
  87.9 4.8 %shard_map.174.up_any.off_any = f8e4m3fn[8192,768]{1,0:T(32,128)(4,1)} custom-call(s32[2,2048,768]{2,1,0:T(8,128)} %refs_0_.8, s32[2,128,768]{2,1,0:T(8,128)} %refs_1_.6, f8e4m3fn[8192,768]{1,0:T(32,128)(4,1)} %shard_map.173.refs_2_), custom_call_target="tpu_custom_call", output_to_operand_aliasing={{}: (2, {})} | custom-call | flops 31457280 | bytes 6291456 | tf_op jit(solution)/shard_map/pallas_call | solution.py:139
  92.9 1.5 collective-permute-done.12
  94.5 0.8 pad_maximum_fusion.2.x_any
  95.3 20.1 %shard_map.175 = (bf16[32,768]{1,0:T(8,128)(2,1)}, bf16[32,768]{1,0:T(8,128)(2,1)}, bf16[32,768]{1,0:T(8,128)(2,1)}, bf16[16,8192]{1,0:T(8,128)(2,1)}, bf16[16,8192]{1,0:T(8,128)(2,1)}) custom-call(s32[1]{0:T(128)} %bitcast.4.mine, bf16[32,8192]{1,0:T(8,128)(2,1)} %pad_maximum_fusion.2.x_any, bf16[32,8192]{1,0:T(8,128)(2,1)} %get-tuple-element.170.cot_any.grad_any, ...), custom_call_target="tpu_custom_call" | custom-call | flops 2013265920 | bytes 25165824 | tf_op jit(solution)/shard_map/pallas_call | solution.py:552
  115.6 1.6 collective-permute-done.13
  117.2 1.0 add_convert_fusion.1
  118.3 0.8 collective-permute-start.14
  119.1 3.5 %shard_map.176.refs_0_ = f32[12,8192]{1,0:T(8,128)} custom-call(bf16[32,768]{1,0:T(8,128)(2,1)} %get-tuple-element.169.x_any, f8e4m3fn[768,8192]{1,0:T(32,128)(4,1)} %shard_map.171.down_any.off_any, bf16[32,8192]{1,0:T(8,128)(2,1)} %get-tuple-element.170.cot_any.grad_any), custom_call_target="tpu_custom_call" | custom-call | flops 805306368 | bytes 3145728 | tf_op jit(solution)/shard_map/pallas_call | solution.py:729
  122.6 1.3 collective-permute-done.14
  123.9 0.6 collective-permute-start.15
  124.5 3.5 %shard_map.177.refs_0_ = f32[12,8192]{1,0:T(8,128)} custom-call(bf16[32,768]{1,0:T(8,128)(2,1)} %get-tuple-element.169.x_any, f8e4m3fn[768,8192]{1,0:T(32,128)(4,1)} %shard_map.171.down_any.off_any, bf16[32,8192]{1,0:T(8,128)(2,1)} %get-tuple-element.170.cot_any.grad_any, f32[12,8192]{1,0:T(8,128)} %shard_map.176.refs_0_), custom_call_target="tpu_custom_call", output_to_operand_aliasing={{}: (3, {})} | custom-call | flops 805306368 | bytes 3145728 | tf_op jit(solution)/shard_map/pallas_call | solution.py:729
  128.4 2.1 %collective-permute-start.16 = (bf16[4,8192]{1,0:T(4,128)(2,1)S(1)}, bf16[4,8192]{1,0:T(4,128)(2,1)S(1)}, u32[]{:S(2)}, u32[]{:S(2)}) collective-permute-start(bf16[4,8192]{1,0:T(4,128)(2,1)S(1)} %add_convert_fusion.5), channel_id=1, source_target_pairs={{0,8},{1,9},{2,10},{3,11},{4,12},{5,13},{6,14},{7,15},{8,0},{9,1},... | collective-permute-start | bytes 196616 | tf_op jit(solution)/shard_map/ppermute | solution.py:760
  130.4 3.5 %shard_map.178.refs_0_ = f32[2,128,768]{2,1,0:T(8,128)} custom-call(bf16[32,8192]{1,0:T(8,128)(2,1)} %pad_maximum_fusion.2.x_any, f8e4m3fn[8192,768]{1,0:T(32,128)(4,1)} %shard_map.172.gate_any.off_any, bf16[32,768]{1,0:T(8,128)(2,1)} %get-tuple-element.180.grad_any), custom_call_target="tpu_custom_call" | custom-call | flops 805306368 | bytes 3145728 | tf_op jit(solution)/shard_map/pallas_call | solution.py:729
  134.0 0.6 collective-permute-start.17
  134.7 3.5 %shard_map.179.refs_0_ = f32[2,128,768]{2,1,0:T(8,128)} custom-call(bf16[32,8192]{1,0:T(8,128)(2,1)} %pad_maximum_fusion.2.x_any, f8e4m3fn[8192,768]{1,0:T(32,128)(4,1)} %shard_map.172.gate_any.off_any, bf16[32,768]{1,0:T(8,128)(2,1)} %get-tuple-element.180.grad_any, f32[2,128,768]{2,1,0:T(8,128)} %shard_map.178.refs_0_), custom_call_target="tpu_custom_call", output_to_operand_aliasing={{}: (3, {})} | custom-call | flops 805306368 | bytes 3145728 | tf_op jit(solution)/shard_map/pallas_call | solution.py:729
  138.2 1.8 collective-permute-done.17
  140.4 1.3 collective-permute-start.18
  141.8 3.5 %shard_map.180.refs_0_ = f32[2,128,768]{2,1,0:T(8,128)} custom-call(bf16[32,8192]{1,0:T(8,128)(2,1)} %pad_maximum_fusion.2.x_any, f8e4m3fn[8192,768]{1,0:T(32,128)(4,1)} %shard_map.174.up_any.off_any, bf16[32,768]{1,0:T(8,128)(2,1)} %get-tuple-element.190.grad_any), custom_call_target="tpu_custom_call" | custom-call | flops 805306368 | bytes 3145728 | tf_op jit(solution)/shard_map/pallas_call | solution.py:729
  145.4 0.8 collective-permute-start.19
  146.2 3.5 %shard_map.181.refs_0_ = f32[2,128,768]{2,1,0:T(8,128)} custom-call(bf16[32,8192]{1,0:T(8,128)(2,1)} %pad_maximum_fusion.2.x_any, f8e4m3fn[8192,768]{1,0:T(32,128)(4,1)} %shard_map.174.up_any.off_any, bf16[32,768]{1,0:T(8,128)(2,1)} %get-tuple-element.190.grad_any, f32[2,128,768]{2,1,0:T(8,128)} %shard_map.180.refs_0_), custom_call_target="tpu_custom_call", output_to_operand_aliasing={{}: (3, {})} | custom-call | flops 805306368 | bytes 3145728 | tf_op jit(solution)/shard_map/pallas_call | solution.py:729
  149.8 0.7 collective-permute-done.19
  150.7 1.5 collective-permute-done.20
  152.3 0.9 pad_maximum_fusion.3.cot_any.grad_any
  153.2 14.6 %shard_map.182 = (bf16[32,768]{1,0:T(8,128)(2,1)}, bf16[32,768]{1,0:T(8,128)(2,1)}, bf16[16,8192]{1,0:T(8,128)(2,1)}, bf16[16,8192]{1,0:T(8,128)(2,1)}) custom-call(s32[1]{0:T(128)} %bitcast.4.mine, bf16[32,8192]{1,0:T(8,128)(2,1)} %pad_maximum_fusion.3.cot_any.grad_any, f32[32,768]{1,0:T(8,128)} %get-tuple-element.193.pre_any, ...), custom_call_target="tpu_custom_call" | custom-call | flops 1207959552 | bytes 18874368 | tf_op jit(solution)/shard_map/pallas_call | solution.py:619
  168.0 0.7 multiply_reduce_fusion.1
  169.6 1.0 add_convert_fusion
  170.6 0.8 collective-permute-start.22
  171.4 6.5 %shard_map.183 = f32[12,2,8192]{2,1,0:T(2,128)} custom-call(bf16[32,768]{1,0:T(8,128)(2,1)} %get-tuple-element.200.x_any, f8e4m3fn[768,8192]{1,0:T(32,128)(4,1)} %get-tuple-element.195.down_any.off_any, bf16[32,8192]{1,0:T(8,128)(2,1)} %pad_maximum_fusion.3.cot_any.grad_any, f32[12,8192]{1,0:T(8,128)} %shard_map.177.refs_0_), custom_call_target="tpu_custom_call" | custom-call | flops 1610612736 | bytes 6291456 | tf_op jit(solution)/shard_map/pallas_call | solution.py:729
  178.0 0.8 collective-permute-start.23
  178.8 5.2 %shard_map.184 = f32[2,128,768]{2,1,0:T(8,128)} custom-call(bf16[32,8192]{1,0:T(8,128)(2,1)} %get-tuple-element.217.x_any, f8e4m3fn[8192,768]{1,0:T(32,128)(4,1)} %shard_map.166.gate_any.off_any, bf16[32,768]{1,0:T(8,128)(2,1)} %get-tuple-element.207.grad_any, f32[2,128,768]{2,1,0:T(8,128)} %shard_map.179.refs_0_), custom_call_target="tpu_custom_call", output_to_operand_aliasing={{}: (3, {})} | custom-call | flops 1610612736 | bytes 6291456 | tf_op jit(solution)/shard_map/pallas_call | solution.py:729
  184.4 3.5 %shard_map.185.refs_0_ = f32[2,128,768]{2,1,0:T(8,128)} custom-call(bf16[32,8192]{1,0:T(8,128)(2,1)} %get-tuple-element.217.x_any, f8e4m3fn[8192,768]{1,0:T(32,128)(4,1)} %shard_map.167.up_any.off_any, bf16[32,768]{1,0:T(8,128)(2,1)} %get-tuple-element.218.grad_any, f32[2,128,768]{2,1,0:T(8,128)} %shard_map.181.refs_0_), custom_call_target="tpu_custom_call", output_to_operand_aliasing={{}: (3, {})} | custom-call | flops 805306368 | bytes 3145728 | tf_op jit(solution)/shard_map/pallas_call | solution.py:729
  188.2 1.0 collective-permute-start.25
  189.3 3.5 %shard_map.186 = f32[2,128,768]{2,1,0:T(8,128)} custom-call(bf16[32,8192]{1,0:T(8,128)(2,1)} %get-tuple-element.217.x_any, f8e4m3fn[8192,768]{1,0:T(32,128)(4,1)} %shard_map.167.up_any.off_any, bf16[32,768]{1,0:T(8,128)(2,1)} %get-tuple-element.218.grad_any, f32[2,128,768]{2,1,0:T(8,128)} %shard_map.185.refs_0_), custom_call_target="tpu_custom_call", output_to_operand_aliasing={{}: (3, {})} | custom-call | flops 805306368 | bytes 3145728 | tf_op jit(solution)/shard_map/pallas_call | solution.py:729
  193.1 0.7 multiply_reduce_fusion
  194.5 0.7 add_convert_fusion.11
  (72 shorter events, 6.6 us)
Async XLA Ops:
  1.5 7.8 %collective-permute-start = (bf16[2,1,8192]{2,1,0:T(2,128)(2,1)S(1)}, bf16[2,1,8192]{2,1,0:T(2,128)(2,1)S(1)}, u32[]{:S(2)}, u32[]{:S(2)}) collective-permute-start(bf16[2,1,8192]{2,1,0:T(2,128)(2,1)S(1)} %pad_maximum_fusion.11), channel_id=1, source_target_pairs={{0,16},{1,17},{2,18},{3,19},{4,20},{5,21},{6,22},{7,23},{8,24},{9,... | collective-permute-start | bytes 98312 | tf_op jit(solution)/shard_map/ppermute | solution.py:757
  10.4 6.3 %collective-permute-start.1 = (bf16[2,2,8192]{2,1,0:T(2,128)(2,1)S(1)}, bf16[2,2,8192]{2,1,0:T(2,128)(2,1)S(1)}, u32[]{:S(2)}, u32[]{:S(2)}) collective-permute-start(bf16[2,2,8192]{2,1,0:T(2,128)(2,1)S(1)} %pad_maximum_fusion.12), channel_id=1, source_target_pairs={{0,8},{1,9},{2,10},{3,11},{4,12},{5,13},{6,14},{7,15},{8,0},{9,1},... | collective-permute-start | bytes 196616 | tf_op jit(solution)/shard_map/ppermute | solution.py:760
  17.4 6.4 %collective-permute-start.2 = (bf16[2,4,8192]{2,1,0:T(4,128)(2,1)S(1)}, bf16[2,4,8192]{2,1,0:T(4,128)(2,1)S(1)}, u32[]{:S(2)}, u32[]{:S(2)}) collective-permute-start(bf16[2,4,8192]{2,1,0:T(4,128)(2,1)S(1)} %pad_maximum_fusion.7), channel_id=1, source_target_pairs={{0,4},{1,5},{2,6},{3,7},{4,0},{5,1},{6,2},{7,3},{8,12},{9,13},{10,... | collective-permute-start | bytes 393224 | tf_op jit(solution)/shard_map/ppermute | solution.py:760
  24.1 9.0 %collective-permute-start.3 = (bf16[2,8,8192]{2,1,0:T(8,128)(2,1)S(1)}, bf16[2,8,8192]{2,1,0:T(8,128)(2,1)S(1)}, u32[]{:S(2)}, u32[]{:S(2)}) collective-permute-start(bf16[2,8,8192]{2,1,0:T(8,128)(2,1)S(1)} %pad_maximum_fusion.4), channel_id=1, source_target_pairs={{0,2},{1,3},{2,0},{3,1},{4,6},{5,7},{6,4},{7,5},{8,10},{9,11},{10,... | collective-permute-start | bytes 786440 | tf_op jit(solution)/shard_map/ppermute | solution.py:760
  33.3 2.0 %collective-permute-start.4 = (bf16[2,16,8192]{2,1,0:T(8,128)(2,1)S(1)}, bf16[2,16,8192]{2,1,0:T(8,128)(2,1)S(1)}, u32[]{:S(2)}, u32[]{:S(2)}) collective-permute-start(bf16[2,16,8192]{2,1,0:T(8,128)(2,1)S(1)} %pad_maximum_fusion.1), channel_id=1, source_target_pairs={{0,1},{1,0},{2,3},{3,2},{4,5},{5,4},{6,7},{7,6},{8,9},{9,8},{10,11... | collective-permute-start | bytes 1572872 | tf_op jit(solution)/shard_map/ppermute | solution.py:757
  52.5 1.8 collective-permute-start.5
  55.4 5.6 %collective-permute-start.6 = (bf16[8,8192]{1,0:T(8,128)(2,1)S(1)}, bf16[8,8192]{1,0:T(8,128)(2,1)S(1)}, u32[]{:S(2)}, u32[]{:S(2)}) collective-permute-start(bf16[8,8192]{1,0:T(8,128)(2,1)S(1)} %get-tuple-element.131), channel_id=1, source_target_pairs={{0,2},{1,3},{2,0},{3,1},{4,6},{5,7},{6,4},{7,5},{8,10},{9,11},{10,... | collective-permute-start | bytes 393224 | tf_op jit(solution)/shard_map/ppermute | solution.py:760
  61.1 5.8 %collective-permute-start.7 = (bf16[4,8192]{1,0:T(4,128)(2,1)S(1)}, bf16[4,8192]{1,0:T(4,128)(2,1)S(1)}, u32[]{:S(2)}, u32[]{:S(2)}) collective-permute-start(bf16[4,8192]{1,0:T(4,128)(2,1)S(1)} %add_convert_fusion.9), channel_id=1, source_target_pairs={{0,4},{1,5},{2,6},{3,7},{4,0},{5,1},{6,2},{7,3},{8,12},{9,13},{10,... | collective-permute-start | bytes 196616 | tf_op jit(solution)/shard_map/ppermute | solution.py:760
  67.0 6.1 %collective-permute-start.8 = (bf16[4,8192]{1,0:T(4,128)(2,1)S(1)}, bf16[4,8192]{1,0:T(4,128)(2,1)S(1)}, u32[]{:S(2)}, u32[]{:S(2)}) collective-permute-start(bf16[4,8192]{1,0:T(4,128)(2,1)S(1)} %add_convert_fusion.8), channel_id=1, source_target_pairs={{0,8},{1,9},{2,10},{3,11},{4,12},{5,13},{6,14},{7,15},{8,0},{9,1},... | collective-permute-start | bytes 196616 | tf_op jit(solution)/shard_map/ppermute | solution.py:760
  73.1 6.5 %collective-permute-start.9 = (bf16[4,8192]{1,0:T(4,128)(2,1)S(1)}, bf16[4,8192]{1,0:T(4,128)(2,1)S(1)}, u32[]{:S(2)}, u32[]{:S(2)}) collective-permute-start(bf16[4,8192]{1,0:T(4,128)(2,1)S(1)} %add_convert_fusion.7), channel_id=1, source_target_pairs={{0,16},{1,17},{2,18},{3,19},{4,20},{5,21},{6,22},{7,23},{8,24},{9,... | collective-permute-start | bytes 196616 | tf_op jit(solution)/shard_map/ppermute | solution.py:760
  80.0 6.3 %collective-permute-start.10 = (bf16[4,8192]{1,0:T(4,128)(2,1)S(1)}, bf16[4,8192]{1,0:T(4,128)(2,1)S(1)}, u32[]{:S(2)}, u32[]{:S(2)}) collective-permute-start(bf16[4,8192]{1,0:T(4,128)(2,1)S(1)} %fusion.8), channel_id=1, source_target_pairs={{0,4},{1,5},{2,6},{3,7},{4,0},{5,1},{6,2},{7,3},{8,12},{9,13},{10,... | collective-permute-start | bytes 196616 | tf_op jit(solution)/shard_map/ppermute | solution.py:760
  86.5 6.1 %collective-permute-start.11 = (bf16[8,8192]{1,0:T(8,128)(2,1)S(1)}, bf16[8,8192]{1,0:T(8,128)(2,1)S(1)}, u32[]{:S(2)}, u32[]{:S(2)}) collective-permute-start(bf16[8,8192]{1,0:T(8,128)(2,1)S(1)} %pad_maximum_fusion.8), channel_id=1, source_target_pairs={{0,2},{1,3},{2,0},{3,1},{4,6},{5,7},{6,4},{7,5},{8,10},{9,11},{10,... | collective-permute-start | bytes 393224 | tf_op jit(solution)/shard_map/ppermute | solution.py:760
  92.8 1.6 collective-permute-start.12
  115.4 1.8 collective-permute-start.13
  118.3 5.6 %collective-permute-start.14 = (bf16[8,8192]{1,0:T(8,128)(2,1)S(1)}, bf16[8,8192]{1,0:T(8,128)(2,1)S(1)}, u32[]{:S(2)}, u32[]{:S(2)}) collective-permute-start(bf16[8,8192]{1,0:T(8,128)(2,1)S(1)} %get-tuple-element.164), channel_id=1, source_target_pairs={{0,2},{1,3},{2,0},{3,1},{4,6},{5,7},{6,4},{7,5},{8,10},{9,11},{10,... | collective-permute-start | bytes 393224 | tf_op jit(solution)/shard_map/ppermute | solution.py:760
  123.9 4.3 %collective-permute-start.15 = (bf16[4,8192]{1,0:T(4,128)(2,1)S(1)}, bf16[4,8192]{1,0:T(4,128)(2,1)S(1)}, u32[]{:S(2)}, u32[]{:S(2)}) collective-permute-start(bf16[4,8192]{1,0:T(4,128)(2,1)S(1)} %add_convert_fusion.6), channel_id=1, source_target_pairs={{0,4},{1,5},{2,6},{3,7},{4,0},{5,1},{6,2},{7,3},{8,12},{9,13},{10,... | collective-permute-start | bytes 196616 | tf_op jit(solution)/shard_map/ppermute | solution.py:760
  128.4 5.6 %collective-permute-start.16 = (bf16[4,8192]{1,0:T(4,128)(2,1)S(1)}, bf16[4,8192]{1,0:T(4,128)(2,1)S(1)}, u32[]{:S(2)}, u32[]{:S(2)}) collective-permute-start(bf16[4,8192]{1,0:T(4,128)(2,1)S(1)} %add_convert_fusion.5), channel_id=1, source_target_pairs={{0,8},{1,9},{2,10},{3,11},{4,12},{5,13},{6,14},{7,15},{8,0},{9,1},... | collective-permute-start | bytes 196616 | tf_op jit(solution)/shard_map/ppermute | solution.py:760
  134.0 5.9 %collective-permute-start.17 = (bf16[4,8192]{1,0:T(4,128)(2,1)S(1)}, bf16[4,8192]{1,0:T(4,128)(2,1)S(1)}, u32[]{:S(2)}, u32[]{:S(2)}) collective-permute-start(bf16[4,8192]{1,0:T(4,128)(2,1)S(1)} %add_convert_fusion.4), channel_id=1, source_target_pairs={{0,16},{1,17},{2,18},{3,19},{4,20},{5,21},{6,22},{7,23},{8,24},{9,... | collective-permute-start | bytes 196616 | tf_op jit(solution)/shard_map/ppermute | solution.py:760
  140.4 4.9 %collective-permute-start.18 = (bf16[4,8192]{1,0:T(4,128)(2,1)S(1)}, bf16[4,8192]{1,0:T(4,128)(2,1)S(1)}, u32[]{:S(2)}, u32[]{:S(2)}) collective-permute-start(bf16[4,8192]{1,0:T(4,128)(2,1)S(1)} %fusion.13), channel_id=1, source_target_pairs={{0,4},{1,5},{2,6},{3,7},{4,0},{5,1},{6,2},{7,3},{8,12},{9,13},{10,... | collective-permute-start | bytes 196616 | tf_op jit(solution)/shard_map/ppermute | solution.py:760
  145.4 5.0 %collective-permute-start.19 = (bf16[8,8192]{1,0:T(8,128)(2,1)S(1)}, bf16[8,8192]{1,0:T(8,128)(2,1)S(1)}, u32[]{:S(2)}, u32[]{:S(2)}) collective-permute-start(bf16[8,8192]{1,0:T(8,128)(2,1)S(1)} %pad_maximum_fusion.9), channel_id=1, source_target_pairs={{0,2},{1,3},{2,0},{3,1},{4,6},{5,7},{6,4},{7,5},{8,10},{9,11},{10,... | collective-permute-start | bytes 393224 | tf_op jit(solution)/shard_map/ppermute | solution.py:760
  150.6 1.6 collective-permute-start.20
  153.2 14.8 %copy-start = (bf16[1,8192]{1,0:T(2,128)(2,1)S(1)}, bf16[1,8192]{1,0:T(2,128)(2,1)}, u32[]{:S(2)}) copy-start(bf16[1,8192]{1,0:T(2,128)(2,1)} %param.14) | copy-start | bytes 49156
  167.8 1.8 collective-permute-start.21
  170.6 7.3 %collective-permute-start.22 = (bf16[8,8192]{1,0:T(8,128)(2,1)S(1)}, bf16[8,8192]{1,0:T(8,128)(2,1)S(1)}, u32[]{:S(2)}, u32[]{:S(2)}) collective-permute-start(bf16[8,8192]{1,0:T(8,128)(2,1)S(1)} %get-tuple-element.199), channel_id=1, source_target_pairs={{0,2},{1,3},{2,0},{3,1},{4,6},{5,7},{6,4},{7,5},{8,10},{9,11},{10,... | collective-permute-start | bytes 393224 | tf_op jit(solution)/shard_map/ppermute | solution.py:760
  178.0 6.0 %collective-permute-start.23 = (bf16[4,8192]{1,0:T(4,128)(2,1)S(1)}, bf16[4,8192]{1,0:T(4,128)(2,1)S(1)}, u32[]{:S(2)}, u32[]{:S(2)}) collective-permute-start(bf16[4,8192]{1,0:T(4,128)(2,1)S(1)} %get-tuple-element.205), channel_id=1, source_target_pairs={{0,4},{1,5},{2,6},{3,7},{4,0},{5,1},{6,2},{7,3},{8,12},{9,13},{10,... | collective-permute-start | bytes 196616 | tf_op jit(solution)/shard_map/ppermute | solution.py:760
  184.2 4.0 %collective-permute-start.24 = (bf16[2,8192]{1,0:T(2,128)(2,1)S(1)}, bf16[2,8192]{1,0:T(2,128)(2,1)S(1)}, u32[]{:S(2)}, u32[]{:S(2)}) collective-permute-start(bf16[2,8192]{1,0:T(2,128)(2,1)S(1)} %get-tuple-element.211), channel_id=1, source_target_pairs={{0,8},{1,9},{2,10},{3,11},{4,12},{5,13},{6,14},{7,15},{8,0},{9,1},... | collective-permute-start | bytes 98312 | tf_op jit(solution)/shard_map/ppermute | solution.py:760
  187.9 5.2 %copy-start.1 = (f32[2,8192]{1,0:T(2,128)S(1)}, f32[2,8192]{1,0:T(2,128)}, u32[]{:S(2)}) copy-start(f32[2,8192]{1,0:T(2,128)} %param.15) | copy-start | bytes 196612
  188.2 4.9 %collective-permute-start.25 = (bf16[1,8192]{1,0:T(2,128)(2,1)S(1)}, bf16[1,8192]{1,0:T(2,128)(2,1)S(1)}, u32[]{:S(2)}, u32[]{:S(2)}) collective-permute-start(bf16[1,8192]{1,0:T(2,128)(2,1)S(1)} %add_convert_fusion.12), channel_id=1, source_target_pairs={{0,16},{1,17},{2,18},{3,19},{4,20},{5,21},{6,22},{7,23},{8,24},{9,... | collective-permute-start | bytes 49160 | tf_op jit(solution)/shard_map/ppermute | solution.py:760
